TPU v7x, 32 devices: a whole 2x2x4 slice. The times are simulated.
32 devices in a mesh: dp: 4 (over y, x), seq: 2 (over core), mp: 4 (over z).
Axes of the slice: x: 2, y: 2, z: 4, core: 2. Of those that a mesh axis runs over, the one named last changes fastest.
Arguments:
- x_in: bfloat16 [3, 4, 2048, 2048], P(None, 'dp', 'seq', 'mp'), may hold values from -6 to 6
- cotangent: bfloat16 [3, 4, 2048, 2048], P(None, 'dp', 'seq', 'mp'), may hold values from -6 to 6
- lengths: int32 [3, 4], P(None, 'dp'), may hold values from 512 to 2048, as said below
- adapter_ids: int32 [3, 4], P(None, 'dp'), may hold values from 0 to 7
- norm_gain: float32 [2048], replicated, may hold values from 0.5 to 1.5
- w_zx: bfloat16 [2048, 2, 4096], P(('dp', 'seq'), None, 'mp'), may hold values from -0.125 to 0.125
- w_bc: bfloat16 [2048, 256], P(('dp', 'seq')), may hold values from -0.125 to 0.125
- w_dt: bfloat16 [2048, 64], P(('dp', 'seq'), 'mp'), may hold values from -0.19921875 to 0.19921875
- dt_bias: float32 [64], P('mp'), may hold values from -9.5 to -4.5
- a_log: float32 [64], P('mp'), may hold values from 0 to 0.7
- d_skip: float32 [64], P('mp'), may hold values from 0.5 to 1.5
- conv_x: float32 [4, 4096], P(None, 'mp'), may hold values from -3 to 3
- conv_bc: float32 [4, 256], replicated, may hold values from -3 to 3
- gate_gain: float32 [4096], P('mp'), may hold values from 0.5 to 1.5
- w_out: bfloat16 [4096, 2048], P('mp', ('dp', 'seq')), may hold values from -0.09375 to 0.09375
- in_down: bfloat16 [8, 2048, 16], P(None, ('dp', 'seq', 'mp')), may hold values from -0.125 to 0.125
- in_up: bfloat16 [128, 2, 4096], P(('dp', 'seq'), None, 'mp'), may hold values from -0.75 to 0.75
- out_down: bfloat16 [4096, 128], P('mp', ('dp', 'seq')), may hold values from -0.09375 to 0.09375
- out_up: bfloat16 [128, 2048], P(None, ('dp', 'seq', 'mp')), may hold values from -0.75 to 0.75
Outputs:
- out: bfloat16 [3, 4, 2048, 2048], P(None, 'dp', 'seq', 'mp')
- x_grad: float32 [3, 4, 2048, 2048], P(None, 'dp', 'seq', 'mp')
- in_down_grad: float32 [8, 2048, 16], P(None, ('dp', 'seq', 'mp'))
- in_up_grad: float32 [128, 2, 4096], P(('dp', 'seq'), None, 'mp')
- out_down_grad: float32 [4096, 128], P('mp', ('dp', 'seq'))
- out_up_grad: float32 [128, 2048], P(None, ('dp', 'seq', 'mp'))
Inputs may be any that keep to these rules, and one draw needn't show every extreme that they name: `lengths`: each slot holds its sequence from its first position; the rest is padding. For every slot column, one of the 3 micro-batches fills it to 2048.
All inputs are finite; a program needn't handle non-finite values.
Results may differ from a plain program's by a relative error of at most 0.0029.
The roundings to bfloat16 on the way count: a program that leaves them out, or rounds other values in their place, can miss the bound.
Values may be sent and summed in bfloat16 or wider, within the bound.
A program may use at most 832 MiB of HBM per device.

v0:
```python
import jax
import jax.numpy as jnp
from jax import lax
from jax.sharding import PartitionSpec as P

D = 2048
P_SIZE = 64
NS = 128
KC = 4
Q = 256
R = 16
ADAPT = 8
DI = 4096


eps = 1e-05
precise = lax.Precision.HIGHEST


def shifted(array, axis, by):
    size = lax.axis_size(axis)
    pairs = [(i, i + by) for i in range(size) if 0 <= i + by < size]
    return lax.ppermute(array, axis, pairs)


def entering(part, axis, combine, identity, reverse):
    count = lax.axis_size(axis)
    place = lax.axis_index(axis)
    ahead = count - 1 - place if reverse else place
    gathered = jax.tree.map(lambda a: lax.all_gather(a, axis), part)
    state = jax.tree.map(lambda a, e: jnp.zeros_like(a) + jnp.asarray(e, a.dtype), part, identity)

    def one(hop, state):
        source = count - 1 - hop if reverse else hop
        return combine(
            state, jax.tree.map(lambda a: lax.dynamic_index_in_dim(a, source, 0, False), gathered)
        )

    return lax.fori_loop(0, ahead, one, state)


def silu_grad(value):
    sigmoid_val = jax.nn.sigmoid(value)
    return sigmoid_val * (1.0 + value * (1.0 - sigmoid_val))


def block_step(carry_state, pieces):
    x_part, b_part, c_part, log_part, step_part = pieces
    length = log_part.shape[0]
    cumulative = jnp.cumsum(log_part, axis=0)
    causal = jnp.arange(length)[:, None] >= jnp.arange(length)[None, :]
    spread = cumulative[:, None, :] - cumulative[None, :, :]
    decay_mat = jnp.exp(jnp.where(causal[:, :, None], spread, -10000.0))
    scores = jnp.dot(c_part, b_part.T, precision=precise)
    mixing = scores[:, :, None] * decay_mat * step_part[None, :, :]
    inner_out = jnp.einsum("tsh,shp->thp", mixing, x_part, precision=precise)
    carried = jnp.exp(cumulative)[:, :, None] * jnp.einsum(
        "tn,hpn->thp", c_part, carry_state, precision=precise
    )
    weights = jnp.exp(cumulative[-1][None, :] - cumulative) * step_part
    update = jnp.einsum("sh,shp,sn->hpn", weights, x_part, b_part, precision=precise)
    new_state = jnp.exp(cumulative[-1])[:, None, None] * carry_state + update
    return (new_state, inner_out + carried)


def local_scan(x_heads, b_rows, c_rows, log_rows, step_rows):
    seg_rows = x_heads.shape[0]
    blocks = seg_rows // Q

    def blocked(tensor):
        return tensor.reshape((blocks, Q) + tensor.shape[1:])

    init_state = jnp.zeros((x_heads.shape[1], x_heads.shape[2], b_rows.shape[1]), jnp.float32)
    final_state, outputs = lax.scan(
        block_step,
        init_state,
        (blocked(x_heads), blocked(b_rows), blocked(c_rows), blocked(log_rows), blocked(step_rows)),
    )
    return (outputs.reshape(x_heads.shape), final_state, jnp.sum(log_rows, axis=0))


def incoming(c_rows, log_rows, state_in):
    cumulative = jnp.cumsum(log_rows, axis=0)
    return jnp.exp(cumulative)[:, :, None] * jnp.einsum(
        "tn,hpn->thp", c_rows, state_in, precision=precise
    )


def compose(earlier, later):
    return (later[0] * earlier[0], later[1] + later[0][..., None, None] * earlier[1])


def fetch_weights(w_zx, w_bc, w_dt, w_out, in_up, out_down):
    return (
        lax.all_gather(w_zx, ("dp", "seq"), axis=0, tiled=True),
        lax.all_gather(w_bc, ("dp", "seq"), axis=0, tiled=True),
        lax.all_gather(w_dt, ("dp", "seq"), axis=0, tiled=True),
        lax.all_gather(w_out, ("dp", "seq"), axis=1, tiled=True),
        lax.all_gather(in_up, ("dp", "seq"), axis=0, tiled=True),
        lax.all_gather(out_down, ("dp", "seq"), axis=1, tiled=True),
    )


def reduce_adapters(grads):
    near_sums = (
        lax.psum_scatter(grads[1], ("dp", "seq"), scatter_dimension=0, tiled=True),
        lax.psum_scatter(grads[2], ("dp", "seq"), scatter_dimension=1, tiled=True),
    )
    wide_sums = (
        lax.psum_scatter(grads[0], ("dp", "seq", "mp"), scatter_dimension=1, tiled=True),
        lax.psum_scatter(grads[3], ("dp", "seq", "mp"), scatter_dimension=1, tiled=True),
    )
    return (wide_sums[0], near_sums[0], near_sums[1], wide_sums[1])


def body(
    x_in,
    cotangent,
    lengths,
    adapter_ids,
    norm_gain,
    w_zx,
    w_bc,
    w_dt,
    dt_bias,
    a_log,
    d_skip,
    conv_x,
    conv_bc,
    gate_gain,
    w_out,
    in_down,
    in_up,
    out_down,
    out_up,
):
    micro_count, slot_count, seg_len, model_part = x_in.shape
    head_local = dt_bias.shape[0]
    inner_local = head_local * P_SIZE
    wide_down, wide_up = (
        lax.all_gather(in_down, ("dp", "seq", "mp"), axis=1, tiled=True),
        lax.all_gather(out_up, ("dp", "seq", "mp"), axis=1, tiled=True),
    )
    wide_down = wide_down.astype(jnp.float32)
    wide_up = wide_up.astype(jnp.float32)
    conv_taps = jnp.concatenate([conv_x, conv_bc], axis=1)
    decay_rate = -jnp.exp(a_log)
    positions = lax.axis_index("seq") * seg_len + jnp.arange(seg_len)
    feature_start = lax.axis_index("mp") * model_part
    scan_local = jax.vmap(local_scan)
    incoming_map = jax.vmap(incoming)
    gathered = None
    outputs = []
    x_grads = []
    running = None
    for batch_index in range(micro_count):
        gathered = fetch_weights(w_zx, w_bc, w_dt, w_out, in_up, out_down)
        zx_weight, bc_weight, dt_weight, out_weight, up_in, down_out = gathered
        rows_own = x_in[batch_index]
        cot_own = cotangent[batch_index]
        rows_full, cot_full = (
            lax.all_gather(rows_own, "mp", axis=2, tiled=True),
            lax.all_gather(cot_own, "mp", axis=2, tiled=True),
        )
        rows_value = rows_full.astype(jnp.float32)
        inv_rms = lax.rsqrt(jnp.mean(rows_value * rows_value, axis=-1, keepdims=True) + eps)
        normed = rows_value * inv_rms * norm_gain
        normed_low = normed.astype(jnp.bfloat16)
        normed_value = normed_low.astype(jnp.float32)
        select = jax.nn.one_hot(adapter_ids[batch_index], ADAPT, dtype=jnp.float32)
        down_sel = jnp.einsum("sa,adr->sdr", select, wide_down, precision=precise)
        up_sel = jnp.einsum(
            "sa,arcf->srcf",
            select,
            up_in.astype(jnp.float32).reshape(ADAPT, R, 2, inner_local),
            precision=precise,
        )
        low_rank = jnp.einsum("std,sdr->str", normed_value, down_sel, precision=precise)
        proj_zx = jnp.einsum(
            "std,dcf->stcf", normed_low, zx_weight, preferred_element_type=jnp.float32
        )
        proj_zx = proj_zx + jnp.einsum("str,srcf->stcf", low_rank, up_sel, precision=precise)
        proj_bc = jnp.einsum(
            "std,dn->stn", normed_low, bc_weight, preferred_element_type=jnp.float32
        )
        proj_dt = jnp.einsum(
            "std,dh->sth", normed_low, dt_weight, preferred_element_type=jnp.float32
        )
        gate_in = proj_zx[:, :, 0]
        conv_in = jnp.concatenate(
            [proj_zx[:, :, 1].astype(jnp.bfloat16), proj_bc.astype(jnp.bfloat16)], axis=-1
        )
        earlier_rows = shifted(conv_in[:, seg_len - (KC - 1) :], "seq", 1)
        extended = jnp.concatenate([earlier_rows, conv_in], axis=1).astype(jnp.float32)
        conv_pre = sum(
            (
                conv_taps[tap_index] * extended[:, tap_index : tap_index + seg_len]
                for tap_index in range(KC)
            )
        )
        conv_out = jax.nn.silu(conv_pre)
        x_heads = conv_out[..., :inner_local].reshape(slot_count, seg_len, head_local, P_SIZE)
        b_rows = conv_out[..., inner_local : inner_local + NS]
        c_rows = conv_out[..., inner_local + NS :]
        mask_rows = (positions[None, :] < lengths[batch_index][:, None]).astype(jnp.float32)
        rate_in = proj_dt + dt_bias
        step_rows = jax.nn.softplus(rate_in) * mask_rows[..., None]
        log_rows = step_rows * decay_rate
        (plain_out, state_local, log_total), scan_back = jax.vjp(
            scan_local, x_heads, b_rows, c_rows, log_rows, step_rows
        )
        factor = jnp.exp(log_total)
        identity = (jnp.ones_like(factor), jnp.zeros_like(state_local))
        state_in = entering((factor, state_local), "seq", compose, identity, False)[1]
        from_state, state_back = jax.vjp(incoming_map, c_rows, log_rows, state_in)
        mixed_heads = plain_out + from_state + d_skip[:, None] * x_heads
        mixed_flat = mixed_heads.reshape(slot_count, seg_len, inner_local)
        gate_act = jax.nn.silu(gate_in)
        gated_out = mixed_flat * gate_act
        square_sum = lax.psum(jnp.sum(gated_out * gated_out, axis=-1), "mp")
        inv_gate = lax.rsqrt(square_sum / DI + eps)
        scaled = gated_out * inv_gate[..., None] * gate_gain
        scaled_low = scaled.astype(jnp.bfloat16)
        scaled_value = scaled_low.astype(jnp.float32)
        out_sel = jnp.einsum(
            "sa,far->sfr",
            select,
            down_out.astype(jnp.float32).reshape(inner_local, ADAPT, R),
            precision=precise,
        )
        up_out = jnp.einsum("sa,ard->srd", select, wide_up.reshape(ADAPT, R, D), precision=precise)
        rank_out = jnp.einsum("stf,sfr->str", scaled_value, out_sel, precision=precise)
        partial_out = jnp.einsum(
            "stf,fd->std", scaled_low, out_weight, preferred_element_type=jnp.float32
        )
        partial_out = partial_out + jnp.einsum("str,srd->std", rank_out, up_out, precision=precise)
        branch = lax.psum_scatter(partial_out, "mp", scatter_dimension=2, tiled=True)
        outputs.append(
            (rows_own.astype(jnp.float32) + mask_rows[..., None] * branch).astype(jnp.bfloat16)
        )
        branch_grad = cot_full * mask_rows[..., None].astype(jnp.bfloat16)
        branch_value = branch_grad.astype(jnp.float32)
        rank_grad = jnp.einsum("std,srd->str", branch_value, up_out, precision=precise)
        grad_up_out = jnp.einsum("str,std->srd", rank_out, branch_value, precision=precise)
        grad_out_sel = jnp.einsum("stf,str->sfr", scaled_value, rank_grad, precision=precise)
        scaled_grad = jnp.einsum(
            "std,fd->stf", branch_grad, out_weight, preferred_element_type=jnp.float32
        )
        scaled_grad = scaled_grad + jnp.einsum(
            "str,sfr->stf", rank_grad, out_sel, precision=precise
        )
        weighted = scaled_grad * gate_gain
        dot_sum = lax.psum(jnp.sum(weighted * gated_out, axis=-1), "mp")
        gated_grad = (
            weighted * inv_gate[..., None] - gated_out * (inv_gate**3 * dot_sum / DI)[..., None]
        )
        mixed_grad = (gated_grad * gate_act).reshape(slot_count, seg_len, head_local, P_SIZE)
        gate_grad = gated_grad * mixed_flat * silu_grad(gate_in)
        c_grad_in, log_grad_in, state_in_grad = state_back(mixed_grad)
        later_grads = entering((factor, state_in_grad), "seq", compose, identity, True)[1]
        total_grad = jnp.sum(later_grads * state_in, axis=(2, 3)) * factor
        x_heads_grad, b_grad, c_grad, log_grad, step_grad = scan_back(
            (mixed_grad, later_grads, total_grad)
        )
        x_heads_grad = x_heads_grad + d_skip[:, None] * mixed_grad
        c_grad = c_grad + c_grad_in
        step_grad = step_grad + (log_grad + log_grad_in) * decay_rate
        rate_grad = step_grad * mask_rows[..., None] * jax.nn.sigmoid(rate_in)
        conv_out_grad = jnp.concatenate(
            [x_heads_grad.reshape(slot_count, seg_len, inner_local), b_grad, c_grad], axis=-1
        )
        pre_grad = conv_out_grad * silu_grad(conv_pre)
        padded_grad = jnp.pad(pre_grad, ((0, 0), (KC - 1, KC - 1), (0, 0)))
        ext_grad = sum(
            (
                conv_taps[tap_index]
                * padded_grad[:, KC - 1 - tap_index : KC - 1 - tap_index + seg_len + KC - 1]
                for tap_index in range(KC)
            )
        )
        returned = shifted(ext_grad[:, : KC - 1], "seq", -1)
        in_grad = ext_grad[:, KC - 1 :]
        in_grad = in_grad.at[:, seg_len - (KC - 1) :].add(returned)
        zx_grad = jnp.stack([gate_grad, in_grad[..., :inner_local]], axis=2).astype(jnp.bfloat16)
        dt_grad_low = rate_grad.astype(jnp.bfloat16)
        zx_grad_value = zx_grad.astype(jnp.float32)
        rank_in_grad = jnp.einsum("stcf,srcf->str", zx_grad_value, up_sel, precision=precise)
        grad_up_sel = jnp.einsum("str,stcf->srcf", low_rank, zx_grad_value, precision=precise)
        grad_down_sel = jnp.einsum("std,str->sdr", normed_value, rank_in_grad, precision=precise)
        normed_part = jnp.einsum(
            "stcf,dcf->std", zx_grad, zx_weight, preferred_element_type=jnp.float32
        )
        normed_part = normed_part + jnp.einsum(
            "sth,dh->std", dt_grad_low, dt_weight, preferred_element_type=jnp.float32
        )
        normed_part = normed_part + jnp.einsum(
            "str,sdr->std", rank_in_grad, down_sel, precision=precise
        )
        bc_partial = in_grad[..., inner_local:]
        normed_sum, bc_sum = lax.psum((normed_part, bc_partial), "mp")
        normed_grad = normed_sum + jnp.einsum(
            "stn,dn->std",
            bc_sum.astype(jnp.bfloat16),
            bc_weight,
            preferred_element_type=jnp.float32,
        )
        scaled_in = normed_grad * norm_gain
        row_grad = inv_rms * scaled_in - rows_value * inv_rms**3 * jnp.mean(
            scaled_in * rows_value, axis=-1, keepdims=True
        )
        own_slice = lax.dynamic_slice_in_dim(row_grad, feature_start, model_part, 2)
        x_grads.append(cot_own.astype(jnp.float32) + own_slice)
        local_grads = (
            jnp.einsum("sa,sdr->adr", select, grad_down_sel, precision=precise),
            jnp.einsum("sa,srcf->arcf", select, grad_up_sel, precision=precise).reshape(
                ADAPT * R, 2, inner_local
            ),
            jnp.einsum("sa,sfr->far", select, grad_out_sel, precision=precise).reshape(
                inner_local, ADAPT * R
            ),
            jnp.einsum("sa,srd->ard", select, grad_up_out, precision=precise).reshape(ADAPT * R, D),
        )
        running = local_grads if running is None else jax.tree.map(jnp.add, running, local_grads)
    running = reduce_adapters(running)
    return (jnp.stack(outputs), jnp.stack(x_grads), running[0], running[1], running[2], running[3])


def solution(mesh):
    in_specs = (
        P(None, "dp", "seq", "mp"),
        P(None, "dp", "seq", "mp"),
        P(None, "dp"),
        P(None, "dp"),
        P(),
        P(("dp", "seq"), None, "mp"),
        P(("dp", "seq"), None),
        P(("dp", "seq"), "mp"),
        P("mp"),
        P("mp"),
        P("mp"),
        P(None, "mp"),
        P(),
        P("mp"),
        P("mp", ("dp", "seq")),
        P(None, ("dp", "seq", "mp"), None),
        P(("dp", "seq"), None, "mp"),
        P("mp", ("dp", "seq")),
        P(None, ("dp", "seq", "mp")),
    )
    out_specs = (
        P(None, "dp", "seq", "mp"),
        P(None, "dp", "seq", "mp"),
        P(None, ("dp", "seq", "mp"), None),
        P(("dp", "seq"), None, "mp"),
        P("mp", ("dp", "seq")),
        P(None, ("dp", "seq", "mp")),
    )
    return jax.shard_map(body, mesh=mesh, in_specs=in_specs, out_specs=out_specs, check_vma=False)
```

profile of v0, /device:TPU:9, one launch (start us, length us, event | category | flops | bytes accessed | tf_op | source)
XLA Modules:
  0.0 4585.6 jit_solution(6936064335897904732)
XLA Ops:
  42.3 69.5 %all_gather.119 = bf16[128,2048]{0,1:T(8,128)(2,1)S(1)} all-gather(bf16[128,64]{0,1:T(8,128)(2,1)S(1)} %copy-done.211), channel_id=1, replica_groups=mesh['dp'=4,'seq'=2,'mp'=4] {'dp','seq','mp'}, dimensions={1}, use_global_device_ids=true | all-gather | bytes 540672 | tf_op jit(solution)/shard_map/all_gather | solution.py:142
  150.0 206.1 %all_gather.111 = bf16[8,2048,16]{2,0,1:T(8,128)(2,1)S(1)} all-gather(bf16[8,64,16]{2,0,1:T(8,128)(2,1)S(1)} %copy.444), channel_id=1, replica_groups=mesh['dp'=4,'seq'=2,'mp'=4] {'dp','seq','mp'}, dimensions={1}, use_global_device_ids=true | all-gather | bytes 540672 | tf_op jit(solution)/shard_map/all_gather | solution.py:141
  495.2 74.6 %all-gather.57.cloned.1.call-done = bf16[1,1,1024,2048]{3,2,1,0:T(8,128)(2,1)} async-done(((bf16[1,1,1024,512]{3,2,1,0:T(8,128)(2,1)}), bf16[1,1,1024,2048]{3,2,1,0:T(8,128)(2,1)}) %all-gather.57.cloned.1.call-update) | async-done | bytes 4194320 | tf_op jit(solution)/shard_map/all_gather | solution.py:163
  659.7 34.3 all-gather.31.cloned.1.call-done
  771.2 38.6 fusion.398
  867.1 211.7 %while.302 = (s32[]{:T(128)}, f32[1,16,64,128]{3,2,1,0:T(8,128)S(1)}, f32[4,1,256,16,64]{2,0,4,3,1:T(4,128)}, f32[4,1,256,256,16]{3,2,4,1,0:T(8,128)}, f32[4,1,1...) while((s32[]{:T(128)}, ...), condition=%wide.region_30.31_spmd.clone.clone, body=%wide.region_27.30_spmd.clone.clone.sunk | while | flops 1721901056 | bytes 31548964 | solution.py:74
  1128.0 212.3 %while.301 = (s32[]{:T(128)}, f32[1,16,64,128]{3,2,1,0:T(8,128)S(1)}, f32[4,1,256,16,64]{2,0,4,3,1:T(4,128)}, f32[4,1,256,256,16]{3,2,4,1,0:T(8,128)}, f32[4,1,1...) while((s32[]{:T(128)}, ...), condition=%wide.region_17.18_spmd.clone.clone, body=%wide.region_14.17_spmd.clone.clone.sunk | while | flops 1721901056 | bytes 31548964 | solution.py:74
  1395.3 211.7 %while.300 = (s32[]{:T(128)}, f32[1,16,64,128]{3,2,1,0:T(8,128)S(1)}, f32[4,1,256,16,64]{2,0,4,3,1:T(4,128)}, f32[4,1,256,256,16]{3,2,4,1,0:T(8,128)}, f32[4,1,1...) while((s32[]{:T(128)}, ...), condition=%wide.region_4.5_spmd.clone.clone, body=%wide.region_1.4_spmd.clone.clone.sunk | while | flops 1721901056 | bytes 31548964 | solution.py:74
  1796.7 286.9 %while.299 = (s32[]{:T(128)}, f32[1,16,64,128]{3,2,1,0:T(8,128)S(1)}, f32[4,1,256,16,64]{2,0,4,3,1:T(4,128)}, f32[4,1,256,128]{3,2,1,0:T(8,128)}, f32[4,1,256,12...) while((s32[]{:T(128)}, ...), condition=%wide.region_97.98_spmd.clone, body=%wide.region_87.97_spmd.clone.sunk | while | flops 3436216320 | bytes 38886384 | solution.py:74
  2089.6 287.5 %while.298 = (s32[]{:T(128)}, f32[1,16,64,128]{3,2,1,0:T(8,128)S(1)}, f32[4,1,256,16,64]{2,0,4,3,1:T(4,128)}, f32[4,1,256,128]{3,2,1,0:T(8,128)}, f32[4,1,256,12...) while((s32[]{:T(128)}, ...), condition=%wide.region_75.76_spmd.clone, body=%wide.region_65.75_spmd.clone.sunk | while | flops 3436216320 | bytes 38886384 | solution.py:74
  2125.0 23.4 dynamic_update_slice.597
  2196.7 23.4 dynamic_update_slice.597
  2268.4 23.4 dynamic_update_slice.597
  2340.2 23.4 dynamic_update_slice.597
  2396.3 287.6 %while.297 = (s32[]{:T(128)}, f32[1,16,64,128]{3,2,1,0:T(8,128)S(1)}, f32[4,1,256,16,64]{2,0,4,3,1:T(4,128)}, f32[4,1,256,128]{3,2,1,0:T(8,128)}, f32[4,1,256,12...) while((s32[]{:T(128)}, ...), condition=%wide.region_53.54_spmd.clone, body=%wide.region_43.53_spmd.clone.sunk | while | flops 3436216320 | bytes 38886384 | solution.py:74
  2431.4 23.4 dynamic_update_slice.592
  2503.1 23.4 dynamic_update_slice.592
  2646.6 23.4 dynamic_update_slice.592
  2727.0 36.9 multiply_add_fusion.2
  3160.7 202.4 %all-reduce.24 = (bf16[1,1024,256]{1,2,0:T(8,128)(2,1)}, bf16[1,1024,256]{1,2,0:T(8,128)(2,1)}, bf16[1,1024,256]{1,2,0:T(8,128)(2,1)}) all-reduce(f32[1,1024,256]{1,2,0:T(8,128)} %slice.624, f32[1,1024,256]{1,2,0:T(8,128)} %slice.617, f32[1,1024,256]{1,2,0:T(8,128)} %slice.610), channel_id=1, replica_groups=mesh['dp'=4,'seq'=2,'mp'=4] {'mp'}, use_global_device_ids=true, to_apply=%region_103.104 | all-reduce | flops 786432 | bytes 4718592 | tf_op jit(solution)/shard_map/psum | solution.py:300
  3366.4 59.4 %reduce-scatter.13.cloned.1.call-done = f32[1,1024,512]{2,1,0:T(8,128)} async-done(((f32[1,1024,2048]{2,1,0:T(8,128)}), f32[1,1024,512]{2,1,0:T(8,128)}) %reduce-scatter.13.cloned.1.call-update) | async-done | bytes 2097168 | tf_op jit(solution)/shard_map/reduce_scatter | solution.py:237
  3425.8 147.9 %reduce-scatter.11.cloned.1.call-done = f32[1,1024,512]{2,1,0:T(8,128)} async-done(((f32[1,1024,2048]{2,1,0:T(8,128)}), f32[1,1024,512]{2,1,0:T(8,128)}) %reduce-scatter.11.cloned.1.call-update) | async-done | bytes 2097168 | tf_op jit(solution)/shard_map/reduce_scatter | solution.py:237
  3579.0 832.1 %all-reduce.23.cloned.1.call-done = (f32[1,1024,2048]{2,1,0:T(8,128)}, f32[1,1024,2048]{2,1,0:T(8,128)}, f32[1,1024,2048]{2,1,0:T(8,128)}) async-done(((f32[1,1024,2048]{2,1,0:T(8,128)}, f32[1,1024,2048]{2,1,0:T(8,128)}, f32[1,1024,2048]{2,1,0:T(8,128)}), (f32[1,1024,2048]{2,1,0:T(8,128)}, f32[1,1024,2048]{2,1,0:T(8,128)}, f32[1,1024,2048]{2,1,0:T(8,128)})) %all-reduce.23.cloned.1.call-update) | async-done | bytes 25165840 | tf_op jit(solution)/shard_map/psum | solution.py:300
  4449.4 129.4 %reduce-scatter.21.cloned.1.call-done = f32[64,128]{1,0:T(8,128)} async-done(((f32[2048,128]{1,0:T(8,128)}), f32[64,128]{1,0:T(8,128)}) %reduce-scatter.21.cloned.1.call-update) | async-done | bytes 32784
  (1858 shorter events, 2570.4 us)
Async XLA Ops:
  7.2 368.5 %all-gather.45.cloned.1.call-start = ((), (), s32[]{:S(2)}) async-start(), calls=%async_computation.17 | async-start | bytes 5242880 | tf_op jit(solution)/shard_map/all_gather | solution.py:162
  11.0 369.5 %all-gather.41.cloned.1.call-start = ((), (), s32[]{:S(2)}) async-start(), calls=%async_computation.15 | async-start | bytes 5242880 | tf_op jit(solution)/shard_map/all_gather | solution.py:162
  11.7 372.5 %all-gather.37.cloned.1.call-start = ((), (), s32[]{:S(2)}) async-start(), calls=%async_computation.13 | async-start | bytes 5242880 | tf_op jit(solution)/shard_map/all_gather | solution.py:162
  12.5 469.0 %all-gather.49.cloned.1.call-start = ((), (), s32[]{:S(2)}) async-start(), calls=%async_computation.19 | async-start | bytes 5242880 | tf_op jit(solution)/shard_map/all_gather | solution.py:163
  14.4 474.5 %all-gather.53.cloned.1.call-start = ((), (), s32[]{:S(2)}) async-start(), calls=%async_computation.21 | async-start | bytes 5242880 | tf_op jit(solution)/shard_map/all_gather | solution.py:163
  15.0 554.8 %all-gather.57.cloned.1.call-start = ((), (), s32[]{:S(2)}) async-start(), calls=%async_computation.23 | async-start | bytes 5242880 | tf_op jit(solution)/shard_map/all_gather | solution.py:163
  15.6 599.0 %all-gather.33.cloned.1.call-start = ((), (), s32[]{:S(2)}) async-start(), calls=%async_computation.7 | async-start | bytes 1179648 | tf_op jit(solution)/shard_map/all_gather | solution.py:96
  16.3 619.7 %all-gather.35.cloned.1.call-start = ((), (), s32[]{:S(2)}) async-start(), calls=%async_computation.8 | async-start | bytes 4718592 | tf_op jit(solution)/shard_map/all_gather | solution.py:98
  17.1 676.8 %all-gather.31.cloned.1.call-start = ((), (), s32[]{:S(2)}) async-start(), calls=%async_computation.6 | async-start | bytes 9437184 | tf_op jit(solution)/shard_map/all_gather | solution.py:95
  19.4 1605.8 %all-gather.47.cloned.1.call-start = ((), (), s32[]{:S(2)}) async-start(), calls=%async_computation.18 | async-start | bytes 1572864 | tf_op jit(solution)/shard_map/all_gather | solution.py:30
  1079.6 547.0 %all-gather.43.cloned.1.call-start = ((), (), s32[]{:S(2)}) async-start(), calls=%async_computation.16 | async-start | bytes 1572864 | tf_op jit(solution)/shard_map/all_gather | solution.py:30
  1358.2 282.1 %all-gather.39.cloned.1.call-start = ((), (), s32[]{:S(2)}) async-start(), calls=%async_computation.14 | async-start | bytes 1572864 | tf_op jit(solution)/shard_map/all_gather | solution.py:30
  1625.2 165.6 %all-gather.59.cloned.1.call-start = ((), (), s32[]{:S(2)}) async-start(), calls=%async_computation.24 | async-start | bytes 1572864 | tf_op jit(solution)/shard_map/all_gather | solution.py:30
  1761.8 321.8 %all-gather.55.cloned.1.call-start = ((), (), s32[]{:S(2)}) async-start(), calls=%async_computation.22 | async-start | bytes 1572864 | tf_op jit(solution)/shard_map/all_gather | solution.py:30
  1783.1 607.2 %all-gather.51.cloned.1.call-start = ((), (), s32[]{:S(2)}) async-start(), calls=%async_computation.20 | async-start | bytes 1572864 | tf_op jit(solution)/shard_map/all_gather | solution.py:30
  1790.7 1572.4 %all-reduce.21.cloned.1.call-start = ((), (), s32[]{:S(2)}) async-start(), calls=%async_computation.27 | async-start | bytes 2097152
  2766.7 34.4 collective-permute-start.3
  2852.8 512.0 %reduce-scatter.19.cloned.1.call-start = ((), (), s32[]{:S(2)}) async-start(), calls=%async_computation.25 | async-start | bytes 1081344
  2873.7 492.7 %reduce-scatter.15.cloned.1.call-start = ((), (), s32[]{:S(2)}) async-start(), calls=%async_computation.11 | async-start | bytes 10485760 | tf_op jit(solution)/shard_map/reduce_scatter | solution.py:237
  2892.4 533.4 %reduce-scatter.13.cloned.1.call-start = ((), (), s32[]{:S(2)}) async-start(), calls=%async_computation.10 | async-start | bytes 10485760 | tf_op jit(solution)/shard_map/reduce_scatter | solution.py:237
  2912.2 661.4 %reduce-scatter.11.cloned.1.call-start = ((), (), s32[]{:S(2)}) async-start(), calls=%async_computation.9 | async-start | bytes 10485760 | tf_op jit(solution)/shard_map/reduce_scatter | solution.py:237
  2931.9 1479.1 %all-reduce.23.cloned.1.call-start = ((), (), s32[]{:S(2)}) async-start(), calls=%async_computation.28 | async-start | bytes 50331648 | tf_op jit(solution)/shard_map/psum | solution.py:300
  3118.2 1331.2 %reduce-scatter.17.cloned.1.call-start = ((), (), s32[]{:S(2)}) async-start(), calls=%async_computation.12 | async-start | bytes 589824 | tf_op jit(solution)/shard_map/reduce_scatter | solution.py:107
  3141.9 1437.0 %reduce-scatter.21.cloned.1.call-start = ((), (), s32[]{:S(2)}) async-start(), calls=%async_computation.26 | async-start | bytes 1081344
  (269 other events, 9044.5 us)
Sparse Core Ops, SparseCore 0:
  11.1 86.8 all-gather.44
  99.6 97.3 all-gather.40
  199.2 121.1 all-gather.36
  321.7 87.5 all-gather.48
  410.8 78.1 all-gather.52
  490.4 79.3 all-gather.56
  571.7 25.0 all-gather.32
  598.6 37.4 all-gather.34
  637.9 55.9 all-gather.30
  1079.8 10.2 all-gather.46
  1358.3 10.3 all-gather.42
  1625.3 10.5 all-gather.38
  1762.0 11.6 all-gather.58
  1783.2 11.5 all-gather.54
  1796.2 10.1 all-gather.50
  2852.9 55.8 all-reduce.20
  2910.8 126.5 reduce-scatter.18
  3039.8 169.0 reduce-scatter.14
  3211.4 214.3 reduce-scatter.12
  3428.1 145.4 reduce-scatter.10
  3576.7 834.2 all-reduce.22
  4414.7 34.6 reduce-scatter.16
  4452.3 126.4 reduce-scatter.20
where the time goes:
time: 4640 us; the launch traced here: 4590 us
  waiting for transfers between devices  1300 us (28%)
  local copies, waits for them, and re-layouts  1270 us (27%)
  matrix products  883 us (19%)
  other arithmetic  566 us (12%)
  blocking collectives  528 us (11%)
    psum x1, waiting for transfers between devices, body(): normed_sum, bc_sum = lax.psum((normed_part, bc_partial), 'mp')  832 us
    dynamic_update_slice x180, local copies, waits for them, and re-layouts, local_scan(): lax.scan(block_step, init_state, (blocked(x_heads), blocked(b_rows), bloc...  699 us
    dot_general x36, matrix products, block_step(): inner_out = jnp.einsum('tsh,shp->thp', mixing, x_part, precision=precise)  234 us
    reduce_scatter x3, waiting for transfers between devices, body(): lax.psum_scatter(partial_out, 'mp', scatter_dimension=2, tiled=True)  207 us
    all_gather x1, blocking collectives, body(): lax.all_gather(in_down, ('dp', 'seq', 'mp'), axis=1, tiled=True)  206 us
    psum x1, blocking collectives, body(): normed_sum, bc_sum = lax.psum((normed_part, bc_partial), 'mp')  202 us
    another operation x240, local copies, waits for them, and re-layouts  177 us
    another operation x75, other arithmetic  165 us
  transfers between devices with their start and end apart: 29, of which 9 were waited for; matrix products, arithmetic and copies ran while one was open for 40% of the time, Pallas kernels for 0%

commit v1 on v0

--- a/solution.py
+++ b/solution.py
@@ -1,6 +1,10 @@
+import functools
+
 import jax
 import jax.numpy as jnp
 from jax import lax
+from jax.experimental import pallas as pl
+from jax.experimental.pallas import tpu as pltpu
 from jax.sharding import PartitionSpec as P
 
 D = 2048
@@ -11,10 +15,13 @@
 R = 16
 ADAPT = 8
 DI = 4096
+HG = 4
+HALO = 16
 
 
 eps = 1e-05
 precise = lax.Precision.HIGHEST
+VMEM_LIMIT = 56 * 1024 * 1024
 
 
 def shifted(array, axis, by):
@@ -325,6 +332,667 @@
     return (jnp.stack(outputs), jnp.stack(x_grads), running[0], running[1], running[2], running[3])
 
 
+def split(v):
+    hi = v.astype(jnp.bfloat16)
+    return hi, (v - hi.astype(jnp.float32)).astype(jnp.bfloat16)
+
+
+def mm(a, b):
+    return lax.dot_general(a, b, (((1,), (0,)), ((), ())), preferred_element_type=jnp.float32)
+
+
+def mm_t(a, b):
+    return lax.dot_general(a, b, (((1,), (1,)), ((), ())), preferred_element_type=jnp.float32)
+
+
+def mm3(a, b):
+    return mm(a[0], b[0]) + mm(a[0], b[1]) + mm(a[1], b[0])
+
+
+def mm3_t(a, b):
+    return mm_t(a[0], b[0]) + mm_t(a[0], b[1]) + mm_t(a[1], b[0])
+
+
+def conv_rows(rows, halo, taps):
+    count = rows.shape[0]
+    ext = jnp.concatenate([halo, rows], axis=0).astype(jnp.float32)
+    total = taps[0:1] * ext[HALO - 3 : HALO - 3 + count]
+    for j in range(1, KC):
+        total = total + taps[j : j + 1] * ext[HALO - 3 + j : HALO - 3 + j + count]
+    return total
+
+
+def conv_rows_back(grad, taps):
+    count, width = grad.shape
+    zero = jnp.zeros((8, width), jnp.float32)
+    ext = jnp.concatenate([zero, grad, zero], axis=0)
+    total = taps[0:1] * ext[3 : 3 + count + 8]
+    for j in range(1, KC):
+        total = total + taps[j : j + 1] * ext[3 - j : 3 - j + count + 8]
+    return total
+
+
+def widen(columns, first):
+    rows = columns.shape[0]
+    lane = lax.broadcasted_iota(jnp.int32, (rows, 2 * P_SIZE), 1)
+    return jnp.where(lane < P_SIZE, columns[:, first : first + 1], columns[:, first + 1 : first + 2])
+
+
+def widen_all(columns):
+    return jnp.concatenate([widen(columns, h) for h in range(0, HG, 2)], axis=1)
+
+
+def head_sums(prod, group):
+    rows = prod.shape[1]
+    row = lax.broadcasted_iota(jnp.int32, (rows, 128), 0) // P_SIZE + group * HG
+    lane = lax.broadcasted_iota(jnp.int32, (rows, 128), 1)
+    pick = (row == lane).astype(jnp.float32).astype(jnp.bfloat16)
+    hi, lo = split(prod)
+    return mm(hi, pick) + mm(lo, pick)
+
+
+def local_kernel(
+    xin_ref, halo_ref, taps_ref, bcin_ref, bchalo_ref, bctaps_ref, cum_ref, cumt_ref, stept_ref, wt_ref, ec_ref,
+    dec_ref, skip_ref, y_ref, state_ref, bc_ref, scores_ref, bt_ref
+):
+    rows = xin_ref.shape[1]
+    blocks = rows // Q
+
+    @pl.when(pl.program_id(1) == 0)
+    def _():
+        pre = conv_rows(bcin_ref[0], bchalo_ref[0], bctaps_ref[...])
+        bc = pre * jax.nn.sigmoid(pre)
+        bc_ref[0] = bc
+        for b in range(blocks):
+            part = bc[b * Q : (b + 1) * Q]
+            b_part = split(part[:, :NS])
+            c_part = split(part[:, NS:])
+            scores_ref[b] = mm3_t(c_part, b_part)
+            hi, lo = split(part[:, :NS].T)
+            bt_ref[0, b] = hi
+            bt_ref[1, b] = lo
+
+    pre = conv_rows(xin_ref[0], halo_ref[0], taps_ref[...])
+    x = pre * jax.nn.sigmoid(pre)
+    lane = lax.broadcasted_iota(jnp.int32, (Q, 2 * P_SIZE), 1)
+    causal = lax.broadcasted_iota(jnp.int32, (Q, Q), 0) >= lax.broadcasted_iota(jnp.int32, (Q, Q), 1)
+    state = None
+    for b in range(blocks):
+        at = slice(b * Q, (b + 1) * Q)
+        scores = scores_ref[b]
+        xb = x[at]
+        if b > 0:
+            carried = widen_all(ec_ref[0, 0, at]) * mm3(split(bc_ref[0, at, NS:]), split(state))
+        for h in range(0, HG, 2):
+            pair = xb[:, h * P_SIZE : (h + 2) * P_SIZE]
+            x_hi, x_lo = split(pair)
+            both = jnp.concatenate([x_hi, x_lo], axis=1)
+            halves = []
+            for k in (h, h + 1):
+                spread = cum_ref[0, 0, at, k : k + 1] - cumt_ref[0, 0, k : k + 1, at]
+                decay = jnp.exp(jnp.where(causal, spread, -10000.0))
+                m_hi, m_lo = split(scores * decay * stept_ref[0, 0, k : k + 1, at])
+                first = mm(m_hi, both)
+                halves.append(first[:, : 2 * P_SIZE] + first[:, 2 * P_SIZE :] + mm(m_lo, x_hi))
+            skip = skip_ref[0:1, h * P_SIZE : (h + 2) * P_SIZE]
+            y_pair = jnp.where(lane < P_SIZE, halves[0], halves[1]) + skip * pair
+            if b > 0:
+                y_pair = y_pair + carried[:, h * P_SIZE : (h + 2) * P_SIZE]
+            y_ref[0, at, h * P_SIZE : (h + 2) * P_SIZE] = y_pair
+        wx = xb * widen_all(wt_ref[0, 0, at])
+        update = mm3((bt_ref[0, b], bt_ref[1, b]), split(wx))
+        state = update if state is None else dec_ref[0, b : b + 1] * state + update
+    state_ref[0] = state
+
+
+def carry_kernel(y_ref, state_ref, bc_ref, el_ref, z_ref, mixed_ref, sum_ref):
+    group = pl.program_id(1)
+    c_part = split(bc_ref[0, :, NS:])
+    mixed = y_ref[0] + widen_all(el_ref[0, 0]) * mm3(c_part, split(state_ref[0]))
+    mixed_ref[0] = mixed
+    z = z_ref[0]
+    gated = mixed * (z * jax.nn.sigmoid(z))
+    square = gated * gated
+    part = square[:, :128]
+    for k in range(1, square.shape[1] // 128):
+        part = part + square[:, k * 128 : (k + 1) * 128]
+
+    @pl.when(group == 0)
+    def _():
+        sum_ref[0] = part
+
+    @pl.when(group > 0)
+    def _():
+        sum_ref[0] += part
+
+
+def gate_back_kernel(
+    gs_ref, mixed_ref, z_ref, inv_ref, coef_ref, gain_ref, bc_ref, el_ref, dy_ref, gz_ref, lam_ref, q_ref, ct_ref
+):
+    group = pl.program_id(1)
+
+    @pl.when(group == 0)
+    def _():
+        hi, lo = split(bc_ref[0, :, NS:].T)
+        ct_ref[0] = hi
+        ct_ref[1] = lo
+
+    z = z_ref[0]
+    mixed = mixed_ref[0]
+    sig = jax.nn.sigmoid(z)
+    act = z * sig
+    g_gated = gs_ref[0] * gain_ref[...] * inv_ref[0] - (mixed * act) * coef_ref[0]
+    dy = g_gated * act
+    dy_ref[0] = dy
+    gz_ref[0] = (g_gated * mixed * (sig * (1.0 + z * (1.0 - sig)))).astype(jnp.bfloat16)
+    lam_ref[0] = mm3((ct_ref[0], ct_ref[1]), split(dy * widen_all(el_ref[0, 0])))
+    q = head_sums(dy * mixed, group)
+
+    @pl.when(group == 0)
+    def _():
+        q_ref[0] = q
+
+    @pl.when(group > 0)
+    def _():
+        q_ref[0] += q
+
+
+def scan_back_kernel(
+    dy_ref, xin_ref, halo_ref, taps_ref, bc_ref, cum_ref, cumt_ref, step_ref, wt0_ref, ec_ref, dec_ref, skip_ref,
+    state_ref, lam_ref, gx_ref, head_ref, tail_ref, gbc_ref, xu_ref, dx_ref, scorest_ref, dscorest_ref, bt_ref, ct_ref
+):
+    group = pl.program_id(1)
+    rows = xin_ref.shape[1]
+    blocks = rows // Q
+
+    @pl.when(group == 0)
+    def _():
+        for b in range(blocks):
+            part = bc_ref[0, b * Q : (b + 1) * Q]
+            scorest_ref[b] = mm3_t(split(part[:, :NS]), split(part[:, NS:]))
+            dscorest_ref[b] = jnp.zeros((Q, Q), jnp.float32)
+            hi, lo = split(part[:, :NS].T)
+            bt_ref[0, b] = hi
+            bt_ref[1, b] = lo
+            hi, lo = split(part[:, NS:].T)
+            ct_ref[0, b] = hi
+            ct_ref[1, b] = lo
+        gbc_ref[0] = jnp.zeros((rows, 2 * NS), jnp.float32)
+        xu_ref[0] = jnp.zeros((rows, 128), jnp.float32)
+        dx_ref[0] = jnp.zeros((rows, 128), jnp.float32)
+
+    pre = conv_rows(xin_ref[0], halo_ref[0], taps_ref[...])
+    sig = jax.nn.sigmoid(pre)
+    x = pre * sig
+    lane = lax.broadcasted_iota(jnp.int32, (Q, 2 * P_SIZE), 1)
+    causal = lax.broadcasted_iota(jnp.int32, (Q, Q), 0) <= lax.broadcasted_iota(jnp.int32, (Q, Q), 1)
+    states = [state_ref[0]]
+    for b in range(blocks - 1):
+        at = slice(b * Q, (b + 1) * Q)
+        wx = x[at] * widen_all(wt0_ref[0, 0, at] * step_ref[0, 0, at])
+        states.append(dec_ref[0, b : b + 1] * states[b] + mm3((bt_ref[0, b], bt_ref[1, b]), split(wx)))
+    lam = lam_ref[0]
+    g_parts = [None] * blocks
+    for b in reversed(range(blocks)):
+        at = slice(b * Q, (b + 1) * Q)
+        xb = x[at]
+        dy = dy_ref[0, at]
+        scores = scorest_ref[b]
+        dscores = dscorest_ref[b]
+        u_parts = []
+        for h in range(0, HG, 2):
+            pair = slice(h * P_SIZE, (h + 2) * P_SIZE)
+            x_hi, x_lo = split(xb[:, pair])
+            d_hi, d_lo = split(dy[:, pair])
+            both = jnp.concatenate([d_hi, d_lo], axis=1)
+            halves = []
+            for k in (h, h + 1):
+                mine = (lane < P_SIZE) if k == h else (lane >= P_SIZE)
+                spread = cumt_ref[0, 0, k : k + 1, at] - cum_ref[0, 0, at, k : k + 1]
+                decay = jnp.exp(jnp.where(causal, spread, -10000.0))
+                zero = jnp.zeros_like(x_hi)
+                xm_hi = jnp.where(mine, x_hi, zero)
+                xm_lo = jnp.where(mine, x_lo, zero)
+                dm = mm_t(xm_hi, d_hi) + mm_t(xm_hi, d_lo) + mm_t(xm_lo, d_hi)
+                dscores = dscores + dm * decay * step_ref[0, 0, at, k : k + 1]
+                m_hi, m_lo = split(scores * decay)
+                first = mm(m_hi, both)
+                halves.append(first[:, : 2 * P_SIZE] + first[:, 2 * P_SIZE :] + mm(m_lo, d_hi))
+            u_parts.append(jnp.where(lane < P_SIZE, halves[0], halves[1]))
+        dscorest_ref[b] = dscores
+        wt0 = widen_all(wt0_ref[0, 0, at])
+        step = widen_all(step_ref[0, 0, at])
+        lam_s = split(lam)
+        part = bc_ref[0, at]
+        u = jnp.concatenate(u_parts, axis=1) + wt0 * mm3(split(part[:, :NS]), lam_s)
+        ev = split(widen_all(ec_ref[0, 0, at]) * dy)
+        gbc_ref[0, at, :NS] += mm3_t(split(wt0 * step * xb), lam_s)
+        gbc_ref[0, at, NS:] += mm3_t(ev, split(states[b]))
+        if b > 0:
+            lam = dec_ref[0, b : b + 1] * lam + mm3((ct_ref[0, b], ct_ref[1, b]), ev)
+        xu_ref[0, at] += head_sums(xb * u, group)
+        dx_ref[0, at] += head_sums(xb * dy * skip_ref[0:1], group)
+        g_parts[b] = step * u + skip_ref[0:1] * dy
+    g_pre = jnp.concatenate(g_parts, axis=0) * (sig * (1.0 + pre * (1.0 - sig)))
+    g_ext = conv_rows_back(g_pre, taps_ref[...])
+    gx_ref[0] = g_ext[8:].astype(jnp.bfloat16)
+    head_ref[0] = g_ext[:8]
+    tail_ref[0] = g_ext[rows:]
+
+    @pl.when(group == pl.num_programs(1) - 1)
+    def _():
+        for b in range(blocks):
+            at = slice(b * Q, (b + 1) * Q)
+            part = bc_ref[0, at]
+            ds = dscorest_ref[b]
+            gbc_ref[0, at, :NS] += mm3(split(ds), split(part[:, NS:]))
+            gbc_ref[0, at, NS:] += mm3(split(ds.T), split(part[:, :NS]))
+
+
+def bc_back_kernel(g_ref, in_ref, halo_ref, taps_ref, out_ref, head_ref, tail_ref):
+    rows = in_ref.shape[1]
+    pre = conv_rows(in_ref[0], halo_ref[0], taps_ref[...])
+    sig = jax.nn.sigmoid(pre)
+    g_ext = conv_rows_back(g_ref[0] * (sig * (1.0 + pre * (1.0 - sig))), taps_ref[...])
+    out_ref[0] = g_ext[8:]
+    head_ref[0] = g_ext[:8]
+    tail_ref[0] = g_ext[rows:]
+
+
+def block(shape, index):
+    return pl.BlockSpec(shape, index)
+
+
+def call(kernel, name, groups, ins, outs, scratch, flops, size):
+    return pl.pallas_call(
+        kernel,
+        name=name,
+        grid=(1, groups),
+        in_specs=[s for _, s in ins],
+        out_specs=[s for _, s in outs],
+        out_shape=[s for s, _ in outs],
+        scratch_shapes=scratch,
+        compiler_params=pltpu.CompilerParams(vmem_limit_bytes=VMEM_LIMIT),
+        cost_estimate=pl.CostEstimate(flops=flops, bytes_accessed=size, transcendentals=0),
+    )(*[a for a, _ in ins])
+
+
+def split_low(v):
+    hi = lax.reduce_precision(v, 8, 7)
+    return jnp.concatenate([hi.astype(jnp.bfloat16), (v - hi).astype(jnp.bfloat16)], axis=-1)
+
+
+def dot32(a, b, dims=((1,), (0,))):
+    return lax.dot_general(a, b, (dims, ((), ())), preferred_element_type=jnp.float32)
+
+
+def fold(v):
+    half = v.shape[-1] // 2
+    return v[..., :half] + v[..., half:]
+
+
+def fast_body(
+    x_in, cotangent, lengths, adapter_ids, norm_gain, w_zx, w_bc, w_dt, dt_bias, a_log, d_skip, conv_x, conv_bc,
+    gate_gain, w_out, in_down, in_up, out_down, out_up
+):
+    bf16, f32 = jnp.bfloat16, jnp.float32
+    micros, _, seg, feats = x_in.shape
+    nz, nd = lax.axis_size("mp"), lax.axis_size("dp")
+    core, z = lax.axis_index("seq"), lax.axis_index("mp")
+    own = seg // nz
+    tokens = 2 * own
+    heads = dt_bias.shape[0] * nz // 2
+    chan = heads * P_SIZE
+    part = chan // nz
+    groups = heads // HG
+    wide = HG * P_SIZE
+    blocks = tokens // Q
+    swap = [(0, 1), (1, 0)]
+
+    def other(v):
+        return lax.ppermute(v, "seq", swap)
+
+    def pair_cat(mine, theirs, axis):
+        return jnp.where(
+            core == 0, jnp.concatenate([mine, theirs], axis), jnp.concatenate([theirs, mine], axis)
+        )
+
+    def halves(v, axis, parts=2):
+        shape = v.shape[:axis] + (parts, v.shape[axis] // parts) + v.shape[axis + 1 :]
+        v = v.reshape(shape)
+        return (
+            lax.dynamic_index_in_dim(v, core, axis, False),
+            lax.dynamic_index_in_dim(v, 1 - core, axis, False),
+        )
+
+    zx_mine, zx_theirs = halves(w_zx, 2)
+    out_mine, out_theirs = halves(w_out, 0)
+    up_mine, up_theirs = halves(in_up, 2)
+    down_mine, down_theirs = halves(out_down, 0)
+    dt_mine, dt_theirs = halves(w_dt, 1)
+    bc_piece = lax.dynamic_slice_in_dim(w_bc, z * (w_bc.shape[0] // nz), w_bc.shape[0] // nz, 0)
+    same = (bc_piece, in_down, out_up)
+    small = [up_mine, down_mine, dt_mine, *same]
+    small_shapes = [v.shape for v in small]
+    pack_mine = jnp.concatenate([v.reshape(-1) for v in small])
+    pack_theirs = jnp.concatenate([v.reshape(-1) for v in (up_theirs, down_theirs, dt_theirs, *same)])
+    zx_pair = pair_cat(zx_mine, other(zx_theirs), 0)
+    out_pair = pair_cat(out_mine, other(out_theirs), 1)
+    pack_pair = pair_cat(pack_mine[None], other(pack_theirs)[None], 0)
+    params = jnp.concatenate([dt_bias, a_log, d_skip, gate_gain, conv_x.reshape(-1)])
+    params = lax.all_gather(params, "mp")
+    packs = lax.all_gather(pack_pair, ("dp", "mp")).reshape(nd, nz, 2, -1)
+    zx_all = lax.all_gather(zx_pair, ("dp", "mp")).reshape((nd, nz) + zx_pair.shape)
+    out_all = lax.all_gather(out_pair, ("dp", "mp")).reshape((nd, nz) + out_pair.shape)
+    zx_weight = jnp.transpose(zx_all, (3, 0, 2, 1, 4)).reshape(2, D, chan)
+    out_weight = jnp.transpose(out_all, (1, 2, 0, 3)).reshape(chan, D)
+    pieces = []
+    at = 0
+    for shape in small_shapes:
+        size = 1
+        for n in shape:
+            size *= n
+        pieces.append(packs[..., at : at + size].reshape((nd, nz, 2) + shape))
+        at += size
+    up_in = jnp.transpose(pieces[0], (0, 2, 3, 4, 1, 5)).reshape(ADAPT, R, 2 * chan)
+    down_out = jnp.transpose(pieces[1], (0, 2, 4, 1, 3)).reshape(ADAPT, R, chan)
+    dt_weight = jnp.transpose(pieces[2], (0, 2, 3, 1, 4)).reshape(D, heads)
+    bc_weight = jnp.transpose(pieces[3], (0, 2, 1, 3, 4)).reshape(D, 2 * NS)
+    wide_down = jnp.transpose(pieces[4], (3, 5, 0, 2, 1, 4)).reshape(ADAPT, R, D)
+    wide_up = jnp.transpose(pieces[5], (3, 0, 2, 1, 4)).reshape(ADAPT, R, D)
+
+    hl = dt_bias.shape[0]
+    def own_part(v):
+        v = v.reshape(v.shape[0], 2, v.shape[1] // 2)
+        return lax.dynamic_index_in_dim(v, core, 1, False).reshape(-1)
+    bias = own_part(params[:, :hl])
+    rate = -jnp.exp(own_part(params[:, hl : 2 * hl]))
+    skip = jnp.repeat(own_part(params[:, 2 * hl : 3 * hl]), P_SIZE)[None]
+    width = gate_gain.shape[0]
+    gain = own_part(params[:, 3 * hl : 3 * hl + width])[None]
+    taps = params[:, 3 * hl + width :].reshape(nz, KC, 2, part)
+    taps = jnp.transpose(lax.dynamic_index_in_dim(taps, core, 2, False), (1, 0, 2)).reshape(KC, chan)
+
+    chunk = nz // 2
+    mine = (z % chunk) * 2 + core
+
+    def flat(c, zz):
+        return c * nz + zz
+
+    def route(step):
+        pairs = []
+        for c in range(2):
+            for zz in range(nz):
+                q = zz ^ step
+                pairs.append((flat(c, zz), flat(q % 2, c * chunk + q // 2)))
+        return pairs
+
+    def to_rows(v):
+        got = [
+            lax.ppermute(lax.dynamic_slice_in_dim(v, (z ^ step) * own, own, 1), ("seq", "mp"), route(step))
+            for step in range(nz)
+        ]
+        full = jnp.zeros(v.shape[:1] + (own, nz * feats), v.dtype)
+        for step in range(nz):
+            full = lax.dynamic_update_slice_in_dim(full, got[step], (mine ^ step) * feats, 2)
+        return full
+
+    def to_features(v):
+        full = jnp.zeros(v.shape[:1] + (seg, feats), v.dtype)
+        for step in range(nz):
+            piece = lax.dynamic_slice_in_dim(v, (mine ^ step) * feats, feats, 2)
+            got = lax.ppermute(piece, ("seq", "mp"), [(b, a) for a, b in route(step)])
+            full = lax.dynamic_update_slice_in_dim(full, got, (z ^ step) * own, 1)
+        return full
+
+    x_rows = to_rows(x_in[:, 0])
+    cot_rows = to_rows(cotangent[:, 0])
+    start = z * tokens
+    own_pos = start + core * own + jnp.arange(own)
+    all_pos = start + jnp.arange(tokens)
+    tri = (jnp.arange(Q)[:, None] >= jnp.arange(Q)[None, :]).astype(f32)
+    tri_all = (jnp.arange(tokens)[:, None] <= jnp.arange(tokens)[None, :]).astype(f32)
+    forward_edge = [(i, i + 1) for i in range(nz - 1)]
+    backward_edge = [(i + 1, i) for i in range(nz - 1)]
+
+    m3 = lambda m, g: (0, 0, g)
+    m0 = lambda m, g: (0, 0, 0)
+    g4 = lambda m, g: (0, g, 0, 0)
+    g2 = lambda m, g: (0, g)
+    z2 = lambda m, g: (0, 0)
+    col = block((1, 1, tokens, HG), g4)
+    row = block((1, 1, HG, tokens), g4)
+    chan_block = block((1, tokens, wide), m3)
+    halo_block = block((1, HALO, wide), m3)
+    taps_block = block((KC, wide), g2)
+    line_block = block((1, wide), g2)
+    state_block = block((1, NS, wide), m3)
+    dec_block = block((1, blocks, wide), m3)
+    bc_block = block((1, tokens, 2 * NS), m0)
+    one_col = block((1, tokens, 1), m0)
+    sums_block = block((1, tokens, 128), m0)
+    tok_f32 = jax.ShapeDtypeStruct((1, tokens, chan), f32)
+    tok_b16 = jax.ShapeDtypeStruct((1, tokens, chan), bf16)
+    state_f32 = jax.ShapeDtypeStruct((1, NS, chan), f32)
+    bc_f32 = jax.ShapeDtypeStruct((1, tokens, 2 * NS), f32)
+    sums_f32 = jax.ShapeDtypeStruct((1, tokens, 128), f32)
+    edge_f32 = jax.ShapeDtypeStruct((1, 8, chan), f32)
+    edge_block = block((1, 8, wide), m3)
+    act_bytes = tokens * chan * 4
+
+    def cols(v):
+        return jnp.transpose(v.reshape(tokens, groups, HG), (1, 0, 2))[None]
+
+    def rows_of(v):
+        return jnp.transpose(v.reshape(tokens, groups, HG), (1, 2, 0))[None]
+
+    S = [dict() for _ in range(micros)]
+    for m in range(micros):
+        s = S[m]
+        x = x_rows[m].astype(f32)
+        s["inv"] = lax.rsqrt(jnp.mean(x * x, axis=-1, keepdims=True) + eps)
+        low_own = (x * s["inv"] * norm_gain).astype(bf16)
+        s["low"] = pair_cat(low_own, other(low_own), 0)
+        cot = cot_rows[m]
+        s["mask_own"] = (own_pos < lengths[m, 0]).astype(f32)[:, None]
+        s["mask"] = (all_pos < lengths[m, 0]).astype(f32)[:, None]
+        gb_own = cot * s["mask_own"].astype(bf16)
+        s["gb"] = pair_cat(gb_own, other(gb_own), 0)
+        k = adapter_ids[m, 0]
+        s["pick"] = (k == jnp.arange(ADAPT)).astype(f32)
+        s["a_in"] = lax.dynamic_index_in_dim(wide_down, k, 0, False)
+        s["u_in"] = lax.dynamic_index_in_dim(up_in, k, 0, False)
+        s["a_out"] = lax.dynamic_index_in_dim(down_out, k, 0, False)
+        s["u_out"] = lax.dynamic_index_in_dim(wide_up, k, 0, False)
+
+    for m in range(micros):
+        s = S[m]
+        low = s["low"]
+        s["lr"] = split_low(dot32(low, s["a_in"], ((1,), (1,))))
+        u2 = jnp.concatenate([s["u_in"], s["u_in"]], 0)
+        s["z"] = (dot32(low, zx_weight[0]) + dot32(s["lr"], u2[:, :chan]))[None]
+        s["xin"] = (dot32(low, zx_weight[1]) + dot32(s["lr"], u2[:, chan:])).astype(bf16)[None]
+        s["bcin"] = dot32(low, bc_weight).astype(bf16)[None]
+        s["rate_in"] = dot32(low, dt_weight) + bias
+        tail = jnp.concatenate([s["xin"][:, tokens - HALO :], s["bcin"][:, tokens - HALO :]], axis=2)
+        halo = lax.ppermute(tail, "mp", forward_edge)
+        s["halo"], s["bchalo"] = halo[..., :chan], halo[..., chan:]
+        step = jax.nn.softplus(s["rate_in"]) * s["mask"]
+        log = (step * rate).reshape(blocks, Q, heads)
+        cum = jnp.einsum("ts,bsh->bth", tri, log, precision=precise)
+        total = cum[:, -1]
+        before = jnp.concatenate([jnp.zeros((1, heads), f32), jnp.cumsum(total, axis=0)[:-1]], 0)
+        s["step"] = cols(step)
+        s["stept"] = rows_of(step)
+        s["cum"] = cols(cum)
+        s["cumt"] = rows_of(cum)
+        rest = jnp.exp(total[:, None] - cum).reshape(tokens, heads)
+        s["wt0"] = cols(rest)
+        s["wt"] = cols(rest * step)
+        s["ec"] = cols(jnp.exp(cum))
+        s["el"] = cols(jnp.exp(cum + before[:, None]))
+        s["dec"] = jnp.repeat(jnp.exp(total), P_SIZE, axis=1)[None]
+        s["all"] = jnp.repeat(jnp.exp(jnp.sum(total, axis=0)), P_SIZE)[None, None]
+        s["y"], s["sloc"], s["bc"] = call(
+            local_kernel, "ssd_local", groups,
+            [(s["xin"], chan_block), (s["halo"], halo_block), (taps, taps_block),
+             (s["bcin"], bc_block), (s["bchalo"], block((1, HALO, 2 * NS), m0)), (conv_bc, block((KC, 2 * NS), z2)),
+             (s["cum"], col), (s["cumt"], row), (s["stept"], row), (s["wt"], col), (s["ec"], col),
+             (s["dec"], dec_block), (skip, line_block)],
+            [(tok_f32, chan_block), (state_f32, state_block), (bc_f32, bc_block)],
+            [pltpu.VMEM((blocks, Q, Q), f32), pltpu.VMEM((2, blocks, NS, Q), bf16)],
+            6 * tokens * Q * chan * 2, act_bytes * 2,
+        )
+    for m in range(micros):
+        s = S[m]
+        state = jnp.zeros_like(s["sloc"])
+        for hop in range(nz - 1):
+            state = state + lax.ppermute(s["all"] * state + s["sloc"], "mp", [(hop, hop + 1)])
+        s["state"] = state
+        s["send"] = s["all"] * state + s["sloc"]
+    for m in range(micros):
+        s = S[m]
+        s["mixed"], square = call(
+            carry_kernel, "ssd_carry", groups,
+            [(s["y"], chan_block), (s["state"], state_block), (s["bc"], bc_block), (s["el"], col), (s["z"], chan_block)],
+            [(tok_f32, chan_block), (sums_f32, sums_block)], [], 6 * tokens * NS * chan, act_bytes * 3,
+        )
+        square = jnp.sum(square, axis=-1)
+        s["inv_gate"] = lax.rsqrt((square + other(square)) / DI + eps)[..., None]
+        zz = s["z"]
+        s["gated"] = s["mixed"] * (zz * jax.nn.sigmoid(zz))
+        scaled = (s["gated"] * s["inv_gate"] * gain).astype(bf16)[0]
+        s["scaled"] = scaled
+        gb = s["gb"]
+        s["ro"] = split_low(dot32(scaled, s["a_out"], ((1,), (1,))))
+        rank_grad = dot32(gb, s["u_out"], ((1,), (1,)))
+        s["rg"] = split_low(rank_grad)
+        a2 = jnp.concatenate([s["a_out"], s["a_out"]], 0)
+        s["gs"] = (dot32(gb, out_weight, ((1,), (1,))) + dot32(s["rg"], a2))[None]
+        dots = jnp.sum(s["gs"] * gain * s["gated"], axis=-1)
+        inv = s["inv_gate"]
+        s["coef"] = inv**3 * ((dots + other(dots)) / DI)[..., None]
+        s["dy"], s["gz"], s["lloc"], s["q"] = call(
+            gate_back_kernel, "gate_back", groups,
+            [(s["gs"], chan_block), (s["mixed"], chan_block), (zz, chan_block), (inv, one_col), (s["coef"], one_col),
+             (gain, line_block), (s["bc"], bc_block), (s["el"], col)],
+            [(tok_f32, chan_block), (tok_b16, chan_block), (state_f32, state_block), (sums_f32, sums_block)],
+            [pltpu.VMEM((2, NS, tokens), bf16)], 6 * tokens * NS * chan, act_bytes * 5,
+        )
+    for m in range(micros):
+        s = S[m]
+        lam = jnp.zeros_like(s["lloc"])
+        for hop in range(nz - 1, 0, -1):
+            lam = lam + lax.ppermute(s["all"] * lam + s["lloc"], "mp", [(hop, hop - 1)])
+        s["lam"] = lam
+
+    def reduce_rows(v):
+        theirs = lax.dynamic_slice_in_dim(v, (1 - core) * own, own, 0)
+        return lax.dynamic_slice_in_dim(v, core * own, own, 0) + other(theirs)
+
+    outs = []
+    for m in range(micros):
+        s = S[m]
+        u2 = jnp.concatenate([s["u_out"], s["u_out"]], 0)
+        branch = reduce_rows(dot32(s["scaled"], out_weight) + dot32(s["ro"], u2))
+        rows = (x_rows[m].astype(f32) + s["mask_own"] * branch).astype(bf16)
+        outs.append(to_features(rows[None]))
+        s["g_up_out"] = dot32(s["ro"], s["gb"], ((0,), (0,)))
+        s["g_up_out"] = s["g_up_out"][:R] + s["g_up_out"][R:]
+        g_out = dot32(s["rg"], s["scaled"], ((0,), (0,)))
+        s["g_out"] = g_out[:R] + g_out[R:]
+
+    grads = []
+    for m in range(micros):
+        s = S[m]
+        gx, head, tail, gbc, xu, dx = call(
+            scan_back_kernel, "ssd_back", groups,
+            [(s["dy"], chan_block), (s["xin"], chan_block), (s["halo"], halo_block), (taps, taps_block), (s["bc"], bc_block),
+             (s["cum"], col), (s["cumt"], row), (s["step"], col), (s["wt0"], col), (s["ec"], col), (s["dec"], dec_block),
+             (skip, line_block), (s["state"], state_block), (s["lam"], state_block)],
+            [(tok_b16, chan_block), (edge_f32, edge_block), (edge_f32, edge_block), (bc_f32, bc_block), (sums_f32, sums_block),
+             (sums_f32, sums_block)],
+            [pltpu.VMEM((blocks, Q, Q), f32), pltpu.VMEM((blocks, Q, Q), f32), pltpu.VMEM((2, blocks, NS, Q), bf16),
+             pltpu.VMEM((2, blocks, NS, Q), bf16)],
+            12 * tokens * Q * chan * 2, act_bytes * 3,
+        )
+        gbc = gbc + other(gbc)
+        one = lambda m, g: (0, 0, 0)
+        edge_bc = jax.ShapeDtypeStruct((1, 8, 2 * NS), f32)
+        gbc, bhead, btail = call(
+            bc_back_kernel, "bc_back", 1,
+            [(gbc, bc_block), (s["bcin"], bc_block), (s["bchalo"], block((1, HALO, 2 * NS), one)),
+             (conv_bc, block((KC, 2 * NS), z2))],
+            [(bc_f32, bc_block), (edge_bc, block((1, 8, 2 * NS), one)), (edge_bc, block((1, 8, 2 * NS), one))],
+            [], 0, tokens * 2 * NS * 8,
+        )
+        back = lax.ppermute(jnp.concatenate([head, bhead], 2), "mp", backward_edge)
+        tail = tail.at[:, 8 - (KC - 1) :].add(back[:, 8 - (KC - 1) :, :chan])
+        btail = btail.at[:, 8 - (KC - 1) :].add(back[:, 8 - (KC - 1) :, chan:])
+        gx = lax.dynamic_update_slice_in_dim(gx, tail.astype(bf16), tokens - 8, 1)[0]
+        gbc = lax.dynamic_update_slice_in_dim(gbc, btail, tokens - 8, 1)[0].astype(bf16)
+        step = s["step"][0].transpose(1, 0, 2).reshape(tokens, heads)
+        xu = xu[0, :, :heads]
+        flow = s["q"][0, :, :heads] - dx[0, :, :heads] - step * xu
+        ends = jnp.sum((s["lam"] * s["send"]).reshape(NS, heads, P_SIZE), axis=(0, 2))
+        g_log = jnp.einsum("ts,sh->th", tri_all, flow, precision=precise) + ends
+        g_rate = ((xu + g_log * rate) * s["mask"] * jax.nn.sigmoid(s["rate_in"])).astype(bf16)
+        gz = s["gz"][0]
+        low = s["low"]
+        ri = dot32(gz, s["u_in"][:, :chan], ((1,), (1,))) + dot32(gx, s["u_in"][:, chan:], ((1,), (1,)))
+        ri = split_low(ri)
+        lr = s["lr"]
+        s["g_up_z"] = dot32(lr, gz, ((0,), (0,)))
+        s["g_up_x"] = dot32(lr, gx, ((0,), (0,)))
+        s["g_up_z"] = s["g_up_z"][:R] + s["g_up_z"][R:]
+        s["g_up_x"] = s["g_up_x"][:R] + s["g_up_x"][R:]
+        g_down = dot32(ri, low, ((0,), (0,)))
+        s["g_down"] = g_down[:R] + g_down[R:]
+        a2 = jnp.concatenate([s["a_in"], s["a_in"]], 0)
+        half = lax.dynamic_slice_in_dim(gbc, core * NS, NS, 1)
+        bc_half = lax.dynamic_slice_in_dim(bc_weight, core * NS, NS, 1)
+        g_low = (
+            dot32(gz, zx_weight[0], ((1,), (1,)))
+            + dot32(gx, zx_weight[1], ((1,), (1,)))
+            + dot32(jnp.concatenate([half, g_rate], 1), jnp.concatenate([bc_half, dt_weight], 1), ((1,), (1,)))
+            + dot32(ri, a2)
+        )
+        g_normed = reduce_rows(g_low)
+        gn = g_normed * norm_gain
+        x = x_rows[m].astype(f32)
+        inv = s["inv"]
+        x_grad = cot_rows[m].astype(f32) + inv * gn - x * (inv**3 * jnp.mean(gn * x, axis=-1, keepdims=True))
+        grads.append(to_features(x_grad[None]))
+
+    picks = jnp.stack([s["pick"] for s in S])
+    near = []
+    for s in S:
+        near.append(
+            jnp.concatenate(
+                [s["g_up_z"].reshape(R, nz, part), s["g_up_x"].reshape(R, nz, part), s["g_out"].reshape(R, nz, part)], 2
+            )
+        )
+    near = jnp.transpose(jnp.stack(near), (2, 0, 1, 3))
+    near = lax.psum_scatter(near, "mp", scatter_dimension=0, tiled=False)
+    near = jnp.einsum("ma,mrf->arf", picks, near, precision=precise)
+    near = lax.psum_scatter(near, "dp", scatter_dimension=0, tiled=True)
+    keep = lax.dynamic_index_in_dim(near, core, 0, False)
+    give = lax.dynamic_index_in_dim(near, 1 - core, 0, False)
+    near = pair_cat(keep[None], other(give)[None], 0)
+    g_in_up = jnp.transpose(near[:, :, : 2 * part].reshape(2, R, 2, part), (1, 2, 0, 3)).reshape(R, 2, 2 * part)
+    g_out_down = jnp.transpose(near[:, :, 2 * part :], (0, 2, 1)).reshape(2 * part, R)
+    far = jnp.stack([jnp.stack([s["g_down"], s["g_up_out"]]) for s in S])
+    each = D // (nd * 2 * nz)
+    far = far.reshape(micros, 2, R, nd, 2, nz, each)
+    far = jnp.transpose(far, (4, 5, 0, 1, 2, 3, 6)).reshape(2 * nz, micros, 2, R, nd, each)
+    far = lax.psum_scatter(far, ("seq", "mp"), scatter_dimension=0, tiled=False)
+    far = jnp.einsum("ma,mkrde->dakre", picks, far, precision=precise)
+    far = lax.psum_scatter(far, "dp", scatter_dimension=0, tiled=False)
+    g_in_down = jnp.transpose(far[:, 0], (0, 2, 1))
+    g_out_up = far[:, 1].reshape(ADAPT * R, each)
+    return (jnp.stack(outs), jnp.stack(grads), g_in_down, g_in_up, g_out_down, g_out_up)
+
+
 def solution(mesh):
     in_specs = (
         P(None, "dp", "seq", "mp"),
@@ -355,4 +1023,12 @@
         P("mp", ("dp", "seq")),
         P(None, ("dp", "seq", "mp")),
     )
-    return jax.shard_map(body, mesh=mesh, in_specs=in_specs, out_specs=out_specs, check_vma=False)
+    sizes = dict(mesh.shape)
+    by_chip = (
+        sizes["seq"] == 2
+        and sizes["dp"] * 2 == ADAPT
+        and sizes["mp"] % 2 == 0
+        and sizes["mp"] & (sizes["mp"] - 1) == 0
+        and (2048 // sizes["mp"]) % Q == 0
+    )
+    return jax.shard_map(fast_body if by_chip else body, mesh=mesh, in_specs=in_specs, out_specs=out_specs, check_vma=False)

time: 4640 us -> 1630 us (0.35)
  local copies, waits for them, and re-layouts: 1270 us -> 291 us
  waiting for transfers between devices: 1300 us -> 495 us
  matrix products: 883 us -> 254 us
  blocking collectives: 528 us -> 0 us
  other arithmetic: 566 us -> 137 us
  Pallas kernels: 0 us -> 246 us
  starting transfers between devices: 16.8 us -> 168 us
    psum x1 -> x0, waiting for transfers between devices: 832 us -> none  [body(): normed_sum, bc_sum = lax.psum((normed_part, bc_partial), 'mp')]
    dynamic_update_slice x180 -> x35, local copies, waits for them, and re-layouts: 699 us -> 9.65 us  [the longest x24 5.88 us: to_features(): full = lax.dynamic_update_slice_in_dim(full, got, (z ^ step) * own, 1)]
    dot_general x222 -> x80, matrix products: 883 us -> 254 us  [the longest x72 244 us: dot32(): lax.dot_general(a, b, (dims, ((), ())), preferred_element_type=jnp.float32)]
    ppermute x6 -> x81, waiting for transfers between devices: 0.03 us -> 446 us  [the longest x8 164 us: to_rows(): lax.ppermute(lax.dynamic_slice_in_dim(v, (z ^ step) * own, own, 1), ('seq...]
    all_gather x5 -> x0, blocking collectives: 309 us -> none  [the longest x1 206 us: body(): lax.all_gather(in_down, ('dp', 'seq', 'mp'), axis=1, tiled=True)]
    pallas_call x0 -> x15, Pallas kernels: none -> 246 us  [call(): pl.pallas_call(kernel, name=name, grid=(1, groups), in_specs=[s for _, s...]
    psum x2 -> x0, blocking collectives: 215 us -> none  [the longest x1 202 us: body(): normed_sum, bc_sum = lax.psum((normed_part, bc_partial), 'mp')]
    reduce_scatter x4 -> x3, waiting for transfers between devices: 216 us -> 4.45 us  [the longest x1 4.43 us: fast_body(): far = lax.psum_scatter(far, ('seq', 'mp'), scatter_dimension=0, tiled=False)]
  transfers between devices with their start and end apart: 29 -> 89, of which waited for: 9 -> 30; matrix products, arithmetic and copies ran while one was open for 40% -> 35% of each run, Pallas kernels for 0% -> 15%
where the time goes in v1:
time: 1630 us; the launch traced here: 1620 us
  waiting for transfers between devices  495 us (30%)
  local copies, waits for them, and re-layouts  291 us (18%)
  matrix products  254 us (16%)
  Pallas kernels  246 us (15%)
  starting transfers between devices  168 us (10%)
  other arithmetic  137 us (8%)
  between operations  27 us (2%)
    pallas_call x15, Pallas kernels, call(): pl.pallas_call(kernel, name=name, grid=(1, groups), in_specs=[s for _, s...  246 us
    dot_general x72, matrix products, dot32(): lax.dot_general(a, b, (dims, ((), ())), preferred_element_type=jnp.float32)  244 us
    ppermute x8, waiting for transfers between devices, to_rows(): lax.ppermute(lax.dynamic_slice_in_dim(v, (z ^ step) * own, own, 1), ('seq...  164 us
    ppermute x24, waiting for transfers between devices, to_features(): got = lax.ppermute(piece, ('seq', 'mp'), [(b, a) for a, b in route(step)])  162 us
    ppermute x9, waiting for transfers between devices, fast_body(): lax.ppermute(s['all'] * state + s['sloc'], 'mp', [(hop, hop + 1)])  59.5 us
    ppermute x9, waiting for transfers between devices, fast_body(): lam = lam + lax.ppermute(s['all'] * lam + s['lloc'], 'mp', [(hop, hop - 1)])  58.6 us
    unnamed x597, local copies, waits for them, and re-layouts  58.2 us
    ppermute x8, starting transfers between devices, to_rows(): lax.ppermute(lax.dynamic_slice_in_dim(v, (z ^ step) * own, own, 1), ('seq...  57.5 us
  transfers between devices with their start and end apart: 89, of which 30 were waited for; matrix products, arithmetic and copies ran while one was open for 35% of the time, Pallas kernels for 15%

profile of v1, /device:TPU:9, one launch (start us, length us, event | category | flops | bytes accessed | tf_op | source)
XLA Modules:
  0.0 1618.2 jit_solution(13622774547670375445)
XLA Ops:
  141.0 19.8 %collective-permute-done.3 = bf16[3,256,512]{2,1,0:T(8,128)(2,1)S(1)} collective-permute-done((bf16[3,256,512]{2,1,0:T(8,128)(2,1)}, bf16[3,256,512]{2,1,0:T(8,128)(2,1)S(1)}, u32[]{:S(2)}, u32[]{:S(2)}) %collective-permute-start.3) | collective-permute-done | bytes 786464 | tf_op jit(solution)/shard_map/ppermute | solution.py:732
  162.7 51.7 %collective-permute-done.40 = bf16[3,256,512]{2,1,0:T(8,128)(2,1)S(1)} collective-permute-done((bf16[3,256,512]{2,1,0:T(8,128)(2,1)}, bf16[3,256,512]{2,1,0:T(8,128)(2,1)S(1)}, u32[]{:S(2)}, u32[]{:S(2)}) %collective-permute-start.40) | collective-permute-done | bytes 786464 | tf_op jit(solution)/shard_map/ppermute | solution.py:732
  217.6 20.1 %collective-permute-done.41 = bf16[3,256,512]{2,1,0:T(8,128)(2,1)S(1)} collective-permute-done((bf16[3,256,512]{2,1,0:T(8,128)(2,1)}, bf16[3,256,512]{2,1,0:T(8,128)(2,1)S(1)}, u32[]{:S(2)}, u32[]{:S(2)}) %collective-permute-start.41) | collective-permute-done | bytes 786464 | tf_op jit(solution)/shard_map/ppermute | solution.py:732
  237.9 37.0 %collective-permute-done.42 = bf16[3,256,512]{2,1,0:T(8,128)(2,1)S(1)} collective-permute-done((bf16[3,256,512]{2,1,0:T(8,128)(2,1)S(1)}, bf16[3,256,512]{2,1,0:T(8,128)(2,1)S(1)}, u32[]{:S(2)}, u32[]{:S(2)}) %collective-permute-start.42) | collective-permute-done | bytes 786464 | tf_op jit(solution)/shard_map/ppermute | solution.py:732
  525.5 19.5 %copy.742 = bf16[4,4,512,2,512]{4,1,2,0,3:T(4,128)(2,1)S(1)} copy(bf16[4,4,512,2,512]{4,2,3,1,0:T(8,128)(2,1)} %bitcast.728) | data formatting | bytes 33554432 | tf_op jit(solution)/shard_map/reshape | solution.py:685
  622.1 18.1 %ssd_local.5 = (f32[1,512,2048]{2,1,0:T(8,128)}, f32[1,128,2048]{2,1,0:T(8,128)}, f32[1,512,256]{2,1,0:T(8,128)}) custom-call(bf16[1,512,2048]{2,1,0:T(8,128)(2,1)} %copy-done.255, bf16[1,16,2048]{2,1,0:T(8,128)(2,1)} %slice.624.halo_ref, f32[4,2048]{1,0:T(4,128)} %bitcast.843, bf16[1,512,256]{2,1,0:T(8,128)(2,1)} %fusion.50.bcin_ref.in_ref, ...), custom_call_target="tpu_custom_call" | custom-call | flops 3221225472 | bytes 8388608 | tf_op jit(solution)/shard_map/ssd_local/pallas_call | solution.py:607
  644.1 18.3 %ssd_local.4 = (f32[1,512,2048]{2,1,0:T(8,128)}, f32[1,128,2048]{2,1,0:T(8,128)}, f32[1,512,256]{2,1,0:T(8,128)}) custom-call(bf16[1,512,2048]{2,1,0:T(8,128)(2,1)} %copy-done.256, bf16[1,16,2048]{2,1,0:T(8,128)(2,1)} %slice.616.halo_ref, f32[4,2048]{1,0:T(4,128)} %bitcast.844, bf16[1,512,256]{2,1,0:T(8,128)(2,1)} %fusion.49.bcin_ref.in_ref, ...), custom_call_target="tpu_custom_call" | custom-call | flops 3221225472 | bytes 8388608 | tf_op jit(solution)/shard_map/ssd_local/pallas_call | solution.py:607
  667.2 18.1 %ssd_local.3 = (f32[1,512,2048]{2,1,0:T(8,128)}, f32[1,128,2048]{2,1,0:T(8,128)}, f32[1,512,256]{2,1,0:T(8,128)}) custom-call(bf16[1,512,2048]{2,1,0:T(8,128)(2,1)} %copy-done.257, bf16[1,16,2048]{2,1,0:T(8,128)(2,1)} %slice.599.halo_ref, f32[4,2048]{1,0:T(4,128)} %bitcast.845, bf16[1,512,256]{2,1,0:T(8,128)(2,1)} %fusion.48.bcin_ref.in_ref, ...), custom_call_target="tpu_custom_call" | custom-call | flops 3221225472 | bytes 8388608 | tf_op jit(solution)/shard_map/ssd_local/pallas_call | solution.py:607
  692.6 21.3 %collective-permute-done.8 = f32[1,128,2048]{2,1,0:T(8,128)S(1)} collective-permute-done((f32[1,128,2048]{2,1,0:T(8,128)S(1)}, f32[1,128,2048]{2,1,0:T(8,128)S(1)}, u32[]{:S(2)}, u32[]{:S(2)}) %collective-permute-start.8) | collective-permute-done | bytes 1048608 | tf_op jit(solution)/shard_map/ppermute | solution.py:850
  716.6 18.0 %collective-permute-done.21 = f32[1,128,2048]{2,1,0:T(8,128)S(1)} collective-permute-done((f32[1,128,2048]{2,1,0:T(8,128)S(1)}, f32[1,128,2048]{2,1,0:T(8,128)S(1)}, u32[]{:S(2)}, u32[]{:S(2)}) %collective-permute-start.21) | collective-permute-done | bytes 1048608 | tf_op jit(solution)/shard_map/ppermute | solution.py:850
  738.1 19.0 %collective-permute-done.9 = f32[1,128,2048]{2,1,0:T(8,128)S(1)} collective-permute-done((f32[1,128,2048]{2,1,0:T(8,128)S(1)}, f32[1,128,2048]{2,1,0:T(8,128)S(1)}, u32[]{:S(2)}, u32[]{:S(2)}) %collective-permute-start.9) | collective-permute-done | bytes 1048608 | tf_op jit(solution)/shard_map/ppermute | solution.py:850
  810.7 15.1 fusion.2
  921.3 14.5 gate_back.4
  953.1 14.5 gate_back.5
  989.3 21.6 %collective-permute-done.47 = f32[1,128,2048]{2,1,0:T(8,128)S(1)} collective-permute-done((f32[1,128,2048]{2,1,0:T(8,128)S(1)}, f32[1,128,2048]{2,1,0:T(8,128)S(1)}, u32[]{:S(2)}, u32[]{:S(2)}) %collective-permute-start.47) | collective-permute-done | bytes 1048608 | tf_op jit(solution)/shard_map/ppermute | solution.py:886
  1013.7 19.6 %collective-permute-done.59 = f32[1,128,2048]{2,1,0:T(8,128)S(1)} collective-permute-done((f32[1,128,2048]{2,1,0:T(8,128)S(1)}, f32[1,128,2048]{2,1,0:T(8,128)S(1)}, u32[]{:S(2)}, u32[]{:S(2)}) %collective-permute-start.59) | collective-permute-done | bytes 1048608 | tf_op jit(solution)/shard_map/ppermute | solution.py:886
  1038.5 17.3 %collective-permute-done.71 = f32[1,128,2048]{2,1,0:T(8,128)S(1)} collective-permute-done((f32[1,128,2048]{2,1,0:T(8,128)S(1)}, f32[1,128,2048]{2,1,0:T(8,128)S(1)}, u32[]{:S(2)}, u32[]{:S(2)}) %collective-permute-start.71) | collective-permute-done | bytes 1048608 | tf_op jit(solution)/shard_map/ppermute | solution.py:886
  1060.7 36.3 %ssd_back.3 = (bf16[1,512,2048]{2,1,0:T(8,128)(2,1)}, f32[1,8,2048]{2,1,0:T(8,128)}, f32[1,8,2048]{2,1,0:T(8,128)}, f32[1,512,256]{2,1,0:T(8,128)}, f32[1,512,128]{2,1,0:T(8,128)}, /*index=5*/f32[1,512,128]{2,1,0:T(8,128)}) custom-call(f32[1,512,2048]{2,1,0:T(8,128)} %get-tuple-element.148.dy_ref, bf16[1,512,2048]{2,1,0:T(8,128)(2,1)} %copy-done.257, ...), custom_call_target="tpu_custom_call" | custom-call | flops 6442450944 | bytes 12582912 | tf_op jit(solution)/shard_map/ssd_back/pallas_call | solution.py:607
  1100.7 36.4 %ssd_back.4 = (bf16[1,512,2048]{2,1,0:T(8,128)(2,1)}, f32[1,8,2048]{2,1,0:T(8,128)}, f32[1,8,2048]{2,1,0:T(8,128)}, f32[1,512,256]{2,1,0:T(8,128)}, f32[1,512,128]{2,1,0:T(8,128)}, /*index=5*/f32[1,512,128]{2,1,0:T(8,128)}) custom-call(f32[1,512,2048]{2,1,0:T(8,128)} %get-tuple-element.161.dy_ref, bf16[1,512,2048]{2,1,0:T(8,128)(2,1)} %copy-done.256, ...), custom_call_target="tpu_custom_call" | custom-call | flops 6442450944 | bytes 12582912 | tf_op jit(solution)/shard_map/ssd_back/pallas_call | solution.py:607
  1139.9 36.7 %ssd_back.5 = (bf16[1,512,2048]{2,1,0:T(8,128)(2,1)}, f32[1,8,2048]{2,1,0:T(8,128)}, f32[1,8,2048]{2,1,0:T(8,128)}, f32[1,512,256]{2,1,0:T(8,128)}, f32[1,512,128]{2,1,0:T(8,128)}, /*index=5*/f32[1,512,128]{2,1,0:T(8,128)}) custom-call(f32[1,512,2048]{2,1,0:T(8,128)} %get-tuple-element.174.dy_ref, bf16[1,512,2048]{2,1,0:T(8,128)(2,1)} %copy-done.255, ...), custom_call_target="tpu_custom_call" | custom-call | flops 6442450944 | bytes 12582912 | tf_op jit(solution)/shard_map/ssd_back/pallas_call | solution.py:607
  1308.2 44.2 %all-reduce.10.cloned.1.call-done = f32[4,8,2,16,64]{4,1,0,3,2:T(8,128)} async-done(((f32[4,8,2,16,64]{4,1,0,3,2:T(8,128)}), f32[4,8,2,16,64]{4,1,0,3,2:T(8,128)}) %all-reduce.10.cloned.1.call-update) | async-done | bytes 262160
  1394.3 26.9 %collective-permute-done.14 = bf16[1,256,512]{2,1,0:T(8,128)(2,1)} collective-permute-done((bf16[1,256,512]{2,1,0:T(8,128)(2,1)}, bf16[1,256,512]{2,1,0:T(8,128)(2,1)}, u32[]{:S(2)}, u32[]{:S(2)}) %collective-permute-start.14) | collective-permute-done | bytes 262176 | tf_op jit(solution)/shard_map/ppermute | solution.py:744
  1525.3 31.8 %collective-permute-done.65 = f32[1,256,512]{2,1,0:T(8,128)S(1)} collective-permute-done((f32[1,256,512]{2,1,0:T(8,128)S(1)}, f32[1,256,512]{2,1,0:T(8,128)S(1)}, u32[]{:S(2)}, u32[]{:S(2)}) %collective-permute-start.65) | collective-permute-done | bytes 524320 | tf_op jit(solution)/shard_map/ppermute | solution.py:744
  1560.6 30.1 %collective-permute-done.76 = f32[1,256,512]{2,1,0:T(8,128)S(1)} collective-permute-done((f32[1,256,512]{2,1,0:T(8,128)S(1)}, f32[1,256,512]{2,1,0:T(8,128)S(1)}, u32[]{:S(2)}, u32[]{:S(2)}) %collective-permute-start.76) | collective-permute-done | bytes 524320 | tf_op jit(solution)/shard_map/ppermute | solution.py:744
  (1245 shorter events, 985.2 us)
Async XLA Ops:
  16.0 278.0 %all-gather.7.cloned.1.call-start = ((), (), s32[]{:S(2)}) async-start(), calls=%async_computation.4 | async-start | bytes 4038656 | tf_op jit(solution)/shard_map/all_gather | solution.py:684
  18.0 453.1 %all-gather.9.cloned.1.call-start = ((), (), s32[]{:S(2)}) async-start(), calls=%async_computation.5 | async-start | bytes 8912896 | tf_op jit(solution)/shard_map/all_gather | solution.py:686
  20.7 504.8 %all-gather.5.cloned.1.call-start = ((), (), s32[]{:S(2)}) async-start(), calls=%async_computation.3 | async-start | bytes 17825792 | tf_op jit(solution)/shard_map/all_gather | solution.py:685
  29.0 1274.0 %reduce-scatter.5.cloned.1.call-start = ((), (), s32[]{:S(2)}) async-start(), calls=%async_computation.6 | async-start | bytes 1769472 | tf_op jit(solution)/shard_map/reduce_scatter | solution.py:988
  49.8 83.0 %collective-permute-start.2 = (bf16[3,256,512]{2,1,0:T(8,128)(2,1)}, bf16[3,256,512]{2,1,0:T(8,128)(2,1)S(1)}, u32[]{:S(2)}, u32[]{:S(2)}) collective-permute-start(bf16[3,256,512]{2,1,0:T(8,128)(2,1)} %get-tuple-element.298), channel_id=1, source_target_pairs={{0,1},{1,5},{2,0},{3,4},{4,3},{5,7},{6,2},{7,6},{8,9},{9,13},{10,8... | collective-permute-start | bytes 2359304 | tf_op jit(solution)/shard_map/ppermute | solution.py:732
  55.5 105.3 %collective-permute-start.3 = (bf16[3,256,512]{2,1,0:T(8,128)(2,1)}, bf16[3,256,512]{2,1,0:T(8,128)(2,1)S(1)}, u32[]{:S(2)}, u32[]{:S(2)}) collective-permute-start(bf16[3,256,512]{2,1,0:T(8,128)(2,1)} %get-tuple-element.295), channel_id=1, source_target_pairs={{0,5},{1,1},{2,4},{3,0},{4,7},{5,3},{6,6},{7,2},{8,13},{9,9},{10,1... | collective-permute-start | bytes 2359304 | tf_op jit(solution)/shard_map/ppermute | solution.py:732
  64.4 150.0 %collective-permute-start.40 = (bf16[3,256,512]{2,1,0:T(8,128)(2,1)}, bf16[3,256,512]{2,1,0:T(8,128)(2,1)S(1)}, u32[]{:S(2)}, u32[]{:S(2)}) collective-permute-start(bf16[3,256,512]{2,1,0:T(8,128)(2,1)} %get-tuple-element.293), channel_id=1, source_target_pairs={{0,0},{1,4},{2,1},{3,5},{4,2},{5,6},{6,3},{7,7},{8,8},{9,12},{10,9... | collective-permute-start | bytes 2359304 | tf_op jit(solution)/shard_map/ppermute | solution.py:732
  94.4 143.4 %collective-permute-start.41 = (bf16[3,256,512]{2,1,0:T(8,128)(2,1)}, bf16[3,256,512]{2,1,0:T(8,128)(2,1)S(1)}, u32[]{:S(2)}, u32[]{:S(2)}) collective-permute-start(bf16[3,256,512]{2,1,0:T(8,128)(2,1)} %get-tuple-element.292), channel_id=1, source_target_pairs={{0,4},{1,0},{2,5},{3,1},{4,6},{5,2},{6,7},{7,3},{8,12},{9,8},{10,1... | collective-permute-start | bytes 2359304 | tf_op jit(solution)/shard_map/ppermute | solution.py:732
  114.9 159.9 %collective-permute-start.42 = (bf16[3,256,512]{2,1,0:T(8,128)(2,1)S(1)}, bf16[3,256,512]{2,1,0:T(8,128)(2,1)S(1)}, u32[]{:S(2)}, u32[]{:S(2)}) collective-permute-start(bf16[3,256,512]{2,1,0:T(8,128)(2,1)S(1)} %copy-done.92), channel_id=1, source_target_pairs={{0,1},{1,5},{2,0},{3,4},{4,3},{5,7},{6,2},{7,6},{8,9},{9,13},{10,8... | collective-permute-start | bytes 2359304 | tf_op jit(solution)/shard_map/ppermute | solution.py:732
  132.8 151.8 %collective-permute-start.43 = (bf16[3,256,512]{2,1,0:T(8,128)(2,1)S(1)}, bf16[3,256,512]{2,1,0:T(8,128)(2,1)S(1)}, u32[]{:S(2)}, u32[]{:S(2)}) collective-permute-start(bf16[3,256,512]{2,1,0:T(8,128)(2,1)S(1)} %copy-done.91), channel_id=1, source_target_pairs={{0,5},{1,1},{2,4},{3,0},{4,7},{5,3},{6,6},{7,2},{8,13},{9,9},{10,1... | collective-permute-start | bytes 2359304 | tf_op jit(solution)/shard_map/ppermute | solution.py:732
  162.6 125.4 %collective-permute-start.29 = (bf16[256,2048]{1,0:T(8,128)(2,1)S(1)}, bf16[256,2048]{1,0:T(8,128)(2,1)S(1)}, u32[]{:S(2)}, u32[]{:S(2)}) collective-permute-start(bf16[256,2048]{1,0:T(8,128)(2,1)S(1)} %get-tuple-element.283), channel_id=1, source_target_pairs={{0,4},{4,0},{1,5},{5,1},{2,6},{6,2},{3,7},{7,3},{8,12},{12,8},{9,1... | collective-permute-start | bytes 3145736 | tf_op jit(solution)/shard_map/ppermute | solution.py:653
  287.5 89.0 %collective-permute-start.68 = (bf16[256,2048]{1,0:T(8,128)(2,1)}, bf16[256,2048]{1,0:T(8,128)(2,1)}, u32[]{:S(2)}, u32[]{:S(2)}) collective-permute-start(bf16[256,2048]{1,0:T(8,128)(2,1)} %get-tuple-element.288), channel_id=1, source_target_pairs={{0,4},{4,0},{1,5},{5,1},{2,6},{6,2},{3,7},{7,3},{8,12},{12,8},{9,1... | collective-permute-start | bytes 3145736 | tf_op jit(solution)/shard_map/ppermute | solution.py:653
  287.5 171.3 %collective-permute-start.56 = (bf16[256,2048]{1,0:T(8,128)(2,1)}, bf16[256,2048]{1,0:T(8,128)(2,1)}, u32[]{:S(2)}, u32[]{:S(2)}) collective-permute-start(bf16[256,2048]{1,0:T(8,128)(2,1)} %get-tuple-element.289), channel_id=1, source_target_pairs={{0,4},{4,0},{1,5},{5,1},{2,6},{6,2},{3,7},{7,3},{8,12},{12,8},{9,1... | collective-permute-start | bytes 3145736 | tf_op jit(solution)/shard_map/ppermute | solution.py:653
  288.0 176.5 %collective-permute-start.44 = (bf16[256,2048]{1,0:T(8,128)(2,1)}, bf16[256,2048]{1,0:T(8,128)(2,1)}, u32[]{:S(2)}, u32[]{:S(2)}) collective-permute-start(bf16[256,2048]{1,0:T(8,128)(2,1)} %get-tuple-element.290), channel_id=1, source_target_pairs={{0,4},{4,0},{1,5},{5,1},{2,6},{6,2},{3,7},{7,3},{8,12},{12,8},{9,1... | collective-permute-start | bytes 3145736 | tf_op jit(solution)/shard_map/ppermute | solution.py:653
  854.2 95.8 %collective-permute-start.69 = (f32[1,512]{1,0:T(1,128)S(1)}, f32[1,512]{1,0:T(1,128)}, u32[]{:S(2)}, u32[]{:S(2)}) collective-permute-start(f32[1,512]{1,0:T(1,128)S(1)} %bitcast.859), channel_id=1, source_target_pairs={{0,4},{4,0},{1,5},{5,1},{2,6},{6,2},{3,7},{7,3},{8,12},{12,8},{9,1... | collective-permute-start | bytes 6152 | tf_op jit(solution)/shard_map/ppermute | solution.py:653
  864.6 498.0 %collective-permute-start.35 = (f32[256,2048]{1,0:T(8,128)}, f32[256,2048]{1,0:T(8,128)}, u32[]{:S(2)}, u32[]{:S(2)}) collective-permute-start(f32[256,2048]{1,0:T(8,128)} %constant_dynamic-slice_fusion.5), channel_id=1, source_target_pairs={{0,4},{4,0},{1,5},{5,1},{2,6},{6,2},{3,7},{7,3},{8,12},{12,8},{9,1... | collective-permute-start | bytes 6291464 | tf_op jit(solution)/shard_map/ppermute | solution.py:653
  869.8 505.4 %collective-permute-start.13 = (f32[256,2048]{1,0:T(8,128)}, f32[256,2048]{1,0:T(8,128)}, u32[]{:S(2)}, u32[]{:S(2)}) collective-permute-start(f32[256,2048]{1,0:T(8,128)} %constant_dynamic-slice_fusion.7), channel_id=1, source_target_pairs={{0,4},{4,0},{1,5},{5,1},{2,6},{6,2},{3,7},{7,3},{8,12},{12,8},{9,1... | collective-permute-start | bytes 6291464 | tf_op jit(solution)/shard_map/ppermute | solution.py:653
  1097.0 86.2 %collective-permute-start.49 = (f32[1,512,256]{2,1,0:T(8,128)}, f32[1,512,256]{2,1,0:T(8,128)S(1)}, u32[]{:S(2)}, u32[]{:S(2)}) collective-permute-start(f32[1,512,256]{2,1,0:T(8,128)} %get-tuple-element.153), channel_id=1, source_target_pairs={{0,4},{4,0},{1,5},{5,1},{2,6},{6,2},{3,7},{7,3},{8,12},{12,8},{9,1... | collective-permute-start | bytes 1572872 | tf_op jit(solution)/shard_map/ppermute | solution.py:653
  1263.7 88.7 %all-reduce.10.cloned.1.call-start = ((), (), s32[]{:S(2)}) async-start(), calls=%async_computation.10 | async-start | bytes 1048576
  1305.2 86.0 %reduce-scatter.7.cloned.1.call-start = ((), (), s32[]{:S(2)}) async-start(), calls=%async_computation.7 | async-start | bytes 1474560 | tf_op jit(solution)/shard_map/reduce_scatter | solution.py:976
  1307.9 294.3 %reduce-scatter.9.cloned.1.call-start = ((), (), s32[]{:S(2)}) async-start(), calls=%async_computation.8 | async-start | bytes 983040 | tf_op jit(solution)/shard_map/reduce_scatter | solution.py:978
  1369.7 137.9 %collective-permute-start.52 = (f32[1,256,512]{2,1,0:T(8,128)}, f32[1,256,512]{2,1,0:T(8,128)}, u32[]{:S(2)}, u32[]{:S(2)}) collective-permute-start(f32[1,256,512]{2,1,0:T(8,128)} %get-tuple-element.302), channel_id=1, source_target_pairs={{0,0},{4,1},{1,2},{5,3},{2,4},{6,5},{3,6},{7,7},{8,8},{12,9},{9,10... | collective-permute-start | bytes 1572872 | tf_op jit(solution)/shard_map/ppermute | solution.py:744
  1374.8 134.3 %collective-permute-start.53 = (f32[1,256,512]{2,1,0:T(8,128)}, f32[1,256,512]{2,1,0:T(8,128)}, u32[]{:S(2)}, u32[]{:S(2)}) collective-permute-start(f32[1,256,512]{2,1,0:T(8,128)} %get-tuple-element.301), channel_id=1, source_target_pairs={{4,0},{0,1},{5,2},{1,3},{6,4},{2,5},{7,6},{3,7},{12,8},{8,9},{13,1... | collective-permute-start | bytes 1572872 | tf_op jit(solution)/shard_map/ppermute | solution.py:744
  1374.8 135.7 %collective-permute-start.54 = (f32[1,256,512]{2,1,0:T(8,128)}, f32[1,256,512]{2,1,0:T(8,128)}, u32[]{:S(2)}, u32[]{:S(2)}) collective-permute-start(f32[1,256,512]{2,1,0:T(8,128)} %get-tuple-element.300), channel_id=1, source_target_pairs={{1,0},{5,1},{0,2},{4,3},{3,4},{7,5},{2,6},{6,7},{9,8},{13,9},{8,10... | collective-permute-start | bytes 1572872 | tf_op jit(solution)/shard_map/ppermute | solution.py:744
  (351 other events, 7236.7 us)
Sparse Core Ops, SparseCore 0:
  16.1 43.7 all-reduce.7
  1263.8 39.1 reduce-scatter.4
  1306.3 46.0 all-reduce.9
  1354.7 30.2 reduce-scatter.6
  1394.4 24.7 reduce-scatter.8
Sparse Core Ops, SparseCore 1:
  19.2 100.8 all-gather.6
  123.1 153.7 all-gather.8
  279.9 191.2 all-gather.4

commit v2 on v0

--- a/solution.py
+++ b/solution.py
@@ -1,6 +1,10 @@
+import functools
+
 import jax
 import jax.numpy as jnp
 from jax import lax
+from jax.experimental import pallas as pl
+from jax.experimental.pallas import tpu as pltpu
 from jax.sharding import PartitionSpec as P
 
 D = 2048
@@ -11,10 +15,13 @@
 R = 16
 ADAPT = 8
 DI = 4096
+HG = 4
+HALO = 16
 
 
 eps = 1e-05
 precise = lax.Precision.HIGHEST
+VMEM_LIMIT = 56 * 1024 * 1024
 
 
 def shifted(array, axis, by):
@@ -325,6 +332,1226 @@
     return (jnp.stack(outputs), jnp.stack(x_grads), running[0], running[1], running[2], running[3])
 
 
+MESH = pl.DeviceIdType.MESH
+
+
+def flip(v, mask, count):
+    total = 0
+    bit = 1
+    while bit < count:
+        b = lax.rem(v // bit, 2)
+        total = total + (1 - b if mask & bit else b) * bit
+        bit *= 2
+    return total
+
+
+def gather_kernel(
+    nd, nz, wt_ref, x_ref, w_ref, rows_ref, local_sem, pair_sem, up_sem, down_sem, zrecv_sem, xsend_sem, xrecv_sem, ysend_sem,
+    yrecv_sem, hsend_sem, hrecv_sem, asend_sem, arecv_sem
+):
+    d, c, z = lax.axis_index("dp"), lax.axis_index("seq"), lax.axis_index("mp")
+    xn, yn = flip(d, 1, nd), flip(d, 2, nd)
+    rows, part = wt_ref.shape[1], wt_ref.shape[2] // 2
+    own, feats = x_ref.shape[1] // nz, x_ref.shape[2]
+    chunk = nz // 2
+    mine = lax.rem(z, chunk) * 2 + c
+
+    def remote(src, dst, send, recv, device):
+        return pltpu.make_async_remote_copy(
+            src_ref=src, dst_ref=dst, send_sem=send, recv_sem=recv, device_id=device, device_id_type=MESH
+        )
+
+    barrier = pltpu.get_barrier_semaphore()
+    for cc in range(2):
+        for r in range(nz):
+            if cc or r:
+                pl.semaphore_signal(barrier, 1, device_id=(d, flip(c, cc, 2), flip(z, r, nz)), device_id_type=MESH)
+    for dd in (xn, yn):
+        pl.semaphore_signal(barrier, 1, device_id=(dd, c, z), device_id_type=MESH)
+    pl.semaphore_wait(barrier, 2 * nz - 1 + 2)
+
+    def cols(s):
+        return pl.ds(pl.multiple_of(s * part, 128), part)
+
+    def area(dd, s):
+        return w_ref.at[:, pl.ds(pl.multiple_of(dd * (2 * rows), 16), 2 * rows), cols(s)]
+
+    def half_area(dd, s, h):
+        return w_ref.at[:, pl.ds(pl.multiple_of(dd * (2 * rows) + h * rows, 16), rows), cols(s)]
+
+    mine_area = w_ref.at[:, pl.ds(pl.multiple_of((2 * d + c) * rows, 16), rows), cols(z)]
+    keep = pltpu.make_async_copy(wt_ref.at[:, :, cols(c)], mine_area, local_sem.at[0])
+    pair = remote(wt_ref.at[:, :, cols(1 - c)], mine_area, pair_sem.at[0], pair_sem.at[1], (d, 1 - c, z))
+    keep.start()
+    pair.start()
+
+    def piece(r):
+        q = flip(z, r, nz)
+        src = x_ref.at[:, pl.ds(pl.multiple_of(q * own, 16), own), :]
+        dst = rows_ref.at[:, :, pl.ds(pl.multiple_of(z * feats, 128), feats)]
+        to_c, to_z = lax.rem(q, 2), c * chunk + q // 2
+        here = jnp.logical_and(to_c == c, to_z == z)
+        far = remote(src, dst, asend_sem.at[r], arecv_sem.at[r], (d, to_c, to_z))
+        near = pltpu.make_async_copy(src, dst, arecv_sem.at[r])
+        return here, far, near
+
+    for r in range(nz):
+        here, far, near = piece(r)
+
+        @pl.when(here)
+        def _():
+            near.start()
+
+        @pl.when(jnp.logical_not(here))
+        def _():
+            far.start()
+
+    keep.wait()
+    pair.wait()
+
+    def spread(s):
+        remote(area(d, s), area(d, s), xsend_sem.at[s], xrecv_sem.at[s], (xn, c, z)).start()
+        remote(area(d, s), area(d, s), ysend_sem.at[s], yrecv_sem.at[s], (yn, c, z)).start()
+
+    def send_up(s):
+        @pl.when(z < nz - 1)
+        def _():
+            remote(area(d, s), area(d, s), up_sem.at[s], zrecv_sem.at[s], (d, c, z + 1)).start()
+
+    def send_down(s):
+        @pl.when(z > 0)
+        def _():
+            remote(area(d, s), area(d, s), down_sem.at[s], zrecv_sem.at[s], (d, c, z - 1)).start()
+
+    def relay(s):
+        remote(area(xn, s), area(xn, s), xsend_sem.at[s], xrecv_sem.at[s], (xn, c, z)).wait_recv()
+        remote(half_area(xn, s, 0), half_area(xn, s, 0), hsend_sem.at[0, s], hrecv_sem.at[0, s], (yn, c, z)).start()
+        remote(area(yn, s), area(yn, s), ysend_sem.at[s], yrecv_sem.at[s], (yn, c, z)).wait_recv()
+        remote(half_area(yn, s, 1), half_area(yn, s, 1), hsend_sem.at[1, s], hrecv_sem.at[1, s], (xn, c, z)).start()
+
+    send_up(z)
+    send_down(z)
+    spread(z)
+    for r in range(1, nz + 1):
+        if r < nz:
+            @pl.when(z - r >= 0)
+            def _():
+                s = z - r
+                remote(area(d, s), area(d, s), up_sem.at[s], zrecv_sem.at[s], (d, c, z)).wait_recv()
+                send_up(s)
+                spread(s)
+
+            @pl.when(z + r < nz)
+            def _():
+                s = z + r
+                remote(area(d, s), area(d, s), up_sem.at[s], zrecv_sem.at[s], (d, c, z)).wait_recv()
+                send_down(s)
+                spread(s)
+
+        if r == 1:
+            relay(z)
+        else:
+            @pl.when(z - r + 1 >= 0)
+            def _():
+                relay(z - r + 1)
+
+            @pl.when(z + r - 1 < nz)
+            def _():
+                relay(z + r - 1)
+
+    for r in range(nz):
+        here, far, near = piece(r)
+        src_z = flip(mine, r, nz)
+        dst = rows_ref.at[:, :, pl.ds(pl.multiple_of(src_z * feats, 128), feats)]
+        pltpu.make_async_copy(dst, dst, arecv_sem.at[r]).wait()
+
+        @pl.when(jnp.logical_not(here))
+        def _():
+            far.wait_send()
+
+    for s in range(nz):
+        remote(half_area(d, s, 0), half_area(d, s, 0), hsend_sem.at[0, s], hrecv_sem.at[0, s], (yn, c, z)).wait()
+        remote(half_area(d, s, 1), half_area(d, s, 1), hsend_sem.at[1, s], hrecv_sem.at[1, s], (xn, c, z)).wait()
+        remote(area(d, s), area(d, s), xsend_sem.at[s], xrecv_sem.at[s], (xn, c, z)).wait_send()
+        remote(area(d, s), area(d, s), ysend_sem.at[s], yrecv_sem.at[s], (yn, c, z)).wait_send()
+
+        @pl.when(jnp.logical_and(s <= z, z < nz - 1))
+        def _():
+            remote(area(d, s), area(d, s), up_sem.at[s], zrecv_sem.at[s], (d, c, z)).wait_send()
+
+        @pl.when(jnp.logical_and(s >= z, z > 0))
+        def _():
+            remote(area(d, s), area(d, s), down_sem.at[s], zrecv_sem.at[s], (d, c, z)).wait_send()
+
+
+def gather(wt, x, nd, nz):
+    half = wt.shape[2] // 2
+    dma = pltpu.SemaphoreType.DMA
+    anywhere = pl.BlockSpec(memory_space=pl.ANY)
+    return pl.pallas_call(
+        functools.partial(gather_kernel, nd, nz),
+        name="gather",
+        out_shape=(
+            jax.ShapeDtypeStruct((2, wt.shape[1] * 2 * nd, half * nz), wt.dtype),
+            jax.ShapeDtypeStruct((x.shape[0], x.shape[1] // nz, x.shape[2] * nz), x.dtype),
+        ),
+        in_specs=[anywhere] * 2,
+        out_specs=(anywhere,) * 2,
+        scratch_shapes=[
+            dma((1,)), dma((2,)), dma((nz,)), dma((nz,)), dma((nz,)), dma((nz,)), dma((nz,)), dma((nz,)), dma((nz,)),
+            dma((2, nz)), dma((2, nz)), dma((nz,)), dma((nz,)),
+        ],
+        compiler_params=pltpu.CompilerParams(collective_id=1, has_side_effects=True),
+    )(wt, x)
+
+
+def split(v):
+    hi = v.astype(jnp.bfloat16)
+    return hi, (v - hi.astype(jnp.float32)).astype(jnp.bfloat16)
+
+
+def mm(a, b):
+    return lax.dot_general(a, b, (((1,), (0,)), ((), ())), preferred_element_type=jnp.float32)
+
+
+def mm_t(a, b):
+    return lax.dot_general(a, b, (((1,), (1,)), ((), ())), preferred_element_type=jnp.float32)
+
+
+def mm3(a, b):
+    return mm(a[0], b[0]) + mm(a[0], b[1]) + mm(a[1], b[0])
+
+
+def mm3_t(a, b):
+    return mm_t(a[0], b[0]) + mm_t(a[0], b[1]) + mm_t(a[1], b[0])
+
+
+def ones_mm(ones, v):
+    hi, lo = split(v)
+    rest = v - hi.astype(jnp.float32) - lo.astype(jnp.float32)
+    return mm(ones, hi) + mm(ones, lo) + mm(ones, rest.astype(jnp.bfloat16))
+
+
+def conv_rows(rows, halo, taps):
+    count = rows.shape[0]
+    ext = jnp.concatenate([halo, rows], axis=0).astype(jnp.float32)
+    first = HALO - (KC - 1)
+    total = taps[0:1] * ext[first : first + count]
+    for j in range(1, KC):
+        total = total + taps[j : j + 1] * ext[first + j : first + j + count]
+    return total
+
+
+def conv_rows_back(grad, taps):
+    count, width = grad.shape
+    zero = jnp.zeros((8, width), jnp.float32)
+    ext = jnp.concatenate([zero, grad, zero], axis=0)
+    total = taps[0:1] * ext[3 : 3 + count + 8]
+    for j in range(1, KC):
+        total = total + taps[j : j + 1] * ext[3 - j : 3 - j + count + 8]
+    return total
+
+
+def widen(columns):
+    rows = columns.shape[0]
+    lane = lax.broadcasted_iota(jnp.int32, (rows, 2 * P_SIZE), 1)
+    return jnp.concatenate(
+        [jnp.where(lane < P_SIZE, columns[:, h : h + 1], columns[:, h + 1 : h + 2]) for h in range(0, HG, 2)], axis=1
+    )
+
+
+def of_group(value, group):
+    return pltpu.roll(value, lax.rem(128 - group * HG, 128), 1)
+
+
+def head_sums(prod, group):
+    rows = prod.shape[1]
+    row = lax.broadcasted_iota(jnp.int32, (rows, 128), 0) // P_SIZE + group * HG
+    lane = lax.broadcasted_iota(jnp.int32, (rows, 128), 1)
+    pick = (row == lane).astype(jnp.float32).astype(jnp.bfloat16)
+    hi, lo = split(prod)
+    return mm(hi, pick) + mm(lo, pick)
+
+
+def lane_sum(v):
+    part = v[:, :128]
+    for k in range(1, v.shape[1] // 128):
+        part = part + v[:, k * 128 : (k + 1) * 128]
+    return part
+
+
+def add_up(ref, value, group):
+    @pl.when(group == 0)
+    def _():
+        ref[0] = value
+
+    @pl.when(group > 0)
+    def _():
+        ref[0] += value
+
+
+class Mover:
+    def __init__(self, src_ref, dst_ref, send_sem, recv_sem, count, first, to_rows):
+        self.refs = src_ref, dst_ref, send_sem, recv_sem
+        self.count, self.first, self.to_rows = count, first, to_rows
+        self.d, self.c, self.z = lax.axis_index("dp"), lax.axis_index("seq"), lax.axis_index("mp")
+        self.chunk = count // 2
+        self.mine = lax.rem(self.z, self.chunk) * 2 + self.c
+
+    def keeper(self, q):
+        return lax.rem(q, 2), self.c * self.chunk + q // 2
+
+    def owner(self, p):
+        return self.z // self.chunk, p
+
+    def target(self, k):
+        at = lax.rem(self.z + k, self.count)
+        return at, *(self.keeper(at) if self.to_rows else self.owner(at))
+
+    def here(self, device):
+        return jnp.logical_and(device[0] == self.c, device[1] == self.z)
+
+    def piece(self, k, near):
+        src_ref, dst_ref, send_sem, recv_sem = self.refs
+        at, to_c, to_z = self.target(k)
+        if self.to_rows:
+            rows, feats = dst_ref.shape[0], src_ref.shape[1]
+            own = src_ref.shape[0] // self.count
+            src = src_ref.at[pl.ds(pl.multiple_of(at * own + self.first, 16), rows), :]
+            slot = self.z
+        else:
+            rows, feats = dst_ref.shape[0] // self.count, dst_ref.shape[1]
+            src = src_ref.at[self.first : self.first + rows, pl.ds(pl.multiple_of(at * feats, 128), feats)]
+            slot = self.mine
+        if near:
+            return pltpu.make_async_copy(src, self.landing(slot), recv_sem.at[slot])
+        return pltpu.make_async_remote_copy(
+            src_ref=src, dst_ref=self.landing(slot), send_sem=send_sem.at[k], recv_sem=recv_sem.at[slot],
+            device_id=(self.d, to_c, to_z), device_id_type=MESH,
+        )
+
+    def landing(self, slot):
+        dst_ref = self.refs[1]
+        if self.to_rows:
+            feats = dst_ref.shape[1] // self.count
+            return dst_ref.at[:, pl.ds(pl.multiple_of(slot * feats, 128), feats)]
+        rows = dst_ref.shape[0] // self.count
+        return dst_ref.at[pl.ds(pl.multiple_of(slot * rows, 16), rows), :]
+
+    def greet(self, barrier):
+        for q in range(self.count):
+            source = self.owner(q) if self.to_rows else self.keeper(q)
+
+            @pl.when(jnp.logical_not(self.here(source)))
+            def _():
+                pl.semaphore_signal(barrier, 1, device_id=(self.d, *source), device_id_type=MESH)
+        return self.count - jnp.where(self.z // self.chunk == self.c, 1, 0)
+
+    def start(self, k):
+        here = self.here(self.target(k)[1:])
+
+        @pl.when(here)
+        def _():
+            self.piece(k, True).start()
+
+        @pl.when(jnp.logical_not(here))
+        def _():
+            self.piece(k, False).start()
+
+    def start_at(self, step, steps):
+        for k in range(self.count):
+            @pl.when(step == k * steps * 3 // (4 * self.count))
+            def _():
+                self.start(k)
+
+    def finish(self):
+        for slot in range(self.count):
+            pltpu.make_async_copy(self.landing(slot), self.landing(slot), self.refs[3].at[slot]).wait()
+        for k in range(self.count):
+            @pl.when(jnp.logical_not(self.here(self.target(k)[1:])))
+            def _():
+                self.piece(k, False).wait_send()
+
+
+class Line:
+    def __init__(self, held_ref, sent_ref, send_sem, recv_sem, count, step):
+        self.refs = held_ref, sent_ref, send_sem, recv_sem
+        self.step = step
+        self.d, self.c, self.z = lax.axis_index("dp"), lax.axis_index("seq"), lax.axis_index("mp")
+        low, high = self.z > 0, self.z < count - 1
+        self.has_source, self.has_target = (low, high) if step > 0 else (high, low)
+
+    def greet(self, barrier):
+        @pl.when(self.has_source)
+        def _():
+            pl.semaphore_signal(barrier, 1, device_id=(self.d, self.c, self.z - self.step), device_id_type=MESH)
+        return jnp.where(self.has_target, 1, 0)
+
+    def copy(self, group):
+        held_ref, sent_ref, send_sem, recv_sem = self.refs
+        return pltpu.make_async_remote_copy(
+            src_ref=sent_ref.at[group], dst_ref=held_ref.at[group], send_sem=send_sem.at[group], recv_sem=recv_sem.at[group],
+            device_id=(self.d, self.c, self.z + self.step), device_id_type=MESH,
+        )
+
+    def receive(self, group):
+        held_ref = self.refs[0]
+
+        @pl.when(self.has_source)
+        def _():
+            self.copy(group).wait_recv()
+
+        @pl.when(jnp.logical_not(self.has_source))
+        def _():
+            held_ref[group] = jnp.zeros(held_ref.shape[1:], jnp.float32)
+
+        return held_ref[group]
+
+    def send(self, group, value):
+        self.refs[1][group] = value
+
+        @pl.when(self.has_target)
+        def _():
+            self.copy(group).start()
+
+    def finish(self):
+        @pl.when(self.has_target)
+        def _():
+            for g in range(self.refs[0].shape[0]):
+                self.copy(g).wait_send()
+
+
+def carried_by(kernel, count, first, to_rows, n_in, n_out, *refs):
+    ins, src_ref, outs, dst_ref = refs[:n_in], refs[n_in], refs[n_in + 1 : n_in + 1 + n_out], refs[n_in + 1 + n_out]
+    scratch, sems = refs[n_in + n_out + 2 : -2], refs[-2:]
+    kernel(*ins, *outs, *scratch, mover=Mover(src_ref, dst_ref, *sems, count, first, to_rows))
+
+
+def begin(step, *parties):
+    if parties:
+        @pl.when(step == 0)
+        def _():
+            barrier = pltpu.get_barrier_semaphore()
+            waits = 0
+            for party in parties:
+                waits = waits + party.greet(barrier)
+            pl.semaphore_wait(barrier, waits)
+
+
+def end(step, steps, *parties):
+    if parties:
+        @pl.when(step == steps - 1)
+        def _():
+            for party in parties:
+                party.finish()
+
+
+def parties_of(*given):
+    return [p for p in given if p is not None]
+
+
+def twice_split(v):
+    hi, lo = split(v)
+    lane = lax.broadcasted_iota(jnp.int32, v.shape, 1)
+    return jnp.where(lane < v.shape[1] // 2, hi.astype(jnp.float32), lo.astype(jnp.float32)).astype(jnp.bfloat16)
+
+
+def fold(v):
+    half = v.shape[0] // 2
+    return v[:half] + v[half:]
+
+
+def project_kernel(
+    low_ref, w_ref, tailw_ref, down_ref, up_ref, xin_ref, z_ref, bcin_ref, rate_ref, lr_ref, mover=None
+):
+    step, steps = pl.program_id(1), pl.num_programs(1)
+    parties = parties_of(mover)
+    begin(step, *parties)
+    if mover:
+        mover.start_at(step, 16)
+    low = low_ref[0]
+
+    @pl.when(step == 0)
+    def _():
+        tail = mm(low, tailw_ref[...])
+        bcin_ref[0] = tail[:, : 2 * NS].astype(jnp.bfloat16)
+        rate_ref[0] = tail[:, 2 * NS :]
+        lr_ref[0] = twice_split(mm_t(low, down_ref[...]))
+
+    value = mm(low, w_ref[0]) + mm(lr_ref[0], up_ref[...])
+
+    @pl.when(step < steps // 2)
+    def _():
+        xin_ref[0] = value.astype(jnp.bfloat16)
+
+    @pl.when(step >= steps // 2)
+    def _():
+        z_ref[0] = value
+
+    end(step, steps, *parties)
+
+
+def prep_kernel(rate_ref, bias_ref, decay_ref, mask_ref, bcin_ref, bchalo_ref, taps_ref, step_ref, cum_ref, lanes_ref, bc_ref):
+    rows = rate_ref.shape[1]
+    value = rate_ref[0] + bias_ref[...]
+    step = (jnp.maximum(value, 0.0) + jnp.log1p(jnp.exp(-jnp.abs(value)))) * mask_ref[0]
+    log = step * decay_ref[...]
+    tri = lax.broadcasted_iota(jnp.int32, (Q, Q), 0) >= lax.broadcasted_iota(jnp.int32, (Q, Q), 1)
+    tri = tri.astype(jnp.float32).astype(jnp.bfloat16)
+    step_ref[0] = step
+    cum = jnp.concatenate([ones_mm(tri, log[b * Q : (b + 1) * Q]) for b in range(rows // Q)], axis=0)
+    cum_ref[0] = cum
+    cum_t, step_t = cum.T, step.T
+    for g in range(lanes_ref.shape[1]):
+        lanes_ref[0, g, :HG] = cum_t[g * HG : (g + 1) * HG]
+        lanes_ref[0, g, HG:] = step_t[g * HG : (g + 1) * HG]
+    pre = conv_rows(bcin_ref[0], bchalo_ref[0], taps_ref[...])
+    bc_ref[0] = pre * jax.nn.sigmoid(pre)
+
+
+def forward_kernel(
+    xin_ref, halo_ref, taps_ref, bc_ref, cum_ref, step_ref, lanes_ref, skip_ref, z_ref, mixed_ref, square_ref, state_ref,
+    end_ref, scores_ref, bt_ref, held_ref, sent_ref, send_sem, recv_sem, mover=None
+):
+    group = pl.program_id(1)
+    rows = xin_ref.shape[1]
+    blocks = rows // Q
+    line = Line(held_ref, sent_ref, send_sem, recv_sem, lax.axis_size("mp"), 1)
+    parties = parties_of(line, mover)
+    begin(group, *parties)
+    if mover:
+        mover.start_at(group, 8)
+
+    @pl.when(group == 0)
+    def _():
+        for b in range(blocks):
+            part = bc_ref[0, b * Q : (b + 1) * Q]
+            b_part = split(part[:, :NS])
+            c_part = split(part[:, NS:])
+            scores_ref[b] = mm3_t(c_part, b_part)
+            hi, lo = split(part[:, :NS].T)
+            bt_ref[0, b] = hi
+            bt_ref[1, b] = lo
+
+    pre = conv_rows(xin_ref[0], halo_ref[0], taps_ref[...])
+    x = pre * jax.nn.sigmoid(pre)
+    cums, decs, updates = [], [], []
+    for b in range(blocks):
+        at = slice(b * Q, (b + 1) * Q)
+        cum = of_group(cum_ref[0, at], group)
+        step = of_group(step_ref[0, at], group)
+        total = cum[Q - 1 : Q]
+        wx = x[at] * widen(jnp.exp(total - cum) * step)
+        cums.append(cum)
+        decs.append(widen(jnp.exp(total)))
+        updates.append(mm3((bt_ref[0, b], bt_ref[1, b]), split(wx)))
+
+    states = [line.receive(group)]
+    for b in range(blocks):
+        states.append(decs[b] * states[b] + updates[b])
+    state_ref[0] = states[0]
+    end_ref[0] = states[blocks]
+    line.send(group, states[blocks])
+    lane = lax.broadcasted_iota(jnp.int32, (Q, 2 * P_SIZE), 1)
+    causal = lax.broadcasted_iota(jnp.int32, (Q, Q), 0) >= lax.broadcasted_iota(jnp.int32, (Q, Q), 1)
+    square = []
+    for b in range(blocks):
+        at = slice(b * Q, (b + 1) * Q)
+        scores = scores_ref[b]
+        xb = x[at]
+        carried = widen(jnp.exp(cums[b])) * mm3(split(bc_ref[0, at, NS:]), split(states[b]))
+        parts = []
+        for h in range(0, HG, 2):
+            pair = xb[:, h * P_SIZE : (h + 2) * P_SIZE]
+            x_hi, x_lo = split(pair)
+            both = jnp.concatenate([x_hi, x_lo], axis=1)
+            halves = []
+            for k in (h, h + 1):
+                spread = cums[b][:, k : k + 1] - lanes_ref[0, 0, k : k + 1, at]
+                decay = jnp.exp(jnp.where(causal, spread, -10000.0))
+                m_hi, m_lo = split(scores * decay * lanes_ref[0, 0, HG + k : HG + k + 1, at])
+                first = mm(m_hi, both)
+                halves.append(first[:, : 2 * P_SIZE] + first[:, 2 * P_SIZE :] + mm(m_lo, x_hi))
+            parts.append(jnp.where(lane < P_SIZE, halves[0], halves[1]))
+        mixed = jnp.concatenate(parts, axis=1) + skip_ref[0:1] * xb + carried
+        mixed_ref[0, at] = mixed
+        z = z_ref[0, at]
+        gated = mixed * (z * jax.nn.sigmoid(z))
+        square.append(lane_sum(gated * gated))
+    add_up(square_ref, jnp.concatenate(square, axis=0), group)
+
+    end(group, pl.num_programs(1), *parties)
+
+
+def chunk_decay(cum_ref, group):
+    rows = cum_ref.shape[1]
+    before = jnp.zeros((1, 128), jnp.float32)
+    parts = []
+    for b in range(rows // Q):
+        cum = of_group(cum_ref[0, b * Q : (b + 1) * Q], group)
+        parts.append(jnp.exp(cum + before))
+        before = before + cum[Q - 1 : Q]
+    return widen(jnp.concatenate(parts, axis=0))
+
+
+def gs_kernel(gb_ref, w_ref, up_ref, down_ref, mixed_ref, z_ref, gain_ref, gs_ref, dot_ref, rg_ref, mover=None):
+    step = pl.program_id(1)
+    parties = parties_of(mover)
+    begin(step, *parties)
+    if mover:
+        mover.start_at(step, 8)
+    gb = gb_ref[0]
+
+    @pl.when(step == 0)
+    def _():
+        rg_ref[0] = twice_split(mm_t(gb, up_ref[...]))
+
+    gs = mm(rg_ref[0], down_ref[...])
+    width = w_ref.shape[3]
+    for n in range(w_ref.shape[0]):
+        gs = gs + mm_t(gb[:, n * width : (n + 1) * width], w_ref[n, 0])
+    gs_ref[0] = gs
+    z = z_ref[0]
+    add_up(dot_ref, lane_sum(gs * gain_ref[...] * (mixed_ref[0] * (z * jax.nn.sigmoid(z)))), step)
+    end(step, pl.num_programs(1), *parties)
+
+
+def branch_kernel(
+    scaled_ref, w_ref, down_ref, up_ref, rg_ref, gb_ref, branch_ref, g_up_ref, g_down_ref, ro_ref, rot_ref, rgt_ref, mover=None
+):
+    step = pl.program_id(1)
+    parties = parties_of(mover)
+    begin(step, *parties)
+    if mover:
+        mover.start_at(step, 4)
+
+    @pl.when(step == 0)
+    def _():
+        ro = twice_split(mm_t(scaled_ref[0], down_ref[...]))
+        ro_ref[...] = ro
+        rot_ref[...] = ro.astype(jnp.float32).T.astype(jnp.bfloat16)
+        rgt_ref[...] = rg_ref[0].astype(jnp.float32).T.astype(jnp.bfloat16)
+
+    width = w_ref.shape[2]
+    total = mm(ro_ref[...], up_ref[...])
+    for n in range(w_ref.shape[1]):
+        total = total + mm(scaled_ref[0, :, n * width : (n + 1) * width], w_ref[0, n])
+    branch_ref[0] = total
+    g_up_ref[0] = fold(mm(rot_ref[...], gb_ref[0]))
+    cols = g_down_ref.shape[2]
+    g_down_ref[0] = fold(mm(rgt_ref[...], scaled_ref[0, :, pl.ds(pl.multiple_of(step * cols, 128), cols)]))
+    end(step, pl.num_programs(1), *parties)
+
+
+def unproject_kernel(
+    gz_ref, gx_ref, tail_ref, w_ref, tailw_ref, up_ref, down_ref, lr_ref, low_ref, g_ref, upz_ref, upx_ref, g_down_ref, ri_ref,
+    rit_ref, lrt_ref, mover=None
+):
+    step = pl.program_id(1)
+    parties = parties_of(mover)
+    begin(step, *parties)
+    if mover:
+        mover.start_at(step, 8)
+    gz, gx = gz_ref[0], gx_ref[0]
+    chan = gz.shape[1]
+
+    @pl.when(step == 0)
+    def _():
+        ri = twice_split(mm_t(gz, up_ref[:, :chan]) + mm_t(gx, up_ref[:, chan:]))
+        ri_ref[...] = ri
+        rit_ref[...] = ri.astype(jnp.float32).T.astype(jnp.bfloat16)
+        lrt_ref[...] = lr_ref[0].astype(jnp.float32).T.astype(jnp.bfloat16)
+
+    g_ref[0] = mm_t(gz, w_ref[0]) + mm_t(gx, w_ref[1]) + mm_t(tail_ref[0], tailw_ref[...]) + mm(ri_ref[...], down_ref[...])
+    cols = upz_ref.shape[2]
+    at = pl.ds(pl.multiple_of(step * cols, 128), cols)
+    upz_ref[0] = fold(mm(lrt_ref[...], gz_ref[0, :, at]))
+    upx_ref[0] = fold(mm(lrt_ref[...], gx_ref[0, :, at]))
+    g_down_ref[0] = fold(mm(rit_ref[...], low_ref[0]))
+    end(step, pl.num_programs(1), *parties)
+
+
+def gate_back_kernel(
+    gs_ref, mixed_ref, z_ref, inv_ref, coef_ref, gain_ref, bc_ref, cum_ref, dy_ref, gz_ref, scaled_ref, lam_ref, q_ref, ct_ref,
+    mover=None
+):
+    group = pl.program_id(1)
+    parties = parties_of(mover)
+    begin(group, *parties)
+    if mover:
+        mover.start_at(group, 8)
+
+    @pl.when(group == 0)
+    def _():
+        hi, lo = split(bc_ref[0, :, NS:].T)
+        ct_ref[0] = hi
+        ct_ref[1] = lo
+
+    z = z_ref[0]
+    mixed = mixed_ref[0]
+    sig = jax.nn.sigmoid(z)
+    act = z * sig
+    gated = mixed * act
+    inv = inv_ref[0]
+    gain = gain_ref[...]
+    scaled_ref[0] = (gated * inv * gain).astype(jnp.bfloat16)
+    g_gated = gs_ref[0] * gain * inv - gated * coef_ref[0]
+    dy = g_gated * act
+    dy_ref[0] = dy
+    gz_ref[0] = (g_gated * mixed * (sig * (1.0 + z * (1.0 - sig)))).astype(jnp.bfloat16)
+    lam_ref[0] = mm3((ct_ref[0], ct_ref[1]), split(dy * chunk_decay(cum_ref, group)))
+    add_up(q_ref, head_sums(dy * mixed, group), group)
+
+    end(group, pl.num_programs(1), *parties)
+
+
+def scan_back_kernel(
+    dy_ref, xin_ref, halo_ref, taps_ref, bc_ref, cum_ref, step_ref, lanes_ref, skip_ref, state_ref, lam_ref, end_ref,
+    gx_ref, head_ref, tail_ref, gbc_ref, xu_ref, dx_ref, scorest_ref, dscorest_ref, bt_ref, ct_ref, held_ref, sent_ref, send_sem,
+    recv_sem, mover=None
+):
+    group = pl.program_id(1)
+    rows = xin_ref.shape[1]
+    blocks = rows // Q
+    line = Line(held_ref, sent_ref, send_sem, recv_sem, lax.axis_size("mp"), -1)
+    parties = parties_of(line, mover)
+    begin(group, *parties)
+    if mover:
+        mover.start_at(group, 8)
+
+    @pl.when(group == 0)
+    def _():
+        for b in range(blocks):
+            part = bc_ref[0, b * Q : (b + 1) * Q]
+            scorest_ref[b] = mm3_t(split(part[:, :NS]), split(part[:, NS:]))
+            dscorest_ref[b] = jnp.zeros((Q, Q), jnp.float32)
+            hi, lo = split(part[:, :NS].T)
+            bt_ref[0, b] = hi
+            bt_ref[1, b] = lo
+            hi, lo = split(part[:, NS:].T)
+            ct_ref[0, b] = hi
+            ct_ref[1, b] = lo
+        gbc_ref[0] = jnp.zeros((rows, 2 * NS), jnp.float32)
+        xu_ref[0] = jnp.zeros((rows, 128), jnp.float32)
+        dx_ref[0] = jnp.zeros((rows, 128), jnp.float32)
+
+    pre = conv_rows(xin_ref[0], halo_ref[0], taps_ref[...])
+    sig = jax.nn.sigmoid(pre)
+    x = pre * sig
+    lane = lax.broadcasted_iota(jnp.int32, (Q, 2 * P_SIZE), 1)
+    causal = lax.broadcasted_iota(jnp.int32, (Q, Q), 0) <= lax.broadcasted_iota(jnp.int32, (Q, Q), 1)
+    cums, steps, decs, rests, wide_steps = [], [], [], [], []
+    for b in range(blocks):
+        at = slice(b * Q, (b + 1) * Q)
+        cum = of_group(cum_ref[0, at], group)
+        step = of_group(step_ref[0, at], group)
+        total = cum[Q - 1 : Q]
+        cums.append(cum)
+        steps.append(step)
+        decs.append(widen(jnp.exp(total)))
+        rests.append(widen(jnp.exp(total - cum)))
+        wide_steps.append(widen(step))
+    states = [state_ref[0]]
+    for b in range(blocks - 1):
+        wx = x[b * Q : (b + 1) * Q] * rests[b] * wide_steps[b]
+        states.append(decs[b] * states[b] + mm3((bt_ref[0, b], bt_ref[1, b]), split(wx)))
+    lam = line.receive(group)
+    whole = decs[0]
+    for dec in decs[1:]:
+        whole = whole * dec
+    line.send(group, whole * lam + lam_ref[0])
+    ends = jnp.sum(lam * end_ref[0], axis=0, keepdims=True)
+    g_parts = [None] * blocks
+    for b in reversed(range(blocks)):
+        at = slice(b * Q, (b + 1) * Q)
+        xb = x[at]
+        dy = dy_ref[0, at]
+        scores = scorest_ref[b]
+        dscores = dscorest_ref[b]
+        u_parts = []
+        for h in range(0, HG, 2):
+            pair = slice(h * P_SIZE, (h + 2) * P_SIZE)
+            x_hi, x_lo = split(xb[:, pair])
+            d_hi, d_lo = split(dy[:, pair])
+            both = jnp.concatenate([d_hi, d_lo], axis=1)
+            halves = []
+            for k in (h, h + 1):
+                mine = (lane < P_SIZE) if k == h else (lane >= P_SIZE)
+                spread = lanes_ref[0, 0, k : k + 1, at] - cums[b][:, k : k + 1]
+                decay = jnp.exp(jnp.where(causal, spread, -10000.0))
+                zero = jnp.zeros_like(x_hi)
+                xm_hi = jnp.where(mine, x_hi, zero)
+                xm_lo = jnp.where(mine, x_lo, zero)
+                dm = mm_t(xm_hi, d_hi) + mm_t(xm_hi, d_lo) + mm_t(xm_lo, d_hi)
+                dscores = dscores + dm * decay * steps[b][:, k : k + 1]
+                m_hi, m_lo = split(scores * decay)
+                first = mm(m_hi, both)
+                halves.append(first[:, : 2 * P_SIZE] + first[:, 2 * P_SIZE :] + mm(m_lo, d_hi))
+            u_parts.append(jnp.where(lane < P_SIZE, halves[0], halves[1]))
+        dscorest_ref[b] = dscores
+        lam_s = split(lam)
+        part = bc_ref[0, at]
+        step = wide_steps[b]
+        u = jnp.concatenate(u_parts, axis=1) + rests[b] * mm3(split(part[:, :NS]), lam_s)
+        ev = split(widen(jnp.exp(cums[b])) * dy)
+        gbc_ref[0, at, :NS] += mm3_t(split(rests[b] * step * xb), lam_s)
+        gbc_ref[0, at, NS:] += mm3_t(ev, split(states[b]))
+        if b > 0:
+            lam = decs[b] * lam + mm3((ct_ref[0, b], ct_ref[1, b]), ev)
+        xu_ref[0, at] += head_sums(xb * u, group)
+        direct = xb * dy * skip_ref[0:1]
+        if b == blocks - 1:
+            row = lax.broadcasted_iota(jnp.int32, (Q, HG * P_SIZE), 0)
+            direct = jnp.where(row == Q - 1, direct - ends, direct)
+        dx_ref[0, at] += head_sums(direct, group)
+        g_parts[b] = step * u + skip_ref[0:1] * dy
+    g_pre = jnp.concatenate(g_parts, axis=0) * (sig * (1.0 + pre * (1.0 - sig)))
+    g_ext = conv_rows_back(g_pre, taps_ref[...])
+    gx_ref[0] = g_ext[8:].astype(jnp.bfloat16)
+    head_ref[0] = g_ext[:8]
+    tail_ref[0] = g_ext[rows:]
+
+    @pl.when(group == pl.num_programs(1) - 1)
+    def _():
+        for b in range(blocks):
+            at = slice(b * Q, (b + 1) * Q)
+            part = bc_ref[0, at]
+            ds = dscorest_ref[b]
+            gbc_ref[0, at, :NS] += mm3(split(ds), split(part[:, NS:]))
+            gbc_ref[0, at, NS:] += mm3(split(ds.T), split(part[:, :NS]))
+
+    end(group, pl.num_programs(1), *parties)
+
+
+def bc_back_kernel(
+    g_ref, in_ref, halo_ref, taps_ref, q_ref, dx_ref, xu_ref, step_ref, rate_ref, bias_ref, decay_ref, mask_ref,
+    out_ref, head_ref, tail_ref, g_rate_ref
+):
+    rows = in_ref.shape[1]
+    pre = conv_rows(in_ref[0], halo_ref[0], taps_ref[...])
+    sig = jax.nn.sigmoid(pre)
+    g_ext = conv_rows_back(g_ref[0] * (sig * (1.0 + pre * (1.0 - sig))), taps_ref[...])
+    out_ref[0] = g_ext[8:].astype(jnp.bfloat16)
+    head_ref[0] = g_ext[:8]
+    tail_ref[0] = g_ext[rows:]
+    xu = xu_ref[0]
+    flow = q_ref[0] - dx_ref[0] - step_ref[0] * xu
+    later = lax.broadcasted_iota(jnp.int32, (rows, rows), 0) <= lax.broadcasted_iota(jnp.int32, (rows, rows), 1)
+    g_log = ones_mm(later.astype(jnp.float32).astype(jnp.bfloat16), flow)
+    sig = jax.nn.sigmoid(rate_ref[0] + bias_ref[...])
+    g_rate_ref[0] = ((xu + g_log * decay_ref[...]) * mask_ref[0] * sig).astype(jnp.bfloat16)
+
+
+class Slot:
+    pass
+
+
+def block(shape, index):
+    return pl.BlockSpec(shape, index)
+
+
+def call(kernel, name, grid, ins, outs, scratch, flops, size, comm=None, load=None):
+    params = dict(vmem_limit_bytes=VMEM_LIMIT)
+    ins, outs, scratch = list(ins), list(outs), list(scratch)
+    if load is not None:
+        rows, result, first, to_rows = load
+        count = lax.axis_size("mp")
+        kernel = functools.partial(carried_by, kernel, count, first, to_rows, len(ins), len(outs))
+        ins.append((rows, pl.BlockSpec(memory_space=pl.ANY)))
+        outs.append((result, pl.BlockSpec(memory_space=pl.ANY)))
+        scratch += [pltpu.SemaphoreType.DMA((count,)), pltpu.SemaphoreType.DMA((count,))]
+    if comm is not None:
+        params.update(collective_id=comm, has_side_effects=True)
+    return pl.pallas_call(
+        kernel,
+        name=name,
+        grid=(1, grid),
+        in_specs=[s for _, s in ins],
+        out_specs=[s for _, s in outs],
+        out_shape=[s for s, _ in outs],
+        scratch_shapes=scratch,
+        compiler_params=pltpu.CompilerParams(**params),
+        cost_estimate=pl.CostEstimate(flops=flops, bytes_accessed=size, transcendentals=0),
+    )(*[a for a, _ in ins])
+
+
+def after(value, *deps):
+    return lax.optimization_barrier((value,) + deps)[0]
+
+
+def move_kernel(count, rows_ref, moved_ref, send_sem, recv_sem):
+    mover = Mover(rows_ref, moved_ref, send_sem, recv_sem, count, 0, False)
+    barrier = pltpu.get_barrier_semaphore()
+    pl.semaphore_wait(barrier, mover.greet(barrier))
+    for k in range(count):
+        mover.start(k)
+    mover.finish()
+
+
+def move_last(rows, moved, count, comm):
+    dma = pltpu.SemaphoreType.DMA
+    anywhere = pl.BlockSpec(memory_space=pl.ANY)
+    return pl.pallas_call(
+        functools.partial(move_kernel, count),
+        name="move",
+        in_specs=[anywhere],
+        out_specs=anywhere,
+        out_shape=moved,
+        scratch_shapes=[dma((count,)), dma((count,))],
+        compiler_params=pltpu.CompilerParams(collective_id=comm, has_side_effects=True),
+    )(rows)
+
+
+def scatter_sum(v, axis):
+    count, me = v.shape[0], lax.axis_index(axis)
+    total = lax.dynamic_index_in_dim(v, me, 0, False)
+    for k in range(1, count):
+        give = lax.dynamic_index_in_dim(v, me ^ k, 0, False)
+        total = total + lax.ppermute(give, axis, [(i, i ^ k) for i in range(count)])
+    return total
+
+
+def fast_body(
+    x_in, cotangent, lengths, adapter_ids, norm_gain, w_zx, w_bc, w_dt, dt_bias, a_log, d_skip, conv_x, conv_bc,
+    gate_gain, w_out, in_down, in_up, out_down, out_up
+):
+    bf16, f32 = jnp.bfloat16, jnp.float32
+    micros, _, seg, feats = x_in.shape
+    nz, nd = lax.axis_size("mp"), lax.axis_size("dp")
+    core, z = lax.axis_index("seq"), lax.axis_index("mp")
+    own = seg // nz
+    tokens = 2 * own
+    heads = dt_bias.shape[0] * nz // 2
+    chan = heads * P_SIZE
+    part = chan // nz
+    groups = heads // HG
+    wide = HG * P_SIZE
+    blocks = tokens // Q
+    each = D // (nd * 2 * nz)
+
+    def other(v):
+        return lax.ppermute(v, "seq", [(0, 1), (1, 0)])
+
+    def pair_cat(mine, theirs, axis):
+        return jnp.where(
+            core == 0, jnp.concatenate([mine, theirs], axis), jnp.concatenate([theirs, mine], axis)
+        )
+
+    def halves(v, axis):
+        v = v.reshape(v.shape[:axis] + (2, v.shape[axis] // 2) + v.shape[axis + 1 :])
+        return (
+            lax.dynamic_index_in_dim(v, core, axis, False),
+            lax.dynamic_index_in_dim(v, 1 - core, axis, False),
+        )
+
+    line = 2 * part
+    bc_piece = lax.dynamic_slice_in_dim(w_bc, z * (w_bc.shape[0] // nz), w_bc.shape[0] // nz, 0)
+    same = [bc_piece, jnp.transpose(in_down, (0, 2, 1)), out_up]
+    sized = [halves(in_up, 2), halves(out_down.T, 1), halves(w_dt.T, 0)]
+    packs = []
+    for k in range(2):
+        packs.append(jnp.concatenate([v.reshape(-1, line) for v in [s[k] for s in sized] + same], 0))
+    bounds = [0]
+    for v in [s[0] for s in sized] + same:
+        bounds.append(bounds[-1] + v.size // line)
+    pack = pair_cat(packs[0][None], other(packs[1])[None], 0)
+    params = jnp.concatenate([dt_bias, a_log, d_skip, gate_gain, conv_x.reshape(-1)])
+    params = lax.all_gather(params, "mp")
+    pack = lax.all_gather(pack, ("dp", "mp")).reshape((nd, nz) + pack.shape)
+    zx_weight, x_rows = gather(jnp.transpose(w_zx, (1, 0, 2)), x_in[:, 0], nd, nz)
+    out_mine, out_theirs = halves(after(w_out, x_rows), 0)
+    out_pair = pair_cat(out_mine, other(out_theirs), 1)
+    out_all = lax.all_gather(out_pair, ("dp", "mp")).reshape((nd, nz) + out_pair.shape)
+    dt_rows = pack[:, :, :, bounds[2] : bounds[3]].reshape(nd, nz, 2, heads // nz, -1)
+    dt_weight = jnp.transpose(dt_rows, (1, 3, 0, 2, 4)).reshape(heads, D)
+    dt_weight = jnp.pad(dt_weight, ((0, 128 - heads), (0, 0)))
+    bc_rows = pack[:, :, :, bounds[3] : bounds[4]].reshape(nd, nz, 2, -1, 2 * NS)
+    bc_weight = jnp.transpose(bc_rows, (0, 2, 1, 3, 4)).reshape(D, 2 * NS)
+    bc_half = lax.dynamic_slice_in_dim(bc_weight, core * NS, NS, 1)
+    dt_weight = dt_weight.T
+    tail_weight = jnp.concatenate([bc_half, dt_weight], 1)
+    first_weight = jnp.concatenate([bc_weight, dt_weight], 1)
+
+    hl = dt_bias.shape[0]
+
+    def own_part(v):
+        v = v.reshape(v.shape[0], 2, v.shape[1] // 2)
+        return lax.dynamic_index_in_dim(v, core, 1, False).reshape(-1)
+
+    bias = jnp.pad(own_part(params[:, :hl]), (0, 128 - heads))[None]
+    rate = jnp.pad(-jnp.exp(own_part(params[:, hl : 2 * hl])), (0, 128 - heads))[None]
+    skip = jnp.repeat(own_part(params[:, 2 * hl : 3 * hl]), P_SIZE)[None]
+    width = gate_gain.shape[0]
+    gain = own_part(params[:, 3 * hl : 3 * hl + width])[None]
+    taps = params[:, 3 * hl + width :].reshape(nz, KC, 2, part)
+    taps = jnp.transpose(lax.dynamic_index_in_dim(taps, core, 2, False), (1, 0, 2)).reshape(KC, chan)
+
+    chunk = nz // 2
+    mine = (z % chunk) * 2 + core
+
+    start = z * tokens
+    own_pos = start + core * own + jnp.arange(own)
+    all_pos = start + jnp.arange(tokens)
+    forward_edge = [(i, i + 1) for i in range(nz - 1)]
+    backward_edge = [(i + 1, i) for i in range(nz - 1)]
+
+    m3 = lambda m, g: (0, 0, g)
+    m0 = lambda m, g: (0, 0, 0)
+    z2 = lambda m, g: (0, 0)
+    chan_block = block((1, tokens, wide), m3)
+    halo_block = block((1, HALO, wide), m3)
+    taps_block = block((KC, wide), lambda m, g: (0, g))
+    line_block = block((1, wide), lambda m, g: (0, g))
+    state_block = block((1, NS, wide), m3)
+    bc_block = block((1, tokens, 2 * NS), m0)
+    bc_halo = block((1, HALO, 2 * NS), m0)
+    bc_taps = block((KC, 2 * NS), z2)
+    bc_edge = block((1, 8, 2 * NS), m0)
+    one_col = block((1, tokens, 1), m0)
+    sums = block((1, tokens, 128), m0)
+    lanes_block = block((1, 1, 2 * HG, tokens), lambda m, g: (0, g, 0, 0))
+    head_line = block((1, 128), z2)
+    edge_block = block((1, 8, wide), m3)
+    shape = jax.ShapeDtypeStruct
+    tok_f32 = shape((1, tokens, chan), f32)
+    tok_b16 = shape((1, tokens, chan), bf16)
+    state_f32 = shape((1, NS, chan), f32)
+    bc_f32 = shape((1, tokens, 2 * NS), f32)
+    sums_f32 = shape((1, tokens, 128), f32)
+    edge_f32 = shape((1, 8, chan), f32)
+    act_bytes = tokens * chan * 4
+
+    dma = pltpu.SemaphoreType.DMA
+    line_scratch = [pltpu.VMEM((groups, NS, wide), f32)] * 2 + [dma((groups,))] * 2
+    anywhere = pl.BlockSpec(memory_space=pl.ANY)
+    moved_b16 = shape((seg, feats), bf16)
+    halfway = own // 2
+    moved_half = shape((seg // 2, feats), bf16)
+    rows_half = shape((halfway, D), bf16)
+
+    slots = [Slot() for _ in range(micros)]
+    for m, s in enumerate(slots):
+        x = x_rows[m].astype(f32)
+        s.inv = lax.rsqrt(jnp.mean(x * x, axis=-1, keepdims=True) + eps)
+        low_own = (x * s.inv * norm_gain).astype(bf16)
+        s.low = pair_cat(low_own, other(low_own), 0)
+        s.mask_own = (own_pos < lengths[m, 0]).astype(f32)[:, None]
+        s.mask = (all_pos < lengths[m, 0]).astype(f32)[:, None]
+        k = adapter_ids[m, 0]
+        s.pick = (k == jnp.arange(ADAPT)).astype(f32)
+        near = lax.dynamic_index_in_dim(lax.dynamic_index_in_dim(pack, k // 2, 0, False), k % 2, 1, False)
+        up = near[:, bounds[0] : bounds[1]].reshape(nz, R, 2, part)
+        s.u_in = jnp.transpose(up, (1, 2, 0, 3)).reshape(R, 2 * chan)
+        down = near[:, bounds[1] : bounds[2]].reshape(nz, R, part)
+        s.a_out = jnp.transpose(down, (1, 0, 2)).reshape(R, chan)
+        wide_rows = []
+        for first in (bounds[4], bounds[5]):
+            got = lax.dynamic_index_in_dim(pack, first + k, 3, False).reshape(nd, nz, 2, R, each)
+            wide_rows.append(jnp.transpose(got, (3, 0, 2, 1, 4)).reshape(R, D))
+        s.a_in, s.u_out = wide_rows
+        factors = [s.a_in, s.u_out, s.u_in, s.a_out]
+        s.a_in, s.u_out, s.u_in, s.a_out = [jnp.concatenate([v, v], 0) for v in factors]
+
+    full_low = block((1, tokens, D), m0)
+    rank_block = block((1, tokens, 2 * R), m0)
+    rank_b16 = shape((1, tokens, 2 * R), bf16)
+    all_down = block((2 * R, D), z2)
+    line_down = block((2 * R, wide), lambda m, g: (0, g))
+    done = None
+    for m, s in enumerate(slots):
+        low = s.low if done is None else after(s.low, done)
+        cot = cotangent[m, 0]
+        s.xin, s.z, s.bcin, s.rate_in, s.lr, s.cot0 = call(
+            project_kernel, "project", 2 * groups,
+            [(low[None], full_low),
+             (zx_weight, block((1, D, wide), lambda m, g: (1 - g // groups, 0, g % groups))),
+             (first_weight, block((D, 2 * NS + 128), z2)), (s.a_in, all_down),
+             (s.u_in, block((2 * R, wide), lambda m, g: (0, (g + groups) % (2 * groups))))],
+            [(tok_b16, block((1, tokens, wide), lambda m, g: (0, 0, jnp.minimum(g, groups - 1)))),
+             (tok_f32, block((1, tokens, wide), lambda m, g: (0, 0, jnp.maximum(g - groups, 0)))),
+             (shape((1, tokens, 2 * NS), bf16), bc_block), (sums_f32, sums), (rank_b16, rank_block)],
+            [], 4 * tokens * D * chan, act_bytes * 4, 2, (cot, rows_half, 0, True),
+        )
+        tail = jnp.concatenate([s.xin[:, tokens - HALO :], s.bcin[:, tokens - HALO :]], axis=2)
+        halo = lax.ppermute(tail, "mp", forward_edge)
+        s.halo, s.bchalo = halo[..., :chan], halo[..., chan:]
+        s.step, s.cum, s.lanes, s.bc = call(
+            prep_kernel, "prep", 1,
+            [(s.rate_in, sums), (bias, head_line), (rate, head_line), (s.mask[None], one_col), (s.bcin, bc_block),
+             (s.bchalo, bc_halo), (conv_bc, bc_taps)],
+            [(sums_f32, sums), (sums_f32, sums),
+             (shape((1, groups, 2 * HG, tokens), f32), block((1, groups, 2 * HG, tokens), lambda m, g: (0, 0, 0, 0))),
+             (bc_f32, bc_block)],
+            [], tokens * Q * 128 * 6, tokens * 128 * 24,
+        )
+        s.mixed, s.square, s.state, s.end, s.cot1 = call(
+            forward_kernel, "ssd_forward", groups,
+            [(s.xin, chan_block), (s.halo, halo_block), (taps, taps_block), (s.bc, bc_block), (s.cum, sums), (s.step, sums),
+             (s.lanes, lanes_block), (skip, line_block), (s.z, chan_block)],
+            [(tok_f32, chan_block), (sums_f32, sums), (state_f32, state_block), (state_f32, state_block)],
+            [pltpu.VMEM((blocks, Q, Q), f32), pltpu.VMEM((2, blocks, NS, Q), bf16), *line_scratch],
+            6 * tokens * Q * chan * 2, act_bytes * 3, 3, (cot, rows_half, halfway, True),
+        )
+        done = s.mixed
+
+    def reduce_rows(v):
+        theirs = lax.dynamic_slice_in_dim(v, (1 - core) * own, own, 0)
+        return lax.dynamic_slice_in_dim(v, core * own, own, 0) + other(theirs)
+
+    def fold(v):
+        return v[:R] + v[R:]
+
+    waiting = []
+    moved = []
+
+    def give(rows):
+        waiting.extend([(rows, moved_half, first, False) for first in (0, halfway)])
+
+    def carry(kernel, name, grid, ins, outs, scratch, flops, size, comm):
+        load = waiting.pop(0) if waiting else None
+        got = call(kernel, name, grid, ins, outs, scratch, flops, size, comm[load is not None] if not load or not load[2] else comm[1] + 10, load)
+        if load is not None:
+            moved.append(got[-1])
+            got = got[:-1]
+        return got
+
+    per = part // wide
+    cols = out_all.shape[3]
+    gs_weight = block((nd, 1, wide, cols), lambda m, g: (0, g // per, g % per, 0))
+    branch_weight = block((1,) + out_all.shape[1:], lambda m, g: (g, 0, 0, 0))
+    step_cols = block((1, tokens, cols), m3)
+    rank_rows = block((1, R, cols), m3)
+    rank_chan = block((1, R, chan // nd), m3)
+    full_chan = block((1, tokens, chan), m0)
+
+    def gated_grad(s):
+        cot = jnp.concatenate([s.cot0, s.cot1], 0)
+        gb_own = cot * s.mask_own.astype(bf16)
+        s.gb = pair_cat(gb_own, other(gb_own), 0)[None]
+        s.gs, dots, s.rg = carry(
+            gs_kernel, "gs", groups,
+            [(s.gb, full_low), (out_all, gs_weight), (s.u_out, all_down), (s.a_out, line_down), (s.mixed, chan_block),
+             (s.z, chan_block), (gain, line_block)],
+            [(tok_f32, chan_block), (sums_f32, sums), (rank_b16, rank_block)], [], 2 * tokens * D * chan, act_bytes * 5, (None, 4),
+        )
+        both = jnp.stack([jnp.sum(s.square, axis=-1), jnp.sum(dots, axis=-1)])
+        both = (both + other(both)) / DI
+        s.inv_gate = lax.rsqrt(both[0] + eps)[..., None]
+        s.coef = s.inv_gate**3 * both[1][..., None]
+
+    def gate_back(s):
+        s.dy, s.gz, s.scaled, s.lloc, s.q = carry(
+            gate_back_kernel, "gate_back", groups,
+            [(s.gs, chan_block), (s.mixed, chan_block), (s.z, chan_block), (s.inv_gate, one_col), (s.coef, one_col),
+             (gain, line_block), (s.bc, bc_block), (s.cum, sums)],
+            [(tok_f32, chan_block), (tok_b16, chan_block), (tok_b16, chan_block), (state_f32, state_block), (sums_f32, sums)],
+            [pltpu.VMEM((2, NS, tokens), bf16)], 6 * tokens * NS * chan, act_bytes * 5, (None, 5),
+        )
+
+    def project_out(m, s):
+        partial, s.g_up_out, s.g_out = carry(
+            branch_kernel, "branch", nd,
+            [(s.scaled, full_chan), (out_all, branch_weight), (s.a_out, block((2 * R, chan), z2)),
+             (s.u_out, block((2 * R, cols), lambda m, g: (0, g))), (s.rg, rank_block), (s.gb, step_cols)],
+            [(shape((1, tokens, D), f32), step_cols), (shape((1, R, D), f32), rank_rows), (shape((1, R, chan), f32), rank_chan)],
+            [pltpu.VMEM((tokens, 2 * R), bf16), pltpu.VMEM((2 * R, tokens), bf16), pltpu.VMEM((2 * R, tokens), bf16)],
+            2 * tokens * D * chan, act_bytes * 4, (None, 6),
+        )
+        branch = reduce_rows(partial[0])
+        give((x_rows[m].astype(f32) + s.mask_own * branch).astype(bf16))
+
+    def scan_back(s):
+        gx, head, tail, gbc, xu, dx = carry(
+            scan_back_kernel, "ssd_back", groups,
+            [(s.dy, chan_block), (s.xin, chan_block), (s.halo, halo_block), (taps, taps_block), (s.bc, bc_block), (s.cum, sums),
+             (s.step, sums), (s.lanes, lanes_block), (skip, line_block), (s.state, state_block), (s.lloc, state_block),
+             (s.end, state_block)],
+            [(tok_b16, chan_block), (edge_f32, edge_block), (edge_f32, edge_block), (bc_f32, bc_block), (sums_f32, sums),
+             (sums_f32, sums)],
+            [pltpu.VMEM((blocks, Q, Q), f32), pltpu.VMEM((blocks, Q, Q), f32), pltpu.VMEM((2, blocks, NS, Q), bf16),
+             pltpu.VMEM((2, blocks, NS, Q), bf16), *line_scratch],
+            12 * tokens * Q * chan * 2, act_bytes * 3, (7, 8),
+        )
+        gbc = gbc + other(gbc)
+        edge_bc = shape((1, 8, 2 * NS), f32)
+        gbc, bhead, btail, g_rate = call(
+            bc_back_kernel, "bc_back", 1,
+            [(gbc, bc_block), (s.bcin, bc_block), (s.bchalo, bc_halo), (conv_bc, bc_taps), (s.q, sums), (dx, sums), (xu, sums),
+             (s.step, sums), (s.rate_in, sums), (bias, head_line), (rate, head_line), (s.mask[None], one_col)],
+            [(shape((1, tokens, 2 * NS), bf16), bc_block), (edge_bc, bc_edge), (edge_bc, bc_edge),
+             (shape((1, tokens, 128), bf16), sums)],
+            [], tokens * tokens * 128 * 6, tokens * 2 * NS * 8,
+        )
+        back = lax.ppermute(jnp.concatenate([head, bhead], 2), "mp", backward_edge)
+        tail = jnp.concatenate([tail, btail], 2).at[:, 8 - (KC - 1) :].add(back[:, 8 - (KC - 1) :]).astype(bf16)
+        gx = lax.dynamic_update_slice_in_dim(gx, tail[..., :chan], tokens - 8, 1)
+        gbc = lax.dynamic_update_slice_in_dim(gbc, tail[..., chan:], tokens - 8, 1)[0]
+        half = lax.dynamic_slice_in_dim(gbc, core * NS, NS, 1)
+        tail = jnp.concatenate([half[None], g_rate], 2)
+        g_low, s.g_up_z, s.g_up_x, s.g_down = carry(
+            unproject_kernel, "unproject", D // wide,
+            [(s.gz, full_chan), (gx, full_chan), (tail, block((1, tokens, NS + 128), m0)),
+             (zx_weight, block((2, wide, chan), lambda m, g: (0, g, 0))), (tail_weight, block((wide, NS + 128), lambda m, g: (g, 0))),
+             (s.u_in, block((2 * R, 2 * chan), z2)), (s.a_in, line_down), (s.lr, rank_block), (s.low[None], chan_block)],
+            [(shape((1, tokens, D), f32), chan_block), (shape((1, R, chan), f32), block((1, R, wide), m3)),
+             (shape((1, R, chan), f32), block((1, R, wide), m3)), (shape((1, R, D), f32), block((1, R, wide), m3))],
+            [pltpu.VMEM((tokens, 2 * R), bf16), pltpu.VMEM((2 * R, tokens), bf16), pltpu.VMEM((2 * R, tokens), bf16)],
+            4 * tokens * D * chan, act_bytes * 3, (None, 9),
+        )
+        return g_low[0]
+
+    def input_grad(m, s, g_low):
+        gn = reduce_rows(g_low) * norm_gain
+        x = x_rows[m].astype(f32)
+        delta = s.inv * gn - x * (s.inv**3 * jnp.mean(gn * x, axis=-1, keepdims=True))
+        return delta.astype(bf16)
+
+    gated_grad(slots[0])
+    for m, s in enumerate(slots):
+        if m + 1 < micros:
+            gated_grad(slots[m + 1])
+        gate_back(s)
+        project_out(m, s)
+    for m, s in enumerate(slots):
+        delta = input_grad(m, s, scan_back(s))
+        if m + 1 < micros:
+            give(delta)
+    together = []
+    for at in range(0, len(moved), 2):
+        pair = jnp.stack([v.reshape(nz, halfway, feats) for v in moved[at : at + 2]], 1)
+        together.append(pair.reshape(seg, feats))
+    together.append(move_last(delta, moved_b16, nz, 30))
+    out = jnp.stack(together[:micros])[:, None]
+    grad = cotangent.astype(f32) + jnp.stack(together[micros:])[:, None].astype(f32)
+
+    picks = jnp.stack([s.pick for s in slots])
+
+    def near_sum(values):
+        v = jnp.stack([jnp.stack([g.reshape(R, nz, part) for g in gs]) for gs in values])
+        v = scatter_sum(jnp.transpose(v, (3, 0, 1, 2, 4)), "mp")
+        v = jnp.sum(picks[:, :, None, None, None] * v[:, None], axis=0)
+        v = scatter_sum(v.reshape((nd, 2) + v.shape[1:]), "dp")
+        keep = lax.dynamic_index_in_dim(v, core, 0, False)
+        give = lax.dynamic_index_in_dim(v, 1 - core, 0, False)
+        return pair_cat(keep[None], other(give)[None], 0)
+
+    def far_sum(values):
+        v = jnp.stack(values).reshape(micros, R, nd, 2, nz, each)
+        v = jnp.transpose(v, (3, 4, 0, 1, 2, 5))
+        v = lax.dynamic_index_in_dim(v, core, 0, False) + other(lax.dynamic_index_in_dim(v, 1 - core, 0, False))
+        v = scatter_sum(v, "mp")
+        v = jnp.sum(picks[:, :, None, None, None] * v[:, None], axis=0)
+        return scatter_sum(jnp.transpose(v, (2, 0, 1, 3)), "dp")
+
+    g_out_down = near_sum([[s.g_out] for s in slots])
+    g_out_down = jnp.transpose(g_out_down[:, 0], (0, 2, 1)).reshape(2 * part, R)
+    g_out_up = far_sum([s.g_up_out for s in slots]).reshape(ADAPT * R, each)
+    g_in_up = near_sum([[s.g_up_z, s.g_up_x] for s in slots])
+    g_in_up = jnp.transpose(g_in_up, (2, 1, 0, 3)).reshape(R, 2, 2 * part)
+    g_in_down = jnp.transpose(far_sum([s.g_down for s in slots]), (0, 2, 1))
+    return (out, grad, g_in_down, g_in_up, g_out_down, g_out_up)
+
+
 def solution(mesh):
     in_specs = (
         P(None, "dp", "seq", "mp"),
@@ -355,4 +1582,12 @@
         P("mp", ("dp", "seq")),
         P(None, ("dp", "seq", "mp")),
     )
-    return jax.shard_map(body, mesh=mesh, in_specs=in_specs, out_specs=out_specs, check_vma=False)
+    sizes = dict(mesh.shape)
+    by_chip = (
+        sizes["seq"] == 2
+        and sizes["dp"] * 2 == ADAPT
+        and sizes["mp"] % 2 == 0
+        and sizes["mp"] & (sizes["mp"] - 1) == 0
+        and (2048 // sizes["mp"]) % Q == 0
+    )
+    return jax.shard_map(fast_body if by_chip else body, mesh=mesh, in_specs=in_specs, out_specs=out_specs, check_vma=False)

time: 4640 us -> 1360 us (0.29)
  waiting for transfers between devices: 1300 us -> 42.6 us
  local copies, waits for them, and re-layouts: 1270 us -> 183 us
  matrix products: 883 us -> 0 us
  Pallas kernels: 0 us -> 882 us
  blocking collectives: 528 us -> 0 us
  other arithmetic: 566 us -> 137 us
  starting transfers between devices: 16.8 us -> 71.2 us
    dot_general x222 -> x0, matrix products: 883 us -> none  [the longest x36 234 us: block_step(): inner_out = jnp.einsum('tsh,shp->thp', mixing, x_part, precision=precise)]
    pallas_call x0 -> x29, Pallas kernels: none -> 882 us  [the longest x27 638 us: call(): pl.pallas_call(kernel, name=name, grid=(1, grid), in_specs=[s for _, s in...]
    psum x1 -> x0, waiting for transfers between devices: 832 us -> none  [body(): normed_sum, bc_sum = lax.psum((normed_part, bc_partial), 'mp')]
    dynamic_update_slice x180 -> x6, local copies, waits for them, and re-layouts: 699 us -> 3.62 us  [the longest x3 1.85 us: scan_back(): gx = lax.dynamic_update_slice_in_dim(gx, tail[..., :chan], tokens - 8, 1)]
    all_gather x5 -> x0, blocking collectives: 309 us -> none  [the longest x1 206 us: body(): lax.all_gather(in_down, ('dp', 'seq', 'mp'), axis=1, tiled=True)]
    reduce_scatter x4 -> x0, waiting for transfers between devices: 216 us -> none  [the longest x3 207 us: body(): lax.psum_scatter(partial_out, 'mp', scatter_dimension=2, tiled=True)]
    psum x2 -> x0, blocking collectives: 215 us -> none  [the longest x1 202 us: body(): normed_sum, bc_sum = lax.psum((normed_part, bc_partial), 'mp')]
    another operation x249 -> x27, local copies, waits for them, and re-layouts: 218 us -> 25.7 us  [the longest x6 7.29 us: near_sum(): jnp.stack([g.reshape(R, nz, part) for g in gs])]
  transfers between devices with their start and end apart: 29 -> 57, of which waited for: 9 -> 21; matrix products, arithmetic and copies ran while one was open for 40% -> 19% of each run, Pallas kernels for 0% -> 48%
where the time goes in v2:
time: 1360 us; the launch traced here: 1350 us
  Pallas kernels  882 us (65%)
  local copies, waits for them, and re-layouts  183 us (13%)
  other arithmetic  137 us (10%)
  starting transfers between devices  71.2 us (5%)
  waiting for transfers between devices  42.6 us (3%)
  between operations  33.3 us (2%)
    pallas_call x27, Pallas kernels, call(): pl.pallas_call(kernel, name=name, grid=(1, grid), in_specs=[s for _, s in...  638 us
    pallas_call x1, Pallas kernels, gather(): pl.pallas_call(functools.partial(gather_kernel, nd, nz), name='gather', o...  217 us
    select_n x11, other arithmetic, pair_cat(): jnp.where(core == 0, jnp.concatenate([mine, theirs], axis), jnp.concatena...  36.9 us
    ppermute x24, waiting for transfers between devices, scatter_sum(): total = total + lax.ppermute(give, axis, [(i, i ^ k) for i in range(count)])  33.5 us
  transfers between devices with their start and end apart: 57, of which 21 were waited for; matrix products, arithmetic and copies ran while one was open for 19% of the time, Pallas kernels for 48%

profile of v2, /device:TPU:9, one launch (start us, length us, event | category | flops | bytes accessed | tf_op | source)
XLA Modules:
  0.0 1349.4 jit_solution(18233241690857856908)
XLA Ops:
  21.7 217.3 %gather.1 = (bf16[2,2048,2048]{2,1,0:T(8,128)(2,1)}, bf16[3,256,2048]{2,1,0:T(8,128)(2,1)}) custom-call(bf16[2,256,1024]{2,1,0:T(8,128)(2,1)} %bitcast.493, bf16[3,1024,512]{2,1,0:T(8,128)(2,1)} %bitcast.494), custom_call_target="tpu_custom_call" | custom-call | tf_op jit(solution)/shard_map/gather/pallas_call | solution.py:491
  337.9 31.9 %project.3 = (bf16[1,512,2048]{2,1,0:T(8,128)(2,1)}, f32[1,512,2048]{2,1,0:T(8,128)}, bf16[1,512,256]{2,1,0:T(8,128)(2,1)}, f32[1,512,128]{2,1,0:T(8,128)}, bf16...) custom-call(bf16[1,512,2048]{2,1,0:T(8,128)(2,1)} %maximum_select_fusion.2.refs_0_.refs_8_, ...), custom_call_target="tpu_custom_call" | custom-call | flops 8589934592 | bytes 16777216 | tf_op jit(solution)/shard_map/project/pallas_call | solution.py:1165
  422.4 42.4 %ssd_forward.3 = (f32[1,512,2048]{2,1,0:T(8,128)}, f32[1,512,128]{2,1,0:T(8,128)}, f32[1,128,2048]{2,1,0:T(8,128)}, f32[1,128,2048]{2,1,0:T(8,128)}, bf16[128,2048]{1,0:T(8,128)(2,1)}) custom-call(bf16[1,512,2048]{2,1,0:T(8,128)(2,1)} %get-tuple-element.179.refs_0_.refs_1_, bf16[1,16,2048]{2,1,0:T(8,128)(2,1)} %slice.295.refs_1_.refs_2_, ...), custom_call_target="tpu_custom_call" | custom-call | flops 3221225472 | bytes 12582912 | tf_op jit(solution)/shard_map/ssd_forward/pallas_call | solution.py:1165
  464.8 33.8 %project.4 = (bf16[1,512,2048]{2,1,0:T(8,128)(2,1)}, f32[1,512,2048]{2,1,0:T(8,128)}, bf16[1,512,256]{2,1,0:T(8,128)(2,1)}, f32[1,512,128]{2,1,0:T(8,128)}, bf16...) custom-call(bf16[1,512,2048]{2,1,0:T(8,128)(2,1)} %bitcast.496, ...), custom_call_target="tpu_custom_call" | custom-call | flops 8589934592 | bytes 16777216 | tf_op jit(solution)/shard_map/project/pallas_call | solution.py:1165
  512.0 42.1 %ssd_forward.4 = (f32[1,512,2048]{2,1,0:T(8,128)}, f32[1,512,128]{2,1,0:T(8,128)}, f32[1,128,2048]{2,1,0:T(8,128)}, f32[1,128,2048]{2,1,0:T(8,128)}, bf16[128,2048]{1,0:T(8,128)(2,1)}) custom-call(bf16[1,512,2048]{2,1,0:T(8,128)(2,1)} %get-tuple-element.189.refs_0_.refs_1_, bf16[1,16,2048]{2,1,0:T(8,128)(2,1)} %slice.302.refs_1_.refs_2_, ...), custom_call_target="tpu_custom_call" | custom-call | flops 3221225472 | bytes 12582912 | tf_op jit(solution)/shard_map/ssd_forward/pallas_call | solution.py:1165
  554.1 34.5 %project.5 = (bf16[1,512,2048]{2,1,0:T(8,128)(2,1)}, f32[1,512,2048]{2,1,0:T(8,128)}, bf16[1,512,256]{2,1,0:T(8,128)(2,1)}, f32[1,512,128]{2,1,0:T(8,128)}, bf16...) custom-call(bf16[1,512,2048]{2,1,0:T(8,128)(2,1)} %bitcast.495, ...), custom_call_target="tpu_custom_call" | custom-call | flops 8589934592 | bytes 16777216 | tf_op jit(solution)/shard_map/project/pallas_call | solution.py:1165
  606.8 14.4 %gs.3 = (f32[1,512,2048]{2,1,0:T(8,128)}, f32[1,512,128]{2,1,0:T(8,128)}, bf16[1,512,32]{2,1,0:T(8,128)(2,1)}) custom-call(bf16[1,512,2048]{2,1,0:T(8,128)(2,1)} %maximum_select_fusion.4.gb_ref, bf16[4,4,512,512]{3,2,1,0:T(8,128)(2,1)} %bitcast.474, bf16[32,2048]{1,0:T(8,128)(2,1)} %copy-done.39, bf16[32,2048]{1,0:T(8,128)(2,1)} %copy-done.38, ...), custom_call_target="tpu_custom_call" | custom-call | flops 4294967296 | bytes 20971520 | tf_op jit(solution)/shard_map/gs/pallas_call | solution.py:1165
  622.4 40.5 %ssd_forward.5 = (f32[1,512,2048]{2,1,0:T(8,128)}, f32[1,512,128]{2,1,0:T(8,128)}, f32[1,128,2048]{2,1,0:T(8,128)}, f32[1,128,2048]{2,1,0:T(8,128)}, bf16[128,2048]{1,0:T(8,128)(2,1)}) custom-call(bf16[1,512,2048]{2,1,0:T(8,128)(2,1)} %get-tuple-element.200.refs_0_.refs_1_, bf16[1,16,2048]{2,1,0:T(8,128)(2,1)} %slice.305.refs_1_.refs_2_, ...), custom_call_target="tpu_custom_call" | custom-call | flops 3221225472 | bytes 12582912 | tf_op jit(solution)/shard_map/ssd_forward/pallas_call | solution.py:1165
  666.7 15.2 %gate_back.3 = (f32[1,512,2048]{2,1,0:T(8,128)}, bf16[1,512,2048]{2,1,0:T(8,128)(2,1)}, bf16[1,512,2048]{2,1,0:T(8,128)(2,1)}, f32[1,128,2048]{2,1,0:T(8,128)}, f32[1,512,128]{2,1,0:T(8,128)}) custom-call(f32[1,512,2048]{2,1,0:T(8,128)} %get-tuple-element.213.gs_ref, f32[1,512,2048]{2,1,0:T(8,128)} %get-tuple-element.187.mixed_ref, ...), custom_call_target="tpu_custom_call" | custom-call | flops 805306368 | bytes 20971520 | tf_op jit(solution)/shard_map/gate_back/pallas_call | solution.py:1165
  681.9 10.9 branch.3
  700.8 14.3 %gs.5 = (f32[1,512,2048]{2,1,0:T(8,128)}, f32[1,512,128]{2,1,0:T(8,128)}, bf16[1,512,32]{2,1,0:T(8,128)(2,1)}) custom-call(bf16[1,512,2048]{2,1,0:T(8,128)(2,1)} %maximum_select_fusion.5.gb_ref, bf16[4,4,512,512]{3,2,1,0:T(8,128)(2,1)} %bitcast.476, bf16[32,2048]{1,0:T(8,128)(2,1)} %copy-done.41, bf16[32,2048]{1,0:T(8,128)(2,1)} %copy-done.40, ...), custom_call_target="tpu_custom_call" | custom-call | flops 4294967296 | bytes 20971520 | tf_op jit(solution)/shard_map/gs/pallas_call | solution.py:1165
  726.6 26.5 %gate_back.4 = (f32[1,512,2048]{2,1,0:T(8,128)}, bf16[1,512,2048]{2,1,0:T(8,128)(2,1)}, bf16[1,512,2048]{2,1,0:T(8,128)(2,1)}, f32[1,128,2048]{2,1,0:T(8,128)}, ...) custom-call(f32[1,512,2048]{2,1,0:T(8,128)} %get-tuple-element.222.refs_0_, ...), custom_call_target="tpu_custom_call" | custom-call | flops 805306368 | bytes 20971520 | tf_op jit(solution)/shard_map/gate_back/pallas_call | solution.py:1165
  753.1 10.9 branch.4
  773.0 20.9 %gs.4 = (f32[1,512,2048]{2,1,0:T(8,128)}, f32[1,512,128]{2,1,0:T(8,128)}, bf16[1,512,32]{2,1,0:T(8,128)(2,1)}, bf16[512,512]{1,0:T(8,128)(2,1)}) custom-call(bf16[1,512,2048]{2,1,0:T(8,128)(2,1)} %maximum_select_fusion.3.refs_0_.refs_5_, bf16[4,4,512,512]{3,2,1,0:T(8,128)(2,1)} %bitcast.478, bf16[32,2048]{1,0:T(8,128)(2,1)} %copy-done.42, ...), custom_call_target="tpu_custom_call" | custom-call | flops 4294967296 | bytes 20971520 | tf_op jit(solution)/shard_map/gs/pallas_call | solution.py:1165
  803.5 20.2 %gate_back.5 = (f32[1,512,2048]{2,1,0:T(8,128)}, bf16[1,512,2048]{2,1,0:T(8,128)(2,1)}, bf16[1,512,2048]{2,1,0:T(8,128)(2,1)}, f32[1,128,2048]{2,1,0:T(8,128)}, ...) custom-call(f32[1,512,2048]{2,1,0:T(8,128)} %get-tuple-element.226.refs_0_, ...), custom_call_target="tpu_custom_call" | custom-call | flops 805306368 | bytes 20971520 | tf_op jit(solution)/shard_map/gate_back/pallas_call | solution.py:1165
  823.7 18.6 %branch.5 = (f32[1,512,2048]{2,1,0:T(8,128)}, f32[1,16,2048]{2,1,0:T(8,128)}, f32[1,16,2048]{2,1,0:T(8,128)}, bf16[512,512]{1,0:T(8,128)(2,1)}) custom-call(bf16[1,512,2048]{2,1,0:T(8,128)(2,1)} %get-tuple-element.233.refs_0_, bf16[4,4,512,512]{3,2,1,0:T(8,128)(2,1)} %bitcast.479, bf16[32,2048]{1,0:T(8,128)(2,1)} %copy-done.37, bf16[32,2048]{1,0:T(8,128)(2,1)} %copy-done.42, ...), custom_call_target="tpu_custom_call" | custom-call | flops 4294967296 | bytes 16777216 | tf_op jit(solution)/shard_map/branch/pallas_call | solution.py:1165
  853.9 56.3 %ssd_back.3 = (bf16[1,512,2048]{2,1,0:T(8,128)(2,1)}, f32[1,8,2048]{2,1,0:T(8,128)}, f32[1,8,2048]{2,1,0:T(8,128)}, f32[1,512,256]{2,1,0:T(8,128)}, f32[1,512,12...) custom-call(f32[1,512,2048]{2,1,0:T(8,128)} %get-tuple-element.236.refs_0_, ...), custom_call_target="tpu_custom_call" | custom-call | flops 6442450944 | bytes 12582912 | tf_op jit(solution)/shard_map/ssd_back/pallas_call | solution.py:1165
  932.5 23.9 %unproject.3 = (f32[1,512,2048]{2,1,0:T(8,128)}, f32[1,16,2048]{2,1,0:T(8,128)}, f32[1,16,2048]{2,1,0:T(8,128)}, f32[1,16,2048]{2,1,0:T(8,128)}, bf16[512,512]{1,0:T(8,128)(2,1)}) custom-call(bf16[1,512,2048]{2,1,0:T(8,128)(2,1)} %get-tuple-element.242.refs_0_, bf16[1,512,2048]{2,1,0:T(8,128)(2,1)} %slice_dynamic-update-slice_fusion.2.refs_1_, ...), custom_call_target="tpu_custom_call" | custom-call | flops 8589934592 | bytes 12582912 | tf_op jit(solution)/shard_map/unproject/pallas_call | solution.py:1165
  993.3 56.3 %ssd_back.4 = (bf16[1,512,2048]{2,1,0:T(8,128)(2,1)}, f32[1,8,2048]{2,1,0:T(8,128)}, f32[1,8,2048]{2,1,0:T(8,128)}, f32[1,512,256]{2,1,0:T(8,128)}, f32[1,512,12...) custom-call(f32[1,512,2048]{2,1,0:T(8,128)} %get-tuple-element.256.refs_0_, ...), custom_call_target="tpu_custom_call" | custom-call | flops 6442450944 | bytes 12582912 | tf_op jit(solution)/shard_map/ssd_back/pallas_call | solution.py:1165
  1073.0 23.9 %unproject.4 = (f32[1,512,2048]{2,1,0:T(8,128)}, f32[1,16,2048]{2,1,0:T(8,128)}, f32[1,16,2048]{2,1,0:T(8,128)}, f32[1,16,2048]{2,1,0:T(8,128)}, bf16[512,512]{1,0:T(8,128)(2,1)}) custom-call(bf16[1,512,2048]{2,1,0:T(8,128)(2,1)} %get-tuple-element.262.refs_0_, bf16[1,512,2048]{2,1,0:T(8,128)(2,1)} %slice_dynamic-update-slice_fusion.1.refs_1_, ...), custom_call_target="tpu_custom_call" | custom-call | flops 8589934592 | bytes 12582912 | tf_op jit(solution)/shard_map/unproject/pallas_call | solution.py:1165
  1143.9 55.3 %ssd_back.5 = (bf16[1,512,2048]{2,1,0:T(8,128)(2,1)}, f32[1,8,2048]{2,1,0:T(8,128)}, f32[1,8,2048]{2,1,0:T(8,128)}, f32[1,512,256]{2,1,0:T(8,128)}, f32[1,512,12...) custom-call(f32[1,512,2048]{2,1,0:T(8,128)} %get-tuple-element.276.refs_0_, ...), custom_call_target="tpu_custom_call" | custom-call | flops 6442450944 | bytes 12582912 | tf_op jit(solution)/shard_map/ssd_back/pallas_call | solution.py:1165
  1224.0 24.3 %unproject.5 = (f32[1,512,2048]{2,1,0:T(8,128)}, f32[1,16,2048]{2,1,0:T(8,128)}, f32[1,16,2048]{2,1,0:T(8,128)}, f32[1,16,2048]{2,1,0:T(8,128)}, bf16[512,512]{1,0:T(8,128)(2,1)}) custom-call(bf16[1,512,2048]{2,1,0:T(8,128)(2,1)} %get-tuple-element.282.refs_0_, bf16[1,512,2048]{2,1,0:T(8,128)(2,1)} %slice_dynamic-update-slice_fusion.refs_1_, ...), custom_call_target="tpu_custom_call" | custom-call | flops 8589934592 | bytes 12582912 | tf_op jit(solution)/shard_map/unproject/pallas_call | solution.py:1165
  1271.1 8.9 collective-permute-done.35
  1310.0 26.9 %move.1 = bf16[1024,512]{1,0:T(8,128)(2,1)} custom-call(bf16[256,2048]{1,0:T(8,128)(2,1)} %fusion.30.rows_ref), custom_call_target="tpu_custom_call" | custom-call | tf_op jit(solution)/shard_map/move/pallas_call | solution.py:1194
  (605 shorter events, 445.7 us)
Async XLA Ops:
  8.0 272.6 %all-reduce.6.cloned.1.call-start = ((), (), s32[]{:S(2)}) async-start(), calls=%async_computation.2 | async-start | bytes 172032
  18.8 281.0 %all-gather.4.cloned.1.call-start = ((), (), s32[]{:S(2)}) async-start(), calls=%async_computation | async-start | bytes 4038656 | tf_op jit(solution)/shard_map/all_gather | solution.py:1260
  20.4 586.4 %all-gather.6.cloned.1.call-start = ((), (), s32[]{:S(2)}) async-start(), calls=%async_computation.1 | async-start | bytes 8912896 | tf_op jit(solution)/shard_map/all_gather | solution.py:1264
  249.5 36.3 %collective-permute-start.2 = (bf16[256,2048]{1,0:T(8,128)(2,1)}, bf16[256,2048]{1,0:T(8,128)(2,1)}, u32[]{:S(2)}, u32[]{:S(2)}) collective-permute-start(bf16[256,2048]{1,0:T(8,128)(2,1)} %get-tuple-element.376), channel_id=1, source_target_pairs={{0,4},{4,0},{1,5},{5,1},{2,6},{6,2},{3,7},{7,3},{8,12},{12,8},{9,1... | collective-permute-start | bytes 3145736 | tf_op jit(solution)/shard_map/ppermute | solution.py:1233
  249.5 40.9 %collective-permute-start.1 = (bf16[256,2048]{1,0:T(8,128)(2,1)}, bf16[256,2048]{1,0:T(8,128)(2,1)}, u32[]{:S(2)}, u32[]{:S(2)}) collective-permute-start(bf16[256,2048]{1,0:T(8,128)(2,1)} %get-tuple-element.375), channel_id=1, source_target_pairs={{0,4},{4,0},{1,5},{5,1},{2,6},{6,2},{3,7},{7,3},{8,12},{12,8},{9,1... | collective-permute-start | bytes 3145736 | tf_op jit(solution)/shard_map/ppermute | solution.py:1233
  250.0 45.1 %collective-permute-start = (bf16[256,2048]{1,0:T(8,128)(2,1)}, bf16[256,2048]{1,0:T(8,128)(2,1)}, u32[]{:S(2)}, u32[]{:S(2)}) collective-permute-start(bf16[256,2048]{1,0:T(8,128)(2,1)} %get-tuple-element.377), channel_id=1, source_target_pairs={{0,4},{4,0},{1,5},{5,1},{2,6},{6,2},{3,7},{7,3},{8,12},{12,8},{9,1... | collective-permute-start | bytes 3145736 | tf_op jit(solution)/shard_map/ppermute | solution.py:1233
  372.1 44.6 %collective-permute-start.4 = (bf16[1,16,2304]{2,1,0:T(8,128)(2,1)}, bf16[1,16,2304]{2,1,0:T(8,128)(2,1)}, u32[]{:S(2)}, u32[]{:S(2)}) collective-permute-start(bf16[1,16,2304]{2,1,0:T(8,128)(2,1)} %pad_maximum_fusion.11), channel_id=1, source_target_pairs={{0,1},{1,2},{2,3},{4,5},{5,6},{6,7},{8,9},{9,10},{10,11},{12,13},{... | collective-permute-start | bytes 221192 | tf_op jit(solution)/shard_map/ppermute | solution.py:1376
  504.7 97.2 %collective-permute-start.9 = (bf16[256,2048]{1,0:T(8,128)(2,1)}, bf16[256,2048]{1,0:T(8,128)(2,1)}, u32[]{:S(2)}, u32[]{:S(2)}) collective-permute-start(bf16[256,2048]{1,0:T(8,128)(2,1)} %maximum_multiply_fusion.1), channel_id=1, source_target_pairs={{0,4},{4,0},{1,5},{5,1},{2,6},{6,2},{3,7},{7,3},{8,12},{12,8},{9,1... | collective-permute-start | bytes 3145736 | tf_op jit(solution)/shard_map/ppermute | solution.py:1233
  594.3 101.9 %collective-permute-start.12 = (bf16[256,2048]{1,0:T(8,128)(2,1)}, bf16[256,2048]{1,0:T(8,128)(2,1)}, u32[]{:S(2)}, u32[]{:S(2)}) collective-permute-start(bf16[256,2048]{1,0:T(8,128)(2,1)} %maximum_multiply_fusion.2), channel_id=1, source_target_pairs={{0,4},{4,0},{1,5},{5,1},{2,6},{6,2},{3,7},{7,3},{8,12},{12,8},{9,1... | collective-permute-start | bytes 3145736 | tf_op jit(solution)/shard_map/ppermute | solution.py:1233
  622.4 40.6 %collective-permute-start.10 = (f32[2,1,512]{2,1,0:T(1,128)S(1)}, f32[2,1,512]{2,1,0:T(1,128)S(1)}, u32[]{:S(2)}, u32[]{:S(2)}) collective-permute-start(f32[2,1,512]{2,1,0:T(1,128)S(1)} %pad_maximum_fusion.17), channel_id=1, source_target_pairs={{0,4},{4,0},{1,5},{5,1},{2,6},{6,2},{3,7},{7,3},{8,12},{12,8},{9,1... | collective-permute-start | bytes 12296 | tf_op jit(solution)/shard_map/ppermute | solution.py:1233
  696.0 27.0 %collective-permute-start.11 = (f32[256,2048]{1,0:T(8,128)}, f32[256,2048]{1,0:T(8,128)}, u32[]{:S(2)}, u32[]{:S(2)}) collective-permute-start(f32[256,2048]{1,0:T(8,128)} %dynamic-slice_bitcast_fusion.5), channel_id=1, source_target_pairs={{0,4},{4,0},{1,5},{5,1},{2,6},{6,2},{3,7},{7,3},{8,12},{12,8},{9,1... | collective-permute-start | bytes 6291464 | tf_op jit(solution)/shard_map/ppermute | solution.py:1233
  719.1 49.2 %collective-permute-start.7 = (bf16[256,2048]{1,0:T(8,128)(2,1)}, bf16[256,2048]{1,0:T(8,128)(2,1)}, u32[]{:S(2)}, u32[]{:S(2)}) collective-permute-start(bf16[256,2048]{1,0:T(8,128)(2,1)} %maximum_multiply_fusion), channel_id=1, source_target_pairs={{0,4},{4,0},{1,5},{5,1},{2,6},{6,2},{3,7},{7,3},{8,12},{12,8},{9,1... | collective-permute-start | bytes 3145736 | tf_op jit(solution)/shard_map/ppermute | solution.py:1233
  767.1 32.8 %collective-permute-start.15 = (f32[256,2048]{1,0:T(8,128)}, f32[256,2048]{1,0:T(8,128)}, u32[]{:S(2)}, u32[]{:S(2)}) collective-permute-start(f32[256,2048]{1,0:T(8,128)} %dynamic-slice_bitcast_fusion.4), channel_id=1, source_target_pairs={{0,4},{4,0},{1,5},{5,1},{2,6},{6,2},{3,7},{7,3},{8,12},{12,8},{9,1... | collective-permute-start | bytes 6291464 | tf_op jit(solution)/shard_map/ppermute | solution.py:1233
  959.6 27.5 %collective-permute-start.19 = (f32[256,2048]{1,0:T(8,128)}, f32[256,2048]{1,0:T(8,128)}, u32[]{:S(2)}, u32[]{:S(2)}) collective-permute-start(f32[256,2048]{1,0:T(8,128)} %dynamic-slice_bitcast_fusion.2), channel_id=1, source_target_pairs={{0,4},{4,0},{1,5},{5,1},{2,6},{6,2},{3,7},{7,3},{8,12},{12,8},{9,1... | collective-permute-start | bytes 6291464 | tf_op jit(solution)/shard_map/ppermute | solution.py:1233
  980.2 129.0 %collective-permute-start.47 = (f32[4,3,16,4,64]{4,2,3,1,0:T(8,128)}, f32[4,3,16,4,64]{4,2,3,1,0:T(8,128)}, u32[]{:S(2)}, u32[]{:S(2)}) collective-permute-start(f32[4,3,16,4,64]{4,2,3,1,0:T(8,128)} %dynamic-slice_bitcast_fusion.6), channel_id=1, source_target_pairs={{0,4},{4,0},{1,5},{5,1},{2,6},{6,2},{3,7},{7,3},{8,12},{12,8},{9,1... | collective-permute-start | bytes 589832 | tf_op jit(solution)/shard_map/ppermute | solution.py:1233
  984.0 67.2 %collective-permute-start.40 = (f32[3,1,16,512]{3,2,0,1:T(8,128)S(1)}, f32[3,1,16,512]{3,2,0,1:T(8,128)S(1)}, u32[]{:S(2)}, u32[]{:S(2)}) collective-permute-start(f32[3,1,16,512]{3,2,0,1:T(8,128)S(1)} %bitcast.552), channel_id=1, source_target_pairs={{0,1},{1,0},{2,3},{3,2},{4,5},{5,4},{6,7},{7,6},{8,9},{9,8},{10,11... | collective-permute-start | bytes 294920 | tf_op jit(solution)/shard_map/ppermute | solution.py:1210
  984.2 67.1 %collective-permute-start.41 = (f32[3,1,16,512]{3,2,0,1:T(8,128)S(1)}, f32[3,1,16,512]{3,2,0,1:T(8,128)S(1)}, u32[]{:S(2)}, u32[]{:S(2)}) collective-permute-start(f32[3,1,16,512]{3,2,0,1:T(8,128)S(1)} %bitcast.553), channel_id=1, source_target_pairs={{0,2},{1,3},{2,0},{3,1},{4,6},{5,7},{6,4},{7,5},{8,10},{9,11},{10,... | collective-permute-start | bytes 294920 | tf_op jit(solution)/shard_map/ppermute | solution.py:1210
  986.7 64.5 %collective-permute-start.42 = (f32[3,1,16,512]{3,2,0,1:T(8,128)S(1)}, f32[3,1,16,512]{3,2,0,1:T(8,128)S(1)}, u32[]{:S(2)}, u32[]{:S(2)}) collective-permute-start(f32[3,1,16,512]{3,2,0,1:T(8,128)S(1)} %bitcast.554), channel_id=1, source_target_pairs={{0,3},{1,2},{2,1},{3,0},{4,7},{5,6},{6,5},{7,4},{8,11},{9,10},{10,... | collective-permute-start | bytes 294920 | tf_op jit(solution)/shard_map/ppermute | solution.py:1210
  1100.1 37.1 %collective-permute-start.22 = (f32[256,2048]{1,0:T(8,128)}, f32[256,2048]{1,0:T(8,128)}, u32[]{:S(2)}, u32[]{:S(2)}) collective-permute-start(f32[256,2048]{1,0:T(8,128)} %dynamic-slice_bitcast_fusion.1), channel_id=1, source_target_pairs={{0,4},{4,0},{1,5},{5,1},{2,6},{6,2},{3,7},{7,3},{8,12},{12,8},{9,1... | collective-permute-start | bytes 6291464 | tf_op jit(solution)/shard_map/ppermute | solution.py:1233
  1256.4 14.7 %collective-permute-start.34 = (f32[3,2,16,512]{3,2,1,0:T(8,128)S(1)}, f32[3,2,16,512]{3,2,1,0:T(8,128)S(1)}, u32[]{:S(2)}, u32[]{:S(2)}) collective-permute-start(f32[3,2,16,512]{3,2,1,0:T(8,128)S(1)} %bitcast.544), channel_id=1, source_target_pairs={{0,2},{1,3},{2,0},{3,1},{4,6},{5,7},{6,4},{7,5},{8,10},{9,11},{10,... | collective-permute-start | bytes 589832 | tf_op jit(solution)/shard_map/ppermute | solution.py:1210
  1258.8 21.1 %collective-permute-start.35 = (f32[3,2,16,512]{3,2,1,0:T(8,128)S(1)}, f32[3,2,16,512]{3,2,1,0:T(8,128)S(1)}, u32[]{:S(2)}, u32[]{:S(2)}) collective-permute-start(f32[3,2,16,512]{3,2,1,0:T(8,128)S(1)} %bitcast.543), channel_id=1, source_target_pairs={{0,3},{1,2},{2,1},{3,0},{4,7},{5,6},{6,5},{7,4},{8,11},{9,10},{10,... | collective-permute-start | bytes 589832 | tf_op jit(solution)/shard_map/ppermute | solution.py:1210
  1260.6 42.8 %collective-permute-start.25 = (f32[256,2048]{1,0:T(8,128)}, f32[256,2048]{1,0:T(8,128)}, u32[]{:S(2)}, u32[]{:S(2)}) collective-permute-start(f32[256,2048]{1,0:T(8,128)} %dynamic-slice_bitcast_fusion), channel_id=1, source_target_pairs={{0,4},{4,0},{1,5},{5,1},{2,6},{6,2},{3,7},{7,3},{8,12},{12,8},{9,1... | collective-permute-start | bytes 6291464 | tf_op jit(solution)/shard_map/ppermute | solution.py:1233
  1264.2 16.3 %collective-permute-start.27 = (f32[3,16,4,64]{3,1,2,0:T(8,128)S(1)}, f32[3,16,4,64]{3,1,2,0:T(8,128)S(1)}, u32[]{:S(2)}, u32[]{:S(2)}) collective-permute-start(f32[3,16,4,64]{3,1,2,0:T(8,128)S(1)} %get-tuple-element.394), channel_id=1, source_target_pairs={{0,1},{1,0},{2,3},{3,2},{4,5},{5,4},{6,7},{7,6},{8,9},{9,8},{10,11... | collective-permute-start | bytes 147464 | tf_op jit(solution)/shard_map/ppermute | solution.py:1210
  1264.9 17.3 %collective-permute-start.28 = (f32[3,16,4,64]{3,1,2,0:T(8,128)S(1)}, f32[3,16,4,64]{3,1,2,0:T(8,128)S(1)}, u32[]{:S(2)}, u32[]{:S(2)}) collective-permute-start(f32[3,16,4,64]{3,1,2,0:T(8,128)S(1)} %get-tuple-element.396), channel_id=1, source_target_pairs={{0,2},{1,3},{2,0},{3,1},{4,6},{5,7},{6,4},{7,5},{8,10},{9,11},{10,... | collective-permute-start | bytes 147464 | tf_op jit(solution)/shard_map/ppermute | solution.py:1210
  (106 other events, 999.8 us)
Sparse Core Ops, SparseCore 0:
  19.0 42.2 all-reduce.5
Sparse Core Ops, SparseCore 1:
  22.1 104.9 all-gather.3
  251.8 116.0 all-gather.5

commit v3 on v0

--- a/solution.py
+++ b/solution.py
@@ -1,6 +1,10 @@
+import functools
+
 import jax
 import jax.numpy as jnp
 from jax import lax
+from jax.experimental import pallas as pl
+from jax.experimental.pallas import tpu as pltpu
 from jax.sharding import PartitionSpec as P
 
 D = 2048
@@ -11,10 +15,14 @@
 R = 16
 ADAPT = 8
 DI = 4096
+HG = 4
+HALO = 16
+SLOTS = 3
 
 
 eps = 1e-05
 precise = lax.Precision.HIGHEST
+VMEM_LIMIT = 56 * 1024 * 1024
 
 
 def shifted(array, axis, by):
@@ -325,6 +333,1309 @@
     return (jnp.stack(outputs), jnp.stack(x_grads), running[0], running[1], running[2], running[3])
 
 
+MESH = pl.DeviceIdType.MESH
+
+
+def split(v):
+    hi = v.astype(jnp.bfloat16)
+    return hi, (v - hi.astype(jnp.float32)).astype(jnp.bfloat16)
+
+
+def mm(a, b):
+    return lax.dot_general(a, b, (((1,), (0,)), ((), ())), preferred_element_type=jnp.float32)
+
+
+def mm_t(a, b):
+    return lax.dot_general(a, b, (((1,), (1,)), ((), ())), preferred_element_type=jnp.float32)
+
+
+def mm3(a, b):
+    return mm(a[0], b[0]) + mm(a[0], b[1]) + mm(a[1], b[0])
+
+
+def mm3_t(a, b):
+    return mm_t(a[0], b[0]) + mm_t(a[0], b[1]) + mm_t(a[1], b[0])
+
+
+def ones_mm(ones, v):
+    hi, lo = split(v)
+    rest = v - hi.astype(jnp.float32) - lo.astype(jnp.float32)
+    return mm(ones, hi) + mm(ones, lo) + mm(ones, rest.astype(jnp.bfloat16))
+
+
+def conv_rows(rows, halo, taps):
+    count = rows.shape[0]
+    ext = jnp.concatenate([halo, rows], axis=0).astype(jnp.float32)
+    first = HALO - (KC - 1)
+    total = taps[0:1] * ext[first : first + count]
+    for j in range(1, KC):
+        total = total + taps[j : j + 1] * ext[first + j : first + j + count]
+    return total
+
+
+def conv_rows_back(grad, taps):
+    count, width = grad.shape
+    zero = jnp.zeros((8, width), jnp.float32)
+    ext = jnp.concatenate([zero, grad, zero], axis=0)
+    total = taps[0:1] * ext[3 : 3 + count + 8]
+    for j in range(1, KC):
+        total = total + taps[j : j + 1] * ext[3 - j : 3 - j + count + 8]
+    return total
+
+
+def widen(columns):
+    rows = columns.shape[0]
+    lane = lax.broadcasted_iota(jnp.int32, (rows, 2 * P_SIZE), 1)
+    return jnp.concatenate(
+        [jnp.where(lane < P_SIZE, columns[:, h : h + 1], columns[:, h + 1 : h + 2]) for h in range(0, HG, 2)], axis=1
+    )
+
+
+def of_group(value, group):
+    return pltpu.roll(value, lax.rem(128 - group * HG, 128), 1)
+
+
+def head_sums(prod, group):
+    rows = prod.shape[1]
+    row = lax.broadcasted_iota(jnp.int32, (rows, 128), 0) // P_SIZE + group * HG
+    lane = lax.broadcasted_iota(jnp.int32, (rows, 128), 1)
+    pick = (row == lane).astype(jnp.float32).astype(jnp.bfloat16)
+    hi, lo = split(prod)
+    return mm(hi, pick) + mm(lo, pick)
+
+
+def lane_sum(v):
+    part = v[:, :128]
+    for k in range(1, v.shape[1] // 128):
+        part = part + v[:, k * 128 : (k + 1) * 128]
+    return part
+
+
+def add_up(ref, value, group):
+    @pl.when(group == 0)
+    def _():
+        ref[0] = value
+
+    @pl.when(group > 0)
+    def _():
+        ref[0] += value
+
+
+def run_of(slot, z):
+    return SLOTS * z + lax.rem(slot + z, SLOTS)
+
+
+def place_of(run):
+    z = run // SLOTS
+    return z, lax.rem(lax.rem(run, SLOTS) + SLOTS * SLOTS - z, SLOTS)
+
+
+class Mover:
+    def __init__(self, src_ref, dst_ref, send_sem, recv_sem, count, slots, to_rows):
+        self.refs = src_ref, dst_ref, send_sem, recv_sem
+        self.count, self.slots, self.to_rows = count, slots, to_rows
+        self.d, self.c, self.z = lax.axis_index("dp"), lax.axis_index("seq"), lax.axis_index("mp")
+        self.pieces = 4 * SLOTS if to_rows else count * len(slots)
+
+    def piece(self, n):
+        src_ref, dst_ref, send_sem, recv_sem = self.refs
+        if self.to_rows:
+            m, h, to_c = n // 4, n // 2 % 2, lax.rem(n + self.c, 2)
+            to_z, slot = place_of(m * self.count + 2 * self.c + h)
+            own = src_ref.shape[1] // 4
+            src = src_ref.at[m, pl.ds(pl.multiple_of((2 * h + to_c) * own, 16), own), :]
+            dst, sem = self.landing(slot - self.slots[0], self.z), (slot, self.z)
+            due = jnp.logical_and(slot >= self.slots[0], slot <= self.slots[-1])
+        else:
+            slot = self.slots[n // self.count]
+            to_z = lax.rem(self.z + n % self.count, self.count)
+            run = run_of(slot, self.z)
+            m, chunk = run // self.count, lax.rem(run, self.count)
+            to_c, q = chunk // 2, lax.rem(chunk, 2) * 2 + self.c
+            feats = dst_ref.shape[2]
+            src = src_ref.at[slot - self.slots[0], :, pl.ds(pl.multiple_of(to_z * feats, 128), feats)]
+            dst, sem = self.landing(m, q), (m, q)
+            due = True
+        here = jnp.logical_and(to_c == self.c, to_z == self.z)
+        near = pltpu.make_async_copy(src, dst, recv_sem.at[sem])
+        far = pltpu.make_async_remote_copy(
+            src_ref=src, dst_ref=dst, send_sem=send_sem.at[n], recv_sem=recv_sem.at[sem],
+            device_id=(self.d, to_c, to_z), device_id_type=MESH,
+        )
+        return jnp.logical_and(due, here), jnp.logical_and(due, jnp.logical_not(here)), near, far
+
+    def landing(self, first, slot):
+        dst_ref = self.refs[1]
+        if self.to_rows:
+            feats = dst_ref.shape[2] // self.count
+            return dst_ref.at[first, :, pl.ds(pl.multiple_of(slot * feats, 128), feats)]
+        rows = dst_ref.shape[1] // 4
+        return dst_ref.at[first, pl.ds(pl.multiple_of(slot * rows, 16), rows), :]
+
+    def greet(self, barrier):
+        for cc in range(2):
+            for r in range(self.count):
+                if cc or r:
+                    device = (self.d, lax.rem(self.c + cc, 2), lax.rem(self.z + r, self.count))
+                    pl.semaphore_signal(barrier, 1, device_id=device, device_id_type=MESH)
+        return 2 * self.count - 1
+
+    def start(self, n):
+        stays, goes, near, far = self.piece(n)
+
+        @pl.when(stays)
+        def _():
+            near.start()
+
+        @pl.when(goes)
+        def _():
+            far.start()
+
+    def start_at(self, step, steps):
+        for n in range(self.pieces):
+            @pl.when(step == n * steps * 7 // (8 * self.pieces))
+            def _():
+                self.start(n)
+
+    def finish(self):
+        recv_sem = self.refs[3]
+        if self.to_rows:
+            for slot in self.slots:
+                for s in range(self.count):
+                    area = self.landing(slot - self.slots[0], s)
+                    pltpu.make_async_copy(area, area, recv_sem.at[slot, s]).wait()
+        else:
+            for m in range(SLOTS):
+                for q in range(4):
+                    run = m * self.count + 2 * self.c + q // 2
+                    slot = place_of(run)[1]
+
+                    @pl.when(jnp.logical_and(slot >= self.slots[0], slot <= self.slots[-1]))
+                    def _():
+                        area = self.landing(m, q)
+                        pltpu.make_async_copy(area, area, recv_sem.at[m, q]).wait()
+        for n in range(self.pieces):
+            _, goes, _, far = self.piece(n)
+
+            @pl.when(goes)
+            def _():
+                far.wait_send()
+
+
+class Line:
+    def __init__(self, held_ref, sent_ref, send_sem, recv_sem, count, step):
+        self.refs = held_ref, sent_ref, send_sem, recv_sem
+        self.step, self.count = step, count
+        self.d, self.c, self.z = lax.axis_index("dp"), lax.axis_index("seq"), lax.axis_index("mp")
+        low, high = self.z > 0, self.z < count - 1
+        self.has_source, self.has_target = (low, high) if step > 0 else (high, low)
+        above, below = count - 1 - self.z, count - 2 - self.z
+        self.from_slot, self.to_slot = (above, below) if step > 0 else (below, above)
+
+    def greet(self, barrier):
+        @pl.when(self.has_source)
+        def _():
+            pl.semaphore_signal(barrier, 1, device_id=(self.d, self.c, self.z - self.step), device_id_type=MESH)
+        return jnp.where(self.has_target, 1, 0)
+
+    def copy(self, group):
+        held_ref, sent_ref, send_sem, recv_sem = self.refs
+        return pltpu.make_async_remote_copy(
+            src_ref=sent_ref.at[group], dst_ref=held_ref.at[group], send_sem=send_sem.at[group], recv_sem=recv_sem.at[group],
+            device_id=(self.d, self.c, self.z + self.step), device_id_type=MESH,
+        )
+
+    def receive(self, slot, group):
+        held_ref, sent_ref = self.refs[:2]
+        remote = jnp.logical_and(self.has_source, slot == self.from_slot)
+        fresh = slot == (0 if self.step > 0 else SLOTS - 1)
+        local = jnp.logical_not(jnp.logical_or(remote, fresh))
+
+        @pl.when(remote)
+        def _():
+            self.copy(group).wait_recv()
+            sent_ref[held_ref.shape[0] + group] = held_ref[group]
+
+        return jnp.where(jnp.logical_or(remote, local), sent_ref[held_ref.shape[0] + group], 0.0)
+
+    def send(self, slot, group, value):
+        held_ref, sent_ref = self.refs[:2]
+        sent_ref[held_ref.shape[0] + group] = value
+
+        @pl.when(jnp.logical_and(self.has_target, slot == self.to_slot))
+        def _():
+            sent_ref[group] = value
+            self.copy(group).start()
+
+    def finish(self):
+        @pl.when(self.has_target)
+        def _():
+            for g in range(self.refs[0].shape[0]):
+                self.copy(g).wait_send()
+
+
+class PairFill:
+    def __init__(self, own_ref, both_ref, buffer_ref, sems):
+        self.d, self.c, self.z = lax.axis_index("dp"), lax.axis_index("seq"), lax.axis_index("mp")
+        own = own_ref.shape[1]
+        mine = buffer_ref.at[:, pl.ds(pl.multiple_of(self.c * own, 16), own), :]
+        theirs = buffer_ref.at[:, pl.ds(pl.multiple_of((1 - self.c) * own, 16), own), :]
+        self.near = pltpu.make_async_copy(own_ref, mine, sems.at[0])
+        self.far = pltpu.make_async_remote_copy(
+            src_ref=own_ref, dst_ref=mine, send_sem=sems.at[1], recv_sem=sems.at[2], device_id=(self.d, 1 - self.c, self.z),
+            device_id_type=MESH,
+        )
+        self.arrival = pltpu.make_async_copy(theirs, theirs, sems.at[2])
+        self.keep = pltpu.make_async_copy(buffer_ref, both_ref, sems.at[3])
+
+    def greet(self, barrier):
+        pl.semaphore_signal(barrier, 1, device_id=(self.d, 1 - self.c, self.z), device_id_type=MESH)
+        return 1
+
+    def fill(self):
+        self.far.start()
+        self.near.start()
+        self.near.wait()
+        self.arrival.wait()
+        self.keep.start()
+
+    def finish(self):
+        self.far.wait_send()
+        self.keep.wait()
+
+
+def carried_by(kernel, count, first, to_rows, n_in, n_out, *refs):
+    ins, src_ref, outs, dst_ref = refs[:n_in], refs[n_in], refs[n_in + 1 : n_in + 1 + n_out], refs[n_in + 1 + n_out]
+    scratch, sems = refs[n_in + n_out + 2 : -2], refs[-2:]
+    kernel(*ins, *outs, *scratch, mover=Mover(src_ref, dst_ref, *sems, count, first, to_rows))
+
+
+def step_of(grid):
+    return pl.program_id(0) * grid[1] + pl.program_id(1)
+
+
+def begin(grid, *parties):
+    parties = [p for p in parties if p is not None]
+    if parties:
+        @pl.when(step_of(grid) == 0)
+        def _():
+            barrier = pltpu.get_barrier_semaphore()
+            waits = 0
+            for party in parties:
+                waits = waits + party.greet(barrier)
+            pl.semaphore_wait(barrier, waits)
+            for party in parties:
+                if isinstance(party, PairFill):
+                    party.fill()
+    for party in parties:
+        if isinstance(party, Mover):
+            party.start_at(step_of(grid), grid[0] * grid[1])
+
+
+def end(grid, *parties):
+    parties = [p for p in parties if p is not None]
+    if parties:
+        @pl.when(step_of(grid) == grid[0] * grid[1] - 1)
+        def _():
+            for party in parties:
+                party.finish()
+
+
+def twice_split(v):
+    hi, lo = split(v)
+    lane = lax.broadcasted_iota(jnp.int32, v.shape, 1)
+    return jnp.where(lane < v.shape[1] // 2, hi.astype(jnp.float32), lo.astype(jnp.float32)).astype(jnp.bfloat16)
+
+
+def fold(v):
+    half = v.shape[0] // 2
+    return v[:half] + v[half:]
+
+
+def merge(ref):
+    return ref[...].reshape(ref.shape[0] * ref.shape[1], ref.shape[2])
+
+
+def project_kernel(
+    grid, own_ref, w_ref, tailw_ref, down_ref, up_ref, xin_ref, z_ref, bcin_ref, rate_ref, lr_ref, both_ref, low_ref, sems,
+    mover=None
+):
+    step = pl.program_id(1)
+    pair = PairFill(own_ref, both_ref, low_ref, sems)
+    begin(grid, pair, mover)
+    slots, tokens = low_ref.shape[:2]
+
+    @pl.when(step == 0)
+    def _():
+        for m in range(slots):
+            tail = mm(low_ref[m], tailw_ref[...])
+            bcin_ref[m] = tail[:, : 2 * NS].astype(jnp.bfloat16)
+            rate_ref[m] = tail[:, 2 * NS :]
+            lr_ref[m] = twice_split(mm_t(low_ref[m], down_ref[m]))
+
+    value = mm(merge(low_ref), w_ref[0])
+    for m in range(slots):
+        part = value[m * tokens : (m + 1) * tokens] + mm(lr_ref[m], up_ref[m])
+
+        @pl.when(step < grid[1] // 2)
+        def _():
+            xin_ref[m] = part.astype(jnp.bfloat16)
+
+        @pl.when(step >= grid[1] // 2)
+        def _():
+            z_ref[m] = part
+
+    end(grid, pair, mover)
+
+
+def prep_kernel(rate_ref, bias_ref, decay_ref, mask_ref, bcin_ref, bchalo_ref, taps_ref, step_ref, cum_ref, lanes_ref, bc_ref):
+    rows = rate_ref.shape[1]
+    value = rate_ref[0] + bias_ref[...]
+    step = (jnp.maximum(value, 0.0) + jnp.log1p(jnp.exp(-jnp.abs(value)))) * mask_ref[0]
+    log = step * decay_ref[...]
+    tri = lax.broadcasted_iota(jnp.int32, (Q, Q), 0) >= lax.broadcasted_iota(jnp.int32, (Q, Q), 1)
+    tri = tri.astype(jnp.float32).astype(jnp.bfloat16)
+    step_ref[0] = step
+    cum = jnp.concatenate([ones_mm(tri, log[b * Q : (b + 1) * Q]) for b in range(rows // Q)], axis=0)
+    cum_ref[0] = cum
+    cum_t, step_t = cum.T, step.T
+    for g in range(lanes_ref.shape[1]):
+        lanes_ref[0, g, :HG] = cum_t[g * HG : (g + 1) * HG]
+        lanes_ref[0, g, HG:] = step_t[g * HG : (g + 1) * HG]
+    pre = conv_rows(bcin_ref[0], bchalo_ref[0], taps_ref[...])
+    bc_ref[0] = pre * jax.nn.sigmoid(pre)
+
+
+def forward_kernel(
+    grid, xin_ref, halo_ref, taps_ref, bc_ref, cum_ref, step_ref, lanes_ref, skip_ref, z_ref, mixed_ref, square_ref, state_ref,
+    end_ref, scores_ref, bt_ref, held_ref, sent_ref, send_sem, recv_sem, mover=None
+):
+    group = pl.program_id(1)
+    rows = xin_ref.shape[1]
+    blocks = rows // Q
+    line = Line(held_ref, sent_ref, send_sem, recv_sem, lax.axis_size("mp"), 1)
+    begin(grid, line, mover)
+
+    @pl.when(step_of(grid) == 0)
+    def _():
+        sent_ref[...] = jnp.zeros(sent_ref.shape, jnp.float32)
+
+    @pl.when(group == 0)
+    def _():
+        for b in range(blocks):
+            part = bc_ref[0, b * Q : (b + 1) * Q]
+            b_part = split(part[:, :NS])
+            c_part = split(part[:, NS:])
+            scores_ref[b] = mm3_t(c_part, b_part)
+            hi, lo = split(part[:, :NS].T)
+            bt_ref[0, b] = hi
+            bt_ref[1, b] = lo
+
+    pre = conv_rows(xin_ref[0], halo_ref[0], taps_ref[...])
+    x = pre * jax.nn.sigmoid(pre)
+    cums, decs, updates = [], [], []
+    for b in range(blocks):
+        at = slice(b * Q, (b + 1) * Q)
+        cum = of_group(cum_ref[0, at], group)
+        step = of_group(step_ref[0, at], group)
+        total = cum[Q - 1 : Q]
+        wx = x[at] * widen(jnp.exp(total - cum) * step)
+        cums.append(cum)
+        decs.append(widen(jnp.exp(total)))
+        updates.append(mm3((bt_ref[0, b], bt_ref[1, b]), split(wx)))
+
+    slot = pl.program_id(0)
+    states = [line.receive(slot, group)]
+    for b in range(blocks):
+        states.append(decs[b] * states[b] + updates[b])
+    state_ref[0] = states[0]
+    end_ref[0] = states[blocks]
+    line.send(slot, group, states[blocks])
+    lane = lax.broadcasted_iota(jnp.int32, (Q, 2 * P_SIZE), 1)
+    causal = lax.broadcasted_iota(jnp.int32, (Q, Q), 0) >= lax.broadcasted_iota(jnp.int32, (Q, Q), 1)
+    square = []
+    for b in range(blocks):
+        at = slice(b * Q, (b + 1) * Q)
+        scores = scores_ref[b]
+        xb = x[at]
+        carried = widen(jnp.exp(cums[b])) * mm3(split(bc_ref[0, at, NS:]), split(states[b]))
+        parts = []
+        for h in range(0, HG, 2):
+            pair = xb[:, h * P_SIZE : (h + 2) * P_SIZE]
+            x_hi, x_lo = split(pair)
+            both = jnp.concatenate([x_hi, x_lo], axis=1)
+            halves = []
+            for k in (h, h + 1):
+                spread = cums[b][:, k : k + 1] - lanes_ref[0, 0, k : k + 1, at]
+                decay = jnp.exp(jnp.where(causal, spread, -10000.0))
+                m_hi, m_lo = split(scores * decay * lanes_ref[0, 0, HG + k : HG + k + 1, at])
+                first = mm(m_hi, both)
+                halves.append(first[:, : 2 * P_SIZE] + first[:, 2 * P_SIZE :] + mm(m_lo, x_hi))
+            parts.append(jnp.where(lane < P_SIZE, halves[0], halves[1]))
+        mixed = jnp.concatenate(parts, axis=1) + skip_ref[0:1] * xb + carried
+        mixed_ref[0, at] = mixed
+        z = z_ref[0, at]
+        gated = mixed * (z * jax.nn.sigmoid(z))
+        square.append(lane_sum(gated * gated))
+    add_up(square_ref, jnp.concatenate(square, axis=0), group)
+
+    end(grid, line, mover)
+
+
+def chunk_decay(cum_ref, group):
+    rows = cum_ref.shape[1]
+    before = jnp.zeros((1, 128), jnp.float32)
+    parts = []
+    for b in range(rows // Q):
+        cum = of_group(cum_ref[0, b * Q : (b + 1) * Q], group)
+        parts.append(jnp.exp(cum + before))
+        before = before + cum[Q - 1 : Q]
+    return widen(jnp.concatenate(parts, axis=0))
+
+
+def gs_kernel(
+    grid, own_ref, w_ref, up_ref, down_ref, mixed_ref, z_ref, gain_ref, gs_ref, dot_ref, rg_ref, both_ref, gb_ref, sems
+):
+    step = pl.program_id(1)
+    pair = PairFill(own_ref, both_ref, gb_ref, sems)
+    begin(grid, pair)
+    slots, tokens = gb_ref.shape[:2]
+
+    @pl.when(step == 0)
+    def _():
+        for m in range(slots):
+            rg_ref[m] = twice_split(mm_t(gb_ref[m], up_ref[m]))
+
+    gb = merge(gb_ref)
+    width = w_ref.shape[3]
+    total = mm_t(gb[:, :width], w_ref[0, 0])
+    for n in range(1, w_ref.shape[0]):
+        total = total + mm_t(gb[:, n * width : (n + 1) * width], w_ref[n, 0])
+    for m in range(slots):
+        gs = total[m * tokens : (m + 1) * tokens] + mm(rg_ref[m], down_ref[m])
+        gs_ref[m] = gs
+        z = z_ref[m]
+        dots = lane_sum(gs * gain_ref[...] * (mixed_ref[m] * (z * jax.nn.sigmoid(z))))
+
+        @pl.when(step == 0)
+        def _():
+            dot_ref[m] = dots
+
+        @pl.when(step > 0)
+        def _():
+            dot_ref[m] += dots
+
+    end(grid, pair)
+
+
+def turned(v):
+    return v.astype(jnp.float32).T.astype(jnp.bfloat16)
+
+
+def branch_kernel(
+    grid, scaled_ref, w_ref, down_ref, up_ref, rg_ref, gb_ref, branch_ref, g_up_ref, g_down_ref, ro_ref, rot_ref, rgt_ref, mover=None
+):
+    step = pl.program_id(1)
+    begin(grid, mover)
+    slots, tokens = scaled_ref.shape[:2]
+
+    @pl.when(step == 0)
+    def _():
+        for m in range(slots):
+            ro = twice_split(mm_t(scaled_ref[m], down_ref[m]))
+            ro_ref[m] = ro
+            rot_ref[m] = turned(ro)
+            rgt_ref[m] = turned(rg_ref[m])
+
+    scaled = merge(scaled_ref)
+    width = w_ref.shape[2]
+    total = mm(scaled[:, :width], w_ref[0, 0])
+    for n in range(1, w_ref.shape[1]):
+        total = total + mm(scaled[:, n * width : (n + 1) * width], w_ref[0, n])
+    cols = g_down_ref.shape[2]
+    for m in range(slots):
+        branch_ref[m] = total[m * tokens : (m + 1) * tokens] + mm(ro_ref[m], up_ref[m])
+        g_up_ref[m] = fold(mm(rot_ref[m], gb_ref[m]))
+        g_down_ref[m] = fold(mm(rgt_ref[m], scaled_ref[m, :, pl.ds(pl.multiple_of(step * cols, 128), cols)]))
+    end(grid, mover)
+
+
+def unproject_kernel(
+    grid, gz_ref, gx_ref, tail_ref, w_ref, tailw_ref, up_ref, down_ref, lr_ref, low_ref, g_ref, upz_ref, upx_ref, g_down_ref,
+    ri_ref, rit_ref, lrt_ref, mover=None
+):
+    step = pl.program_id(1)
+    begin(grid, mover)
+    slots, tokens, chan = gz_ref.shape
+
+    @pl.when(step == 0)
+    def _():
+        for m in range(slots):
+            ri = twice_split(mm_t(gz_ref[m], up_ref[m, :, :chan]) + mm_t(gx_ref[m], up_ref[m, :, chan:]))
+            ri_ref[m] = ri
+            rit_ref[m] = turned(ri)
+            lrt_ref[m] = turned(lr_ref[m])
+
+    total = mm_t(merge(gz_ref), w_ref[0]) + mm_t(merge(gx_ref), w_ref[1]) + mm_t(merge(tail_ref), tailw_ref[...])
+    cols = upz_ref.shape[2]
+    at = pl.ds(pl.multiple_of(step * cols, 128), cols)
+    for m in range(slots):
+        g_ref[m] = total[m * tokens : (m + 1) * tokens] + mm(ri_ref[m], down_ref[m])
+        upz_ref[m] = fold(mm(lrt_ref[m], gz_ref[m, :, at]))
+        upx_ref[m] = fold(mm(lrt_ref[m], gx_ref[m, :, at]))
+        g_down_ref[m] = fold(mm(rit_ref[m], low_ref[m]))
+    end(grid, mover)
+
+
+def gate_back_kernel(
+    grid, gs_ref, mixed_ref, z_ref, inv_ref, coef_ref, gain_ref, bc_ref, cum_ref, dy_ref, gz_ref, scaled_ref, lam_ref, q_ref, ct_ref,
+    mover=None
+):
+    group = pl.program_id(1)
+    begin(grid, mover)
+
+    @pl.when(group == 0)
+    def _():
+        hi, lo = split(bc_ref[0, :, NS:].T)
+        ct_ref[0] = hi
+        ct_ref[1] = lo
+
+    z = z_ref[0]
+    mixed = mixed_ref[0]
+    sig = jax.nn.sigmoid(z)
+    act = z * sig
+    gated = mixed * act
+    inv = inv_ref[0]
+    gain = gain_ref[...]
+    scaled_ref[0] = (gated * inv * gain).astype(jnp.bfloat16)
+    g_gated = gs_ref[0] * gain * inv - gated * coef_ref[0]
+    dy = g_gated * act
+    dy_ref[0] = dy
+    gz_ref[0] = (g_gated * mixed * (sig * (1.0 + z * (1.0 - sig)))).astype(jnp.bfloat16)
+    lam_ref[0] = mm3((ct_ref[0], ct_ref[1]), split(dy * chunk_decay(cum_ref, group)))
+    add_up(q_ref, head_sums(dy * mixed, group), group)
+
+    end(grid, mover)
+
+
+def scan_back_kernel(
+    grid, dy_ref, xin_ref, halo_ref, taps_ref, bc_ref, cum_ref, step_ref, lanes_ref, skip_ref, state_ref, lam_ref, end_ref,
+    gx_ref, head_ref, tail_ref, gbc_ref, xu_ref, dx_ref, scorest_ref, dscorest_ref, bt_ref, ct_ref, held_ref, sent_ref, send_sem,
+    recv_sem, mover=None
+):
+    group = pl.program_id(1)
+    rows = xin_ref.shape[1]
+    blocks = rows // Q
+    line = Line(held_ref, sent_ref, send_sem, recv_sem, lax.axis_size("mp"), -1)
+    begin(grid, line, mover)
+
+    @pl.when(step_of(grid) == 0)
+    def _():
+        sent_ref[...] = jnp.zeros(sent_ref.shape, jnp.float32)
+
+    @pl.when(group == 0)
+    def _():
+        for b in range(blocks):
+            part = bc_ref[0, b * Q : (b + 1) * Q]
+            scorest_ref[b] = mm3_t(split(part[:, :NS]), split(part[:, NS:]))
+            dscorest_ref[b] = jnp.zeros((Q, Q), jnp.float32)
+            hi, lo = split(part[:, :NS].T)
+            bt_ref[0, b] = hi
+            bt_ref[1, b] = lo
+            hi, lo = split(part[:, NS:].T)
+            ct_ref[0, b] = hi
+            ct_ref[1, b] = lo
+        gbc_ref[0] = jnp.zeros((rows, 2 * NS), jnp.float32)
+        xu_ref[0] = jnp.zeros((rows, 128), jnp.float32)
+        dx_ref[0] = jnp.zeros((rows, 128), jnp.float32)
+
+    pre = conv_rows(xin_ref[0], halo_ref[0], taps_ref[...])
+    sig = jax.nn.sigmoid(pre)
+    x = pre * sig
+    lane = lax.broadcasted_iota(jnp.int32, (Q, 2 * P_SIZE), 1)
+    causal = lax.broadcasted_iota(jnp.int32, (Q, Q), 0) <= lax.broadcasted_iota(jnp.int32, (Q, Q), 1)
+    cums, step_cols, decs, rests, wide_steps = [], [], [], [], []
+    for b in range(blocks):
+        at = slice(b * Q, (b + 1) * Q)
+        cum = of_group(cum_ref[0, at], group)
+        step = of_group(step_ref[0, at], group)
+        total = cum[Q - 1 : Q]
+        cums.append(cum)
+        step_cols.append(step)
+        decs.append(widen(jnp.exp(total)))
+        rests.append(widen(jnp.exp(total - cum)))
+        wide_steps.append(widen(step))
+    states = [state_ref[0]]
+    for b in range(blocks - 1):
+        wx = x[b * Q : (b + 1) * Q] * rests[b] * wide_steps[b]
+        states.append(decs[b] * states[b] + mm3((bt_ref[0, b], bt_ref[1, b]), split(wx)))
+    slot = SLOTS - 1 - pl.program_id(0)
+    lam = line.receive(slot, group)
+    whole = decs[0]
+    for dec in decs[1:]:
+        whole = whole * dec
+    line.send(slot, group, whole * lam + lam_ref[0])
+    ends = jnp.sum(lam * end_ref[0], axis=0, keepdims=True)
+    g_parts = [None] * blocks
+    for b in reversed(range(blocks)):
+        at = slice(b * Q, (b + 1) * Q)
+        xb = x[at]
+        dy = dy_ref[0, at]
+        scores = scorest_ref[b]
+        dscores = dscorest_ref[b]
+        u_parts = []
+        for h in range(0, HG, 2):
+            pair = slice(h * P_SIZE, (h + 2) * P_SIZE)
+            x_hi, x_lo = split(xb[:, pair])
+            d_hi, d_lo = split(dy[:, pair])
+            both = jnp.concatenate([d_hi, d_lo], axis=1)
+            halves = []
+            for k in (h, h + 1):
+                mine = (lane < P_SIZE) if k == h else (lane >= P_SIZE)
+                spread = lanes_ref[0, 0, k : k + 1, at] - cums[b][:, k : k + 1]
+                decay = jnp.exp(jnp.where(causal, spread, -10000.0))
+                zero = jnp.zeros_like(x_hi)
+                xm_hi = jnp.where(mine, x_hi, zero)
+                xm_lo = jnp.where(mine, x_lo, zero)
+                dm = mm_t(xm_hi, d_hi) + mm_t(xm_hi, d_lo) + mm_t(xm_lo, d_hi)
+                dscores = dscores + dm * decay * step_cols[b][:, k : k + 1]
+                m_hi, m_lo = split(scores * decay)
+                first = mm(m_hi, both)
+                halves.append(first[:, : 2 * P_SIZE] + first[:, 2 * P_SIZE :] + mm(m_lo, d_hi))
+            u_parts.append(jnp.where(lane < P_SIZE, halves[0], halves[1]))
+        dscorest_ref[b] = dscores
+        lam_s = split(lam)
+        part = bc_ref[0, at]
+        step = wide_steps[b]
+        u = jnp.concatenate(u_parts, axis=1) + rests[b] * mm3(split(part[:, :NS]), lam_s)
+        ev = split(widen(jnp.exp(cums[b])) * dy)
+        gbc_ref[0, at, :NS] += mm3_t(split(rests[b] * step * xb), lam_s)
+        gbc_ref[0, at, NS:] += mm3_t(ev, split(states[b]))
+        if b > 0:
+            lam = decs[b] * lam + mm3((ct_ref[0, b], ct_ref[1, b]), ev)
+        xu_ref[0, at] += head_sums(xb * u, group)
+        direct = xb * dy * skip_ref[0:1]
+        if b == blocks - 1:
+            row = lax.broadcasted_iota(jnp.int32, (Q, HG * P_SIZE), 0)
+            direct = jnp.where(row == Q - 1, direct - ends, direct)
+        dx_ref[0, at] += head_sums(direct, group)
+        g_parts[b] = step * u + skip_ref[0:1] * dy
+    g_pre = jnp.concatenate(g_parts, axis=0) * (sig * (1.0 + pre * (1.0 - sig)))
+    g_ext = conv_rows_back(g_pre, taps_ref[...])
+    gx_ref[0] = g_ext[8:].astype(jnp.bfloat16)
+    head_ref[0] = g_ext[:8]
+    tail_ref[0] = g_ext[rows:]
+
+    @pl.when(group == pl.num_programs(1) - 1)
+    def _():
+        for b in range(blocks):
+            at = slice(b * Q, (b + 1) * Q)
+            part = bc_ref[0, at]
+            ds = dscorest_ref[b]
+            gbc_ref[0, at, :NS] += mm3(split(ds), split(part[:, NS:]))
+            gbc_ref[0, at, NS:] += mm3(split(ds.T), split(part[:, :NS]))
+
+    end(grid, line, mover)
+
+
+def finish_kernel(
+    count, near_ref, far_ref, picks_ref, rows_ref, moved_ref, near_out_ref, far_out_ref, near1_ref, far1_ref, near2_ref,
+    near2_in_ref, far2_ref, far2_in_ref, n1s, n1r, f1s, f1r, n2s, n2r, f2s, f2r, send_sem, recv_sem
+):
+    d, c, z = lax.axis_index("dp"), lax.axis_index("seq"), lax.axis_index("mp")
+    mover = Mover(rows_ref, moved_ref, send_sem, recv_sem, count, tuple(range(SLOTS)), False)
+    blocks = far2_ref.shape[0]
+    barrier = pltpu.get_barrier_semaphore()
+    waits = mover.greet(barrier)
+    others = [(i, j) for i in range(blocks) for j in range(2) if i or j]
+    for i, j in others:
+        device = (lax.rem(d + i, blocks), lax.rem(c + j, 2), z)
+        pl.semaphore_signal(barrier, 1, device_id=device, device_id_type=MESH)
+    pl.semaphore_wait(barrier, waits + len(others))
+
+    def remote(src, dst, send, recv, *device):
+        return pltpu.make_async_remote_copy(
+            src_ref=src, dst_ref=dst, send_sem=send, recv_sem=recv, device_id=device, device_id_type=MESH
+        )
+
+    def arrival(ref, at, sem):
+        pltpu.make_async_copy(ref.at[at], ref.at[at], sem.at[at]).wait()
+
+    me = c * count + z
+    copies = []
+    for i in range(1, count):
+        to = lax.rem(z + i, count)
+        copies.append(remote(near_ref.at[to], near1_ref.at[z], n1s.at[i], n1r.at[z], d, c, to))
+    column = [(j, i) for j in range(2) for i in range(count) if i or j]
+    for j, i in column:
+        to_c, to = lax.rem(c + j, 2), lax.rem(z + i, count)
+        copies.append(remote(far_ref.at[to_c * count + to], far1_ref.at[me], f1s.at[j * count + i], f1r.at[me], d, to_c, to))
+    for copy in copies:
+        copy.start()
+    for n in range(mover.pieces):
+        mover.start(n)
+
+    near = near_ref[z].astype(jnp.float32)
+    for i in range(1, count):
+        at = lax.rem(z + i, count)
+        arrival(near1_ref, at, n1r)
+        near = near + near1_ref[at].astype(jnp.float32)
+    far = far_ref[me].astype(jnp.float32)
+    for j, i in column:
+        at = lax.rem(c + j, 2) * count + lax.rem(z + i, count)
+        arrival(far1_ref, at, f1r)
+        far = far + far1_ref[at].astype(jnp.float32)
+    for a in range(ADAPT):
+        near2_ref[a] = sum(picks_ref[m, a] * near[m] for m in range(SLOTS))
+        for b in range(blocks):
+            far2_ref[b, a] = sum(picks_ref[m, a] * far[m, :, b] for m in range(SLOTS))
+
+    here = d * 2 + c
+    copies2 = []
+    for i, j in others:
+        to_d, to_c = lax.rem(d + i, blocks), lax.rem(c + j, 2)
+        copies2.append(
+            remote(near2_ref.at[to_d * 2 + to_c], near2_in_ref.at[here], n2s.at[i * 2 + j], n2r.at[here], to_d, to_c, z)
+        )
+    for i in range(1, blocks):
+        to = lax.rem(d + i, blocks)
+        copies2.append(remote(far2_ref.at[to], far2_in_ref.at[d], f2s.at[i], f2r.at[d], to, c, z))
+    for copy in copies2:
+        copy.start()
+    near2_in_ref[here] = near2_ref[here]
+    far_sum = far2_ref[d]
+    for i in range(1, blocks):
+        at = lax.rem(d + i, blocks)
+        arrival(far2_in_ref, at, f2r)
+        far_sum = far_sum + far2_in_ref[at]
+    far_out_ref[...] = far_sum
+    for i, j in others:
+        arrival(near2_in_ref, lax.rem(d + i, blocks) * 2 + lax.rem(c + j, 2), n2r)
+    for half in range(2):
+        near_out_ref[half] = sum(near2_in_ref[b * 2 + half] for b in range(blocks))
+    for copy in copies + copies2:
+        copy.wait_send()
+    mover.finish()
+
+
+def bc_back_kernel(
+    g_ref, in_ref, halo_ref, taps_ref, q_ref, dx_ref, xu_ref, step_ref, rate_ref, bias_ref, decay_ref, mask_ref,
+    out_ref, head_ref, tail_ref, g_rate_ref
+):
+    rows = in_ref.shape[1]
+    pre = conv_rows(in_ref[0], halo_ref[0], taps_ref[...])
+    sig = jax.nn.sigmoid(pre)
+    g_ext = conv_rows_back(g_ref[0] * (sig * (1.0 + pre * (1.0 - sig))), taps_ref[...])
+    out_ref[0] = g_ext[8:].astype(jnp.bfloat16)
+    head_ref[0] = g_ext[:8]
+    tail_ref[0] = g_ext[rows:]
+    xu = xu_ref[0]
+    flow = q_ref[0] - dx_ref[0] - step_ref[0] * xu
+    later = lax.broadcasted_iota(jnp.int32, (rows, rows), 0) <= lax.broadcasted_iota(jnp.int32, (rows, rows), 1)
+    g_log = ones_mm(later.astype(jnp.float32).astype(jnp.bfloat16), flow)
+    sig = jax.nn.sigmoid(rate_ref[0] + bias_ref[...])
+    g_rate_ref[0] = ((xu + g_log * decay_ref[...]) * mask_ref[0] * sig).astype(jnp.bfloat16)
+
+
+def flip(v, mask, count):
+    total = 0
+    bit = 1
+    while bit < count:
+        b = lax.rem(v // bit, 2)
+        total = total + (1 - b if mask & bit else b) * bit
+        bit *= 2
+    return total
+
+
+def gather_kernel(
+    nd, nz, wt_ref, x_ref, w_ref, rows_ref, local_sem, pair_sem, up_sem, down_sem, zrecv_sem, xsend_sem, xrecv_sem, ysend_sem,
+    yrecv_sem, hsend_sem, hrecv_sem, asend_sem, arecv_sem
+):
+    d, c, z = lax.axis_index("dp"), lax.axis_index("seq"), lax.axis_index("mp")
+    xn, yn = flip(d, 1, nd), flip(d, 2, nd)
+    rows, part = wt_ref.shape[1], wt_ref.shape[2] // 2
+
+    def remote(src, dst, send, recv, device):
+        return pltpu.make_async_remote_copy(
+            src_ref=src, dst_ref=dst, send_sem=send, recv_sem=recv, device_id=device, device_id_type=MESH
+        )
+
+    barrier = pltpu.get_barrier_semaphore()
+    for cc in range(2):
+        for r in range(nz):
+            if cc or r:
+                pl.semaphore_signal(barrier, 1, device_id=(d, flip(c, cc, 2), flip(z, r, nz)), device_id_type=MESH)
+    for dd in (xn, yn):
+        pl.semaphore_signal(barrier, 1, device_id=(dd, c, z), device_id_type=MESH)
+    pl.semaphore_wait(barrier, 2 * nz - 1 + 2)
+
+    def cols(s):
+        return pl.ds(pl.multiple_of(s * part, 128), part)
+
+    def area(dd, s):
+        return w_ref.at[:, pl.ds(pl.multiple_of(dd * (2 * rows), 16), 2 * rows), cols(s)]
+
+    def half_area(dd, s, h):
+        return w_ref.at[:, pl.ds(pl.multiple_of(dd * (2 * rows) + h * rows, 16), rows), cols(s)]
+
+    mine_area = w_ref.at[:, pl.ds(pl.multiple_of((2 * d + c) * rows, 16), rows), cols(z)]
+    keep = pltpu.make_async_copy(wt_ref.at[:, :, cols(c)], mine_area, local_sem.at[0])
+    pair = remote(wt_ref.at[:, :, cols(1 - c)], mine_area, pair_sem.at[0], pair_sem.at[1], (d, 1 - c, z))
+    keep.start()
+    pair.start()
+
+    mover = Mover(x_ref, rows_ref, asend_sem, arecv_sem, nz, tuple(range(SLOTS)), True)
+    for n in range(mover.pieces):
+        mover.start(n)
+
+    keep.wait()
+    pair.wait()
+
+    def spread(s):
+        remote(area(d, s), area(d, s), xsend_sem.at[s], xrecv_sem.at[s], (xn, c, z)).start()
+        remote(area(d, s), area(d, s), ysend_sem.at[s], yrecv_sem.at[s], (yn, c, z)).start()
+
+    def send_up(s):
+        @pl.when(z < nz - 1)
+        def _():
+            remote(area(d, s), area(d, s), up_sem.at[s], zrecv_sem.at[s], (d, c, z + 1)).start()
+
+    def send_down(s):
+        @pl.when(z > 0)
+        def _():
+            remote(area(d, s), area(d, s), down_sem.at[s], zrecv_sem.at[s], (d, c, z - 1)).start()
+
+    def relay(s):
+        remote(area(xn, s), area(xn, s), xsend_sem.at[s], xrecv_sem.at[s], (xn, c, z)).wait_recv()
+        remote(half_area(xn, s, 0), half_area(xn, s, 0), hsend_sem.at[0, s], hrecv_sem.at[0, s], (yn, c, z)).start()
+        remote(area(yn, s), area(yn, s), ysend_sem.at[s], yrecv_sem.at[s], (yn, c, z)).wait_recv()
+        remote(half_area(yn, s, 1), half_area(yn, s, 1), hsend_sem.at[1, s], hrecv_sem.at[1, s], (xn, c, z)).start()
+
+    send_up(z)
+    send_down(z)
+    spread(z)
+    for r in range(1, nz + 1):
+        if r < nz:
+            @pl.when(z - r >= 0)
+            def _():
+                s = z - r
+                remote(area(d, s), area(d, s), up_sem.at[s], zrecv_sem.at[s], (d, c, z)).wait_recv()
+                send_up(s)
+                spread(s)
+
+            @pl.when(z + r < nz)
+            def _():
+                s = z + r
+                remote(area(d, s), area(d, s), up_sem.at[s], zrecv_sem.at[s], (d, c, z)).wait_recv()
+                send_down(s)
+                spread(s)
+
+        if r == 1:
+            relay(z)
+        else:
+            @pl.when(z - r + 1 >= 0)
+            def _():
+                relay(z - r + 1)
+
+            @pl.when(z + r - 1 < nz)
+            def _():
+                relay(z + r - 1)
+
+    mover.finish()
+    for s in range(nz):
+        remote(half_area(d, s, 0), half_area(d, s, 0), hsend_sem.at[0, s], hrecv_sem.at[0, s], (yn, c, z)).wait()
+        remote(half_area(d, s, 1), half_area(d, s, 1), hsend_sem.at[1, s], hrecv_sem.at[1, s], (xn, c, z)).wait()
+        remote(area(d, s), area(d, s), xsend_sem.at[s], xrecv_sem.at[s], (xn, c, z)).wait_send()
+        remote(area(d, s), area(d, s), ysend_sem.at[s], yrecv_sem.at[s], (yn, c, z)).wait_send()
+
+        @pl.when(jnp.logical_and(s <= z, z < nz - 1))
+        def _():
+            remote(area(d, s), area(d, s), up_sem.at[s], zrecv_sem.at[s], (d, c, z)).wait_send()
+
+        @pl.when(jnp.logical_and(s >= z, z > 0))
+        def _():
+            remote(area(d, s), area(d, s), down_sem.at[s], zrecv_sem.at[s], (d, c, z)).wait_send()
+
+
+def gather(wt, x, nd, nz):
+    half = wt.shape[2] // 2
+    dma = pltpu.SemaphoreType.DMA
+    anywhere = pl.BlockSpec(memory_space=pl.ANY)
+    return pl.pallas_call(
+        functools.partial(gather_kernel, nd, nz),
+        name="gather",
+        out_shape=(
+            jax.ShapeDtypeStruct((2, wt.shape[1] * 2 * nd, half * nz), wt.dtype),
+            jax.ShapeDtypeStruct((SLOTS, x.shape[1] // 4, x.shape[2] * nz), x.dtype),
+        ),
+        in_specs=[anywhere] * 2,
+        out_specs=(anywhere,) * 2,
+        scratch_shapes=[
+            dma((1,)), dma((2,)), dma((nz,)), dma((nz,)), dma((nz,)), dma((nz,)), dma((nz,)), dma((nz,)), dma((nz,)),
+            dma((2, nz)), dma((2, nz)), dma((4 * SLOTS,)), dma((SLOTS, nz)),
+        ],
+        compiler_params=pltpu.CompilerParams(collective_id=1, has_side_effects=True),
+    )(wt, x)
+
+
+def block(shape, index):
+    return pl.BlockSpec(shape, index)
+
+
+def call(kernel, name, grid, ins, outs, scratch, flops, size, comm=None, load=None):
+    params = dict(vmem_limit_bytes=VMEM_LIMIT)
+    kernel = functools.partial(kernel, grid)
+    ins, outs, scratch = list(ins), list(outs), list(scratch)
+    if load is not None:
+        rows, result, first, to_rows = load
+        count = lax.axis_size("mp")
+        kernel = functools.partial(carried_by, kernel, count, first, to_rows, len(ins), len(outs))
+        ins.append((rows, pl.BlockSpec(memory_space=pl.ANY)))
+        outs.append((result, pl.BlockSpec(memory_space=pl.ANY)))
+        sends = 4 * SLOTS if to_rows else count * len(first)
+        scratch += [pltpu.SemaphoreType.DMA((sends,)), pltpu.SemaphoreType.DMA((SLOTS, 4))]
+    if comm is not None:
+        params.update(collective_id=comm, has_side_effects=True)
+    return pl.pallas_call(
+        kernel,
+        name=name,
+        grid=grid,
+        in_specs=[s for _, s in ins],
+        out_specs=[s for _, s in outs],
+        out_shape=[s for s, _ in outs],
+        scratch_shapes=scratch,
+        compiler_params=pltpu.CompilerParams(**params),
+        cost_estimate=pl.CostEstimate(flops=flops, bytes_accessed=size, transcendentals=0),
+    )(*[a for a, _ in ins])
+
+
+def skip_grid(kernel):
+    return lambda grid, *refs: kernel(*refs)
+
+
+def after(value, *deps):
+    return lax.optimization_barrier((value,) + deps)[0]
+
+
+def finish(near, far, picks, rows, moved, count):
+    dma, f32 = pltpu.SemaphoreType.DMA, jnp.float32
+    anywhere, vmem = pl.BlockSpec(memory_space=pl.ANY), pl.BlockSpec(memory_space=pltpu.VMEM)
+    blocks = far.shape[3]
+    near_shape, far_shape = near.shape[2:], far.shape[2:3] + far.shape[4:]
+    return pl.pallas_call(
+        functools.partial(finish_kernel, count),
+        name="finish",
+        in_specs=[vmem, vmem, pl.BlockSpec(memory_space=pltpu.SMEM), anywhere],
+        out_specs=[anywhere, vmem, vmem],
+        out_shape=[moved, jax.ShapeDtypeStruct((2,) + near_shape, f32), jax.ShapeDtypeStruct((ADAPT,) + far_shape, f32)],
+        scratch_shapes=[
+            pltpu.VMEM(near.shape, near.dtype), pltpu.VMEM(far.shape, far.dtype), pltpu.VMEM((ADAPT,) + near_shape, f32),
+            pltpu.VMEM((2 * blocks,) + near_shape, f32), pltpu.VMEM((blocks, ADAPT) + far_shape, f32),
+            pltpu.VMEM((blocks, ADAPT) + far_shape, f32), dma((count,)), dma((count,)), dma((2 * count,)), dma((2 * count,)),
+            dma((2 * blocks,)), dma((2 * blocks,)), dma((blocks,)), dma((blocks,)), dma((count * SLOTS,)), dma((SLOTS, 4)),
+        ],
+        compiler_params=pltpu.CompilerParams(vmem_limit_bytes=VMEM_LIMIT, collective_id=5, has_side_effects=True),
+    )(near, far, picks, rows)
+
+
+def fast_body(
+    x_in, cotangent, lengths, adapter_ids, norm_gain, w_zx, w_bc, w_dt, dt_bias, a_log, d_skip, conv_x, conv_bc,
+    gate_gain, w_out, in_down, in_up, out_down, out_up
+):
+    bf16, f32 = jnp.bfloat16, jnp.float32
+    micros, _, seg, feats = x_in.shape
+    nz, nd = lax.axis_size("mp"), lax.axis_size("dp")
+    core, z = lax.axis_index("seq"), lax.axis_index("mp")
+    own = seg // nz
+    tokens = 2 * own
+    heads = dt_bias.shape[0] * nz // 2
+    chan = heads * P_SIZE
+    part = chan // nz
+    groups = heads // HG
+    wide = HG * P_SIZE
+    blocks = tokens // Q
+    each = D // (nd * 2 * nz)
+
+    def other(v):
+        return lax.ppermute(v, "seq", [(0, 1), (1, 0)])
+
+    def pair_cat(mine, theirs, axis):
+        return jnp.where(
+            core == 0, jnp.concatenate([mine, theirs], axis), jnp.concatenate([theirs, mine], axis)
+        )
+
+    def halves(v, axis):
+        v = v.reshape(v.shape[:axis] + (2, v.shape[axis] // 2) + v.shape[axis + 1 :])
+        return (
+            lax.dynamic_index_in_dim(v, core, axis, False),
+            lax.dynamic_index_in_dim(v, 1 - core, axis, False),
+        )
+
+    line = 2 * part
+    bc_piece = lax.dynamic_slice_in_dim(w_bc, z * (w_bc.shape[0] // nz), w_bc.shape[0] // nz, 0)
+    pairs = jnp.stack([jnp.transpose(in_down, (0, 2, 1)), out_up.reshape(ADAPT, R, -1)], 1)
+    same = [bc_piece, pairs]
+    sized = [halves(in_up, 2), halves(out_down.T, 1), halves(w_dt.T, 0)]
+    packs = []
+    for k in range(2):
+        packs.append(jnp.concatenate([v.reshape(-1, line) for v in [s[k] for s in sized] + same], 0))
+    bounds = [0]
+    for v in [s[0] for s in sized] + same:
+        bounds.append(bounds[-1] + v.size // line)
+    pack = pair_cat(packs[0][None], other(packs[1])[None], 0)
+    params = jnp.concatenate([dt_bias, a_log, d_skip, gate_gain, conv_x.reshape(-1)])
+    params = lax.all_gather(params, "mp")
+    pack = lax.all_gather(pack, ("dp", "mp")).reshape((nd, nz) + pack.shape)
+    zx_weight, x_rows = gather(jnp.transpose(w_zx, (1, 0, 2)), x_in[:, 0], nd, nz)
+    out_mine, out_theirs = halves(after(w_out, x_rows), 0)
+    out_pair = pair_cat(out_mine, other(out_theirs), 1)
+    out_all = lax.all_gather(out_pair, ("dp", "mp")).reshape((nd, nz) + out_pair.shape)
+    dt_rows = pack[:, :, :, bounds[2] : bounds[3]].reshape(nd, nz, 2, heads // nz, -1)
+    dt_weight = jnp.transpose(dt_rows, (1, 3, 0, 2, 4)).reshape(heads, D)
+    dt_weight = jnp.pad(dt_weight, ((0, 128 - heads), (0, 0)))
+    bc_rows = pack[:, :, :, bounds[3] : bounds[4]].reshape(nd, nz, 2, -1, 2 * NS)
+    bc_weight = jnp.transpose(bc_rows, (0, 2, 1, 3, 4)).reshape(D, 2 * NS)
+    bc_half = lax.dynamic_slice_in_dim(bc_weight, core * NS, NS, 1)
+    dt_weight = dt_weight.T
+    tail_weight = jnp.concatenate([bc_half, dt_weight], 1)
+    first_weight = jnp.concatenate([bc_weight, dt_weight], 1)
+
+    hl = dt_bias.shape[0]
+
+    def own_part(v):
+        v = v.reshape(v.shape[0], 2, v.shape[1] // 2)
+        return lax.dynamic_index_in_dim(v, core, 1, False).reshape(-1)
+
+    bias = jnp.pad(own_part(params[:, :hl]), (0, 128 - heads))[None]
+    rate = jnp.pad(-jnp.exp(own_part(params[:, hl : 2 * hl])), (0, 128 - heads))[None]
+    skip = jnp.repeat(own_part(params[:, 2 * hl : 3 * hl]), P_SIZE)[None]
+    width = gate_gain.shape[0]
+    gain = own_part(params[:, 3 * hl : 3 * hl + width])[None]
+    taps = params[:, 3 * hl + width :].reshape(nz, KC, 2, part)
+    taps = jnp.transpose(lax.dynamic_index_in_dim(taps, core, 2, False), (1, 0, 2)).reshape(KC, chan)
+
+    order = jnp.arange(micros)
+    runs = run_of(order, z)
+    sequence, chunk = runs // nz, lax.rem(runs, nz)
+    lengths = jnp.take(lengths[:, 0], sequence)[:, None]
+    ids = jnp.take(adapter_ids[:, 0], sequence)
+    all_pos = (chunk * tokens)[:, None] + jnp.arange(tokens)
+    own_pos = (chunk * tokens)[:, None] + core * own + jnp.arange(own)
+    enters = (order == nz - 1 - z)[:, None, None]
+    leaves = (order == nz - 2 - z)[:, None, None]
+    forward_edge = [(i, i + 1) for i in range(nz - 1)]
+    backward_edge = [(i + 1, i) for i in range(nz - 1)]
+
+    m3 = lambda m, g: (m, 0, g)
+    m0 = lambda m, g: (m, 0, 0)
+    z2 = lambda m, g: (0, 0)
+    shape = jax.ShapeDtypeStruct
+
+    def per_token(width, index=m3):
+        return block((1, tokens, width), index)
+
+    chan_block = per_token(wide)
+    halo_block = block((1, HALO, wide), m3)
+    taps_block = block((KC, wide), lambda m, g: (0, g))
+    line_block = block((1, wide), lambda m, g: (0, g))
+    state_block = block((1, NS, wide), m3)
+    bc_block = per_token(2 * NS, m0)
+    bc_halo = block((1, HALO, 2 * NS), m0)
+    bc_taps = block((KC, 2 * NS), z2)
+    bc_edge = block((1, 8, 2 * NS), m0)
+    one_col = per_token(1, m0)
+    sums = per_token(128, m0)
+    lanes_block = block((1, 1, 2 * HG, tokens), lambda m, g: (m, g, 0, 0))
+    head_line = block((1, 128), z2)
+    edge_block = block((1, 8, wide), m3)
+    tok_f32 = shape((micros, tokens, chan), f32)
+    tok_b16 = shape((micros, tokens, chan), bf16)
+    state_f32 = shape((micros, NS, chan), f32)
+    bc_f32 = shape((micros, tokens, 2 * NS), f32)
+    sums_f32 = shape((micros, tokens, 128), f32)
+    edge_f32 = shape((micros, 8, chan), f32)
+    act_bytes = tokens * chan * 4
+    dma = pltpu.SemaphoreType.DMA
+    line_scratch = [pltpu.VMEM((groups, NS, wide), f32), pltpu.VMEM((2 * groups, NS, wide), f32)] + [dma((groups,))] * 2
+    scan_grid = (micros, groups)
+
+    x_rows = x_rows.astype(f32)
+    inv_rms = lax.rsqrt(jnp.mean(x_rows * x_rows, axis=-1, keepdims=True) + eps)
+    low_own = (x_rows * inv_rms * norm_gain).astype(bf16)
+    mask_own = (own_pos < lengths).astype(f32)[..., None]
+    mask = (all_pos < lengths).astype(f32)[..., None]
+    picks = (adapter_ids == jnp.arange(ADAPT)).astype(f32)
+    near, wide_rows = [], []
+    for m in range(micros):
+        got = lax.dynamic_index_in_dim(pack, ids[m] // 2, 0, False)[:, :, : bounds[2]]
+        near.append(lax.dynamic_index_in_dim(got, ids[m] % 2, 1, False))
+        wide_rows.append(lax.dynamic_slice_in_dim(pack, bounds[4] + 2 * ids[m], 2, 3))
+    near = jnp.stack(near)
+    u_in = near[:, :, : bounds[1]].reshape(micros, nz, R, 2, part)
+    u_in = jnp.transpose(u_in, (0, 2, 3, 1, 4)).reshape(micros, R, 2 * chan)
+    a_out = near[:, :, bounds[1] :].reshape(micros, nz, R, part)
+    a_out = jnp.transpose(a_out, (0, 2, 1, 3)).reshape(micros, R, chan)
+    wide_rows = jnp.stack(wide_rows).reshape(micros, nd, nz, 2, 2, R, each)
+    wide_rows = jnp.transpose(wide_rows, (4, 0, 5, 1, 3, 2, 6)).reshape(2, micros, R, D)
+    u_in, a_out = [jnp.concatenate([v, v], 1) for v in (u_in, a_out)]
+    a_in, u_out = jnp.concatenate([wide_rows, wide_rows], 2)
+
+    def every(width, index=None):
+        if index is None:
+            return pl.BlockSpec((micros, tokens, width), lambda m, g: (0, 0, 0), pipeline_mode=pl.Buffered(1))
+        return block((micros, tokens, width), index)
+
+    by_step = lambda m, g: (0, 0, g)
+    rank_b16 = shape((micros, tokens, 2 * R), bf16)
+    all_down = block((micros, 2 * R, D), lambda m, g: (0, 0, 0))
+    half_steps = chan // part
+    steps = 2 * half_steps
+    cot = cotangent[:, 0]
+    early = 1
+    hbm = pl.BlockSpec(memory_space=pl.ANY)
+    pair_scratch = [pltpu.VMEM((micros, tokens, D), bf16), dma((4,))]
+    xin, z_in, bcin, rate_in, lr, low, cot_early = call(
+        project_kernel, "project", (1, steps),
+        [(low_own, hbm), (zx_weight, block((1, D, part), lambda m, g: (1 - g // half_steps, 0, g % half_steps))),
+         (first_weight, block((D, 2 * NS + 128), z2)), (a_in, all_down),
+         (u_in, block((micros, 2 * R, part), lambda m, g: (0, 0, (g + half_steps) % steps)))],
+        [(tok_b16, every(part, lambda m, g: (0, 0, jnp.minimum(g, half_steps - 1)))),
+         (tok_f32, every(part, lambda m, g: (0, 0, jnp.maximum(g - half_steps, 0)))),
+         (shape((micros, tokens, 2 * NS), bf16), every(2 * NS)), (sums_f32, every(128)), (rank_b16, every(2 * R)), (shape((micros, tokens, D), bf16), hbm)],
+        pair_scratch, 4 * tokens * D * chan, act_bytes * 4, 2, (cot, shape((early, own, D), bf16), tuple(range(early)), True),
+    )
+    tail = jnp.concatenate([xin[:, tokens - HALO :], bcin[:, tokens - HALO :]], axis=2)
+    goes = jnp.sum(jnp.where(leaves, tail, 0), axis=0, dtype=bf16)
+    halo = jnp.where(enters, lax.ppermute(goes, "mp", forward_edge)[None], jnp.pad(tail[:-1], ((1, 0), (0, 0), (0, 0))))
+    halo, bchalo = halo[..., :chan], halo[..., chan:]
+    step, cum, lanes, bc = call(
+        skip_grid(prep_kernel), "prep", (micros, 1),
+        [(rate_in, sums), (bias, head_line), (rate, head_line), (mask, one_col), (bcin, bc_block), (bchalo, bc_halo),
+         (conv_bc, bc_taps)],
+        [(sums_f32, sums), (sums_f32, sums),
+         (shape((micros, groups, 2 * HG, tokens), f32), block((1, groups, 2 * HG, tokens), lambda m, g: (m, 0, 0, 0))),
+         (bc_f32, bc_block)],
+        [], tokens * Q * 128 * 6, tokens * 128 * 24,
+    )
+    mixed, square, state, end_state, cot_late = call(
+        forward_kernel, "ssd_forward", scan_grid,
+        [(xin, chan_block), (halo, halo_block), (taps, taps_block), (bc, bc_block), (cum, sums), (step, sums),
+         (lanes, lanes_block), (skip, line_block), (z_in, chan_block)],
+        [(tok_f32, chan_block), (sums_f32, sums), (state_f32, state_block), (state_f32, state_block)],
+        [pltpu.VMEM((blocks, Q, Q), f32), pltpu.VMEM((2, blocks, NS, Q), bf16), *line_scratch],
+        6 * tokens * Q * chan * 2, act_bytes * 3, 3, (cot, shape((micros - early, own, D), bf16), tuple(range(early, micros)), True),
+    )
+
+    def reduce_rows(v):
+        theirs = lax.dynamic_slice_in_dim(v, (1 - core) * own, own, 1)
+        return lax.dynamic_slice_in_dim(v, core * own, own, 1) + other(theirs)
+
+    cols = out_all.shape[3]
+    gb_own = jnp.concatenate([cot_early, cot_late], 0) * mask_own.astype(bf16)
+    part_block = every(part, by_step)
+    gs, dots, rg, gb = call(
+        gs_kernel, "gs", (1, nz),
+        [(gb_own, hbm), (out_all, block((nd, 1, part, cols), lambda m, g: (0, g, 0, 0))), (u_out, all_down),
+         (a_out, block((micros, 2 * R, part), by_step)), (mixed, part_block), (z_in, part_block),
+         (gain, block((1, part), lambda m, g: (0, g)))],
+        [(tok_f32, part_block), (sums_f32, every(128)), (rank_b16, every(2 * R)), (shape((micros, tokens, D), bf16), hbm)],
+        pair_scratch, 6 * tokens * D * chan, act_bytes * 15, 7,
+    )
+    both = jnp.stack([jnp.sum(square, axis=-1), jnp.sum(dots, axis=-1)])
+    both = (both + other(both)) / DI
+    inv_gate = lax.rsqrt(both[0] + eps)[..., None]
+    coef = inv_gate**3 * both[1][..., None]
+    dy, gz, scaled, lloc, q = call(
+        gate_back_kernel, "gate_back", scan_grid,
+        [(gs, chan_block), (mixed, chan_block), (z_in, chan_block), (inv_gate, one_col), (coef, one_col), (gain, line_block),
+         (bc, bc_block), (cum, sums)],
+        [(tok_f32, chan_block), (tok_b16, chan_block), (tok_b16, chan_block), (state_f32, state_block), (sums_f32, sums)],
+        [pltpu.VMEM((2, NS, tokens), bf16)], 6 * tokens * NS * chan, act_bytes * 5,
+    )
+    step_cols = every(cols, by_step)
+    rank_scratch = [pltpu.VMEM((micros, tokens, 2 * R), bf16)] + [pltpu.VMEM((micros, 2 * R, tokens), bf16)] * 2
+    rank_cols = block((micros, R, cols), by_step)
+    partial, g_up_out, g_out = call(
+        branch_kernel, "branch", (1, nd),
+        [(scaled, every(chan)), (out_all, block((1,) + out_all.shape[1:], lambda m, g: (g, 0, 0, 0))),
+         (a_out, block((micros, 2 * R, chan), lambda m, g: (0, 0, 0))), (u_out, block((micros, 2 * R, cols), by_step)),
+         (rg, every(2 * R)), (gb, step_cols)],
+        [(shape((micros, tokens, D), f32), step_cols), (shape((micros, R, D), f32), rank_cols),
+         (shape((micros, R, chan), f32), block((micros, R, chan // nd), by_step))],
+        rank_scratch, 6 * tokens * D * chan, act_bytes * 12,
+    )
+    out_rows = (x_rows + mask_own * reduce_rows(partial)).astype(bf16)
+
+    first_slots, last_slots = tuple(range(micros - 1)), (micros - 1,)
+
+    def last_first(spec):
+        index = spec.index_map
+        return block(spec.block_shape, lambda m, g: index(micros - 1 - m, g))
+
+    ins = [(dy, chan_block), (xin, chan_block), (halo, halo_block), (taps, taps_block), (bc, bc_block), (cum, sums), (step, sums),
+           (lanes, lanes_block), (skip, line_block), (state, state_block), (lloc, state_block), (end_state, state_block)]
+    outs = [(tok_b16, chan_block), (edge_f32, edge_block), (edge_f32, edge_block), (bc_f32, bc_block), (sums_f32, sums),
+            (sums_f32, sums)]
+    gx, head, tail, gbc, xu, dx, out_first = call(
+        scan_back_kernel, "ssd_back", scan_grid,
+        [(a, last_first(s)) for a, s in ins], [(a, last_first(s)) for a, s in outs],
+        [pltpu.VMEM((blocks, Q, Q), f32), pltpu.VMEM((blocks, Q, Q), f32), pltpu.VMEM((2, blocks, NS, Q), bf16),
+         pltpu.VMEM((2, blocks, NS, Q), bf16), *line_scratch],
+        12 * tokens * Q * chan * 2, act_bytes * 3, 4, (out_rows, shape((micros, seg, feats), bf16), first_slots, False),
+    )
+    gbc = gbc + other(gbc)
+    edge_bc = shape((micros, 8, 2 * NS), f32)
+    gbc, bhead, btail, g_rate = call(
+        skip_grid(bc_back_kernel), "bc_back", (micros, 1),
+        [(gbc, bc_block), (bcin, bc_block), (bchalo, bc_halo), (conv_bc, bc_taps), (q, sums), (dx, sums), (xu, sums),
+         (step, sums), (rate_in, sums), (bias, head_line), (rate, head_line), (mask, one_col)],
+        [(shape((micros, tokens, 2 * NS), bf16), bc_block), (edge_bc, bc_edge), (edge_bc, bc_edge),
+         (shape((micros, tokens, 128), bf16), sums)],
+        [], tokens * tokens * 128 * 6, tokens * 2 * NS * 8,
+    )
+    head = jnp.concatenate([head, bhead], 2)
+    goes = lax.ppermute(jnp.sum(jnp.where(enters, head, 0), axis=0), "mp", backward_edge)
+    back = jnp.pad(jnp.where(enters, 0, head)[1:], ((0, 1), (0, 0), (0, 0))) + jnp.where(leaves, goes[None], 0)
+    tail = jnp.concatenate([tail, btail], 2).at[:, 8 - (KC - 1) :].add(back[:, 8 - (KC - 1) :]).astype(bf16)
+    gx = lax.dynamic_update_slice_in_dim(gx, tail[..., :chan], tokens - 8, 1)
+    gbc = lax.dynamic_update_slice_in_dim(gbc, tail[..., chan:], tokens - 8, 1)
+    tail = jnp.concatenate([lax.dynamic_slice_in_dim(gbc, core * NS, NS, 2), g_rate], 2)
+    wide_cols = D // nz
+    g_low, g_up_z, g_up_x, g_down, out_last = call(
+        unproject_kernel, "unproject", (1, nz),
+        [(gz, every(chan)), (gx, every(chan)), (tail, every(NS + 128)),
+         (zx_weight, block((2, wide_cols, chan), lambda m, g: (0, g, 0))), (tail_weight, block((wide_cols, NS + 128), lambda m, g: (g, 0))),
+         (u_in, block((micros, 2 * R, 2 * chan), lambda m, g: (0, 0, 0))), (a_in, block((micros, 2 * R, wide_cols), by_step)),
+         (lr, every(2 * R)), (low, every(wide_cols, by_step))],
+        [(shape((micros, tokens, D), f32), every(wide_cols, by_step)), (shape((micros, R, chan), f32), block((micros, R, part), by_step)),
+         (shape((micros, R, chan), f32), block((micros, R, part), by_step)),
+         (shape((micros, R, D), f32), block((micros, R, wide_cols), by_step))],
+        rank_scratch, 12 * tokens * D * chan, act_bytes * 9, 6, (out_rows[-1:], shape((micros, seg, feats), bf16), last_slots, False),
+    )
+    gn = reduce_rows(g_low) * norm_gain
+    delta = inv_rms * gn - x_rows * (inv_rms**3 * jnp.mean(gn * x_rows, axis=-1, keepdims=True))
+    held_runs = jnp.arange(micros)[:, None] * nz + 2 * core + jnp.arange(2)
+    in_last = place_of(held_runs)[1] == micros - 1
+    in_last = jnp.repeat(in_last, tokens, axis=1)[..., None]
+    out = jnp.where(in_last, out_last, out_first)[:, None]
+    mine = (sequence == jnp.arange(micros)[:, None]).astype(f32)
+
+    def by_sequence(v):
+        return jnp.sum(mine.reshape(mine.shape + (1,) * (v.ndim - 1)) * v[None], axis=1)
+
+    near = jnp.stack([by_sequence(g).reshape(micros, R, nz, part) for g in (g_out, g_up_z, g_up_x)])
+    near = jnp.transpose(near, (3, 1, 0, 2, 4)).astype(bf16)
+    far = jnp.stack([by_sequence(g).reshape(micros, R, nd, 2, nz, each) for g in (g_up_out, g_down)])
+    far = jnp.transpose(far, (4, 5, 1, 0, 3, 2, 6)).astype(bf16).reshape(2 * nz, micros, 2, nd, R, each)
+    delta, near, far = finish(near, far, picks, delta.astype(bf16), shape((micros, seg, feats), bf16), nz)
+    grad = cotangent.astype(f32) + delta[:, None].astype(f32)
+    g_out_down = jnp.transpose(near[:, 0], (0, 2, 1)).reshape(2 * part, R)
+    g_in_up = jnp.transpose(near[:, 1:], (2, 1, 0, 3)).reshape(R, 2, 2 * part)
+    g_out_up = far[:, 0].reshape(ADAPT * R, each)
+    g_in_down = jnp.transpose(far[:, 1], (0, 2, 1))
+    return (out, grad, g_in_down, g_in_up, g_out_down, g_out_up)
+
+
 def solution(mesh):
     in_specs = (
         P(None, "dp", "seq", "mp"),
@@ -355,4 +1666,10 @@
         P("mp", ("dp", "seq")),
         P(None, ("dp", "seq", "mp")),
     )
-    return jax.shard_map(body, mesh=mesh, in_specs=in_specs, out_specs=out_specs, check_vma=False)
+    sizes = dict(mesh.shape)
+    by_chip = (
+        sizes["seq"] == 2
+        and sizes["dp"] * 2 == ADAPT
+        and sizes["mp"] == SLOTS + 1
+    )
+    return jax.shard_map(fast_body if by_chip else body, mesh=mesh, in_specs=in_specs, out_specs=out_specs, check_vma=False)

time: 4640 us -> 1070 us (0.23)
  waiting for transfers between devices: 1300 us -> 17.4 us
  local copies, waits for them, and re-layouts: 1270 us -> 123 us
  matrix products: 883 us -> 0 us
  Pallas kernels: 0 us -> 810 us
  blocking collectives: 528 us -> 0 us
  other arithmetic: 566 us -> 67.8 us
    dot_general x222 -> x0, matrix products: 883 us -> none  [the longest x36 234 us: block_step(): inner_out = jnp.einsum('tsh,shp->thp', mixing, x_part, precision=precise)]
    psum x1 -> x0, waiting for transfers between devices: 832 us -> none  [body(): normed_sum, bc_sum = lax.psum((normed_part, bc_partial), 'mp')]
    pallas_call x0 -> x11, Pallas kernels: none -> 810 us  [the longest x9 488 us: call(): pl.pallas_call(kernel, name=name, grid=grid, in_specs=[s for _, s in ins]...]
    dynamic_update_slice x180 -> x2, local copies, waits for them, and re-layouts: 699 us -> 1.3 us  [the longest x1 0.69 us: fast_body(): gx = lax.dynamic_update_slice_in_dim(gx, tail[..., :chan], tokens - 8, 1)]
    all_gather x5 -> x0, blocking collectives: 309 us -> none  [the longest x1 206 us: body(): lax.all_gather(in_down, ('dp', 'seq', 'mp'), axis=1, tiled=True)]
    reduce_scatter x4 -> x0, waiting for transfers between devices: 216 us -> none  [the longest x3 207 us: body(): lax.psum_scatter(partial_out, 'mp', scatter_dimension=2, tiled=True)]
    psum x2 -> x0, blocking collectives: 215 us -> none  [the longest x1 202 us: body(): normed_sum, bc_sum = lax.psum((normed_part, bc_partial), 'mp')]
    another operation x249 -> x17, local copies, waits for them, and re-layouts: 218 us -> 21.3 us  [the longest x6 10.2 us: fast_body(): jnp.stack([by_sequence(g).reshape(micros, R, nz, part) for g in (g_out, g...]
  transfers between devices with their start and end apart: 29 -> 11, of which waited for: 9 -> 5; matrix products, arithmetic and copies ran while one was open for 40% -> 12% of each run, Pallas kernels for 0% -> 37%
where the time goes in v3:
time: 1070 us; the launch traced here: 1050 us
  Pallas kernels  810 us (76%)
  local copies, waits for them, and re-layouts  123 us (11%)
  other arithmetic  67.8 us (6%)
  between operations  26.9 us (3%)
  waiting for transfers between devices  17.4 us (2%)
    pallas_call x9, Pallas kernels, call(): pl.pallas_call(kernel, name=name, grid=grid, in_specs=[s for _, s in ins]...  488 us
    pallas_call x1, Pallas kernels, gather(): pl.pallas_call(functools.partial(gather_kernel, nd, nz), name='gather', o...  217 us
    pallas_call x1, Pallas kernels, finish(): pl.pallas_call(functools.partial(finish_kernel, count), name='finish', in...  106 us
  transfers between devices with their start and end apart: 11, of which 5 were waited for; matrix products, arithmetic and copies ran while one was open for 12% of the time, Pallas kernels for 37%

profile of v3, /device:TPU:9, one launch (start us, length us, event | category | flops | bytes accessed | tf_op | source)
XLA Modules:
  0.0 1054.9 jit_solution(16434130334987233645)
XLA Ops:
  21.5 216.9 %gather.11 = (bf16[2,2048,2048]{2,1,0:T(8,128)(2,1)}, bf16[3,256,2048]{2,1,0:T(8,128)(2,1)}) custom-call(bf16[2,256,1024]{2,1,0:T(8,128)(2,1)} %bitcast.134, bf16[3,1024,512]{2,1,0:T(8,128)(2,1)} %bitcast.135), custom_call_target="tpu_custom_call" | custom-call | tf_op jit(solution)/shard_map/gather/pallas_call | solution.py:1264
  293.8 5.1 dynamic-slice_bitcast_fusion.2
  327.8 70.1 %project.1 = (bf16[3,512,2048]{2,1,0:T(8,128)(2,1)}, f32[3,512,2048]{2,1,0:T(8,128)}, bf16[3,512,256]{2,1,0:T(8,128)(2,1)}, f32[3,512,128]{2,1,0:T(8,128)}, bf16...) custom-call(bf16[3,256,2048]{2,1,0:T(8,128)(2,1)} %fusion.2.refs_0_, ...), custom_call_target="tpu_custom_call" | custom-call | flops 8589934592 | bytes 16777216 | tf_op jit(solution)/shard_map/project/pallas_call | solution.py:1299
  399.7 3.5 collective-permute-start.1
  406.2 5.4 prep.1
  411.7 99.7 %ssd_forward.1 = (f32[3,512,2048]{2,1,0:T(8,128)}, f32[3,512,128]{2,1,0:T(8,128)}, f32[3,128,2048]{2,1,0:T(8,128)}, f32[3,128,2048]{2,1,0:T(8,128)}, bf16[2,256,2048]{2,1,0:T(8,128)(2,1)}) custom-call(bf16[3,512,2048]{2,1,0:T(8,128)(2,1)} %get-tuple-element.72.refs_0_.refs_1_, bf16[3,16,2048]{2,1,0:T(8,128)(2,1)} %slice.167.refs_1_.refs_2_, ...), custom_call_target="tpu_custom_call" | custom-call | flops 3221225472 | bytes 12582912 | tf_op jit(solution)/shard_map/ssd_forward/pallas_call | solution.py:1299
  512.9 3.9 maximum_multiply_fusion.own_ref
  516.8 32.1 %gs.1 = (f32[3,512,2048]{2,1,0:T(8,128)}, f32[3,512,128]{2,1,0:T(8,128)}, bf16[3,512,32]{2,1,0:T(8,128)(2,1)}, bf16[3,512,2048]{2,1,0:T(8,128)(2,1)}) custom-call(bf16[3,256,2048]{2,1,0:T(8,128)(2,1)} %maximum_multiply_fusion.own_ref, bf16[4,4,512,512]{3,2,1,0:T(8,128)(2,1)} %bitcast.167, bf16[3,32,2048]{2,1,0:T(8,128)(2,1)} %get-tuple-element.181.up_ref, ...), custom_call_target="tpu_custom_call" | custom-call | flops 12884901888 | bytes 62914560 | tf_op jit(solution)/shard_map/gs/pallas_call | solution.py:1299
  557.8 40.8 %gate_back.1 = (f32[3,512,2048]{2,1,0:T(8,128)}, bf16[3,512,2048]{2,1,0:T(8,128)(2,1)}, bf16[3,512,2048]{2,1,0:T(8,128)(2,1)}, f32[3,128,2048]{2,1,0:T(8,128)}, f32[3,512,128]{2,1,0:T(8,128)}) custom-call(f32[3,512,2048]{2,1,0:T(8,128)} %get-tuple-element.83.gs_ref, f32[3,512,2048]{2,1,0:T(8,128)} %get-tuple-element.82.mixed_ref, ...), custom_call_target="tpu_custom_call" | custom-call | flops 805306368 | bytes 20971520 | tf_op jit(solution)/shard_map/gate_back/pallas_call | solution.py:1299
  598.6 25.0 %branch.1 = (f32[3,512,2048]{2,1,0:T(8,128)}, f32[3,16,2048]{2,1,0:T(8,128)}, f32[3,16,2048]{2,1,0:T(8,128)}) custom-call(bf16[3,512,2048]{2,1,0:T(8,128)(2,1)} %get-tuple-element.91.scaled_ref, bf16[4,4,512,512]{3,2,1,0:T(8,128)(2,1)} %bitcast.168, bf16[3,32,2048]{2,1,0:T(8,128)(2,1)} %copy-done.19, bf16[3,32,2048]{2,1,0:T(8,128)(2,1)} %get-tuple-element.181.up_ref, ...), custom_call_target="tpu_custom_call" | custom-call | flops 12884901888 | bytes 50331648 | tf_op jit(solution)/shard_map/branch/pallas_call | solution.py:1299
  623.6 6.3 constant_dynamic-slice_fusion.3
  630.0 10.3 collective-permute-done.4
  640.3 8.3 fusion.3.refs_12_
  648.7 160.1 %ssd_back.1 = (bf16[3,512,2048]{2,1,0:T(8,128)(2,1)}, f32[3,8,2048]{2,1,0:T(8,128)}, f32[3,8,2048]{2,1,0:T(8,128)}, f32[3,512,256]{2,1,0:T(8,128)}, f32[3,512,12...) custom-call(f32[3,512,2048]{2,1,0:T(8,128)} %get-tuple-element.87.refs_0_, ...), custom_call_target="tpu_custom_call" | custom-call | flops 6442450944 | bytes 12582912 | tf_op jit(solution)/shard_map/ssd_back/pallas_call | solution.py:1299
  818.0 7.5 bc_back.1
  829.0 3.1 collective-permute-done.6
  837.3 47.0 %unproject.1 = (f32[3,512,2048]{2,1,0:T(8,128)}, f32[3,16,2048]{2,1,0:T(8,128)}, f32[3,16,2048]{2,1,0:T(8,128)}, f32[3,16,2048]{2,1,0:T(8,128)}, bf16[3,1024,512]{2,1,0:T(8,128)(2,1)}) custom-call(bf16[3,512,2048]{2,1,0:T(8,128)(2,1)} %get-tuple-element.86.refs_0_, bf16[3,512,2048]{2,1,0:T(8,128)(2,1)} %slice_dynamic-update-slice_fusion.refs_1_, ...), custom_call_target="tpu_custom_call" | custom-call | flops 25769803776 | bytes 37748736 | tf_op jit(solution)/shard_map/unproject/pallas_call | solution.py:1299
  884.3 6.3 constant_dynamic-slice_fusion
  892.7 3.1 multiply_reduce_fusion.1
  915.9 4.3 select_bitcast_fusion
  920.2 4.2 fusion.4
  924.5 4.9 fusion.6.rows_ref
  929.3 105.8 %finish.1 = (bf16[3,1024,512]{2,1,0:T(8,128)(2,1)}, f32[2,3,16,512]{3,2,1,0:T(8,128)}, f32[8,2,16,64]{3,2,1,0:T(8,128)}) custom-call(bf16[4,3,3,16,512]{4,3,2,1,0:T(8,128)(2,1)} %maximum_bitcast_fusion.2.near_ref, bf16[8,3,2,4,16,64]{5,4,3,2,1,0:T(8,128)(2,1)} %bitcast.136, f32[3,8]{1,0:T(4,128)} %fusion.23.picks_ref, bf16[3,256,2048]{2,1,0:T(8,128)(2,1)} %fusion.6.rows_ref), custom_call_target="tpu_custom_call" | custom-call | tf_op jit(solution)/shard_map/finish/pallas_call | solution.py:1325
  1040.7 6.5 fusion.7
  (251 shorter events, 147.8 us)
Async XLA Ops:
  8.0 12.2 %copy-start.13 = (bf16[256,2,1024]{2,1,0:T(2,128)(2,1)S(1)}, bf16[256,2,1024]{2,1,0:T(2,128)(2,1)}, u32[]{:S(2)}) copy-start(bf16[256,2,1024]{2,1,0:T(2,128)(2,1)} %param.28) | copy-start | bytes 3145732
  8.0 253.8 %all-reduce.8.cloned.1.call-start = ((), (), s32[]{:S(2)}) async-start(), calls=%async_computation.2 | async-start | bytes 172032
  13.4 5.8 collective-permute-start
  18.7 248.2 %all-gather.4.cloned.1.call-start = ((), (), s32[]{:S(2)}) async-start(), calls=%async_computation | async-start | bytes 4038656 | tf_op jit(solution)/shard_map/all_gather | solution.py:1388
  20.2 496.6 %all-gather.6.cloned.1.call-start = ((), (), s32[]{:S(2)}) async-start(), calls=%async_computation.1 | async-start | bytes 8912896 | tf_op jit(solution)/shard_map/all_gather | solution.py:1392
  21.5 222.5 %copy-start.3 = (s32[3,1]{0,1:T(1,128)S(1)}, s32[3,1]{0,1:T(1,128)}, u32[]{:S(2)}) copy-start(s32[3,1]{0,1:T(1,128)} %param.25) | copy-start | bytes 40
  21.5 223.2 %copy-start.2 = (s32[3,1]{0,1:T(1,128)S(1)}, s32[3,1]{0,1:T(1,128)}, u32[]{:S(2)}) copy-start(s32[3,1]{0,1:T(1,128)} %param.26) | copy-start | bytes 40
  238.4 19.1 %copy-start.4 = (bf16[3,256,2048]{2,1,0:T(8,128)(2,1)S(1)}, bf16[3,256,2048]{2,1,0:T(8,128)(2,1)}, u32[]{:S(2)}) copy-start(bf16[3,256,2048]{2,1,0:T(8,128)(2,1)} %get-tuple-element.69) | copy-start | bytes 9437188
  238.4 20.9 %copy-start.20 = (f32[2048]{0:T(1024)S(1)}, f32[2048]{0:T(1024)}, u32[]{:S(2)}) copy-start(f32[2048]{0:T(1024)} %param.27) | copy-start | bytes 24580
  239.7 3.3 collective-permute-start.2
  244.0 17.8 %copy-start.24 = (s32[3]{0:T(128)}, s32[3]{0:T(128)S(1)}, u32[]{:S(2)}) copy-start(s32[3]{0:T(128)S(1)} %get-tuple-element.173) | copy-start | bytes 40
  327.8 71.8 %copy-start.25 = (pred[3]{0:T(512)(128)(4,1)S(1)}, pred[3]{0:T(512)(128)(4,1)}, u32[]{:S(2)}) copy-start(pred[3]{0:T(512)(128)(4,1)} %iota_compare_fusion.2) | copy-start | bytes 13
  327.8 77.0 %copy-start.27 = (pred[3]{0:T(512)(128)(4,1)S(1)}, pred[3]{0:T(512)(128)(4,1)}, u32[]{:S(2)}) copy-start(pred[3]{0:T(512)(128)(4,1)} %iota_compare_fusion.3) | copy-start | bytes 13
  399.7 5.1 collective-permute-start.1
  403.3 108.1 %copy-start.19 = (bf16[3,32,2048]{2,1,0:T(8,128)(2,1)}, bf16[3,32,2048]{2,1,0:T(8,128)(2,1)S(1)}, u32[]{:S(2)}) copy-start(bf16[3,32,2048]{2,1,0:T(8,128)(2,1)S(1)} %constant_dynamic-update-slice_fusion.4.down_ref) | copy-start | bytes 1179652
  550.3 1.2 collective-permute-start.3
  623.6 16.8 %copy-start.23 = (f32[3,256]{1,0:T(4,128)S(1)}, f32[3,256]{1,0:T(4,128)}, u32[]{:S(2)}) copy-start(f32[3,256]{1,0:T(4,128)} %get-tuple-element.194) | copy-start | bytes 9220
  629.8 10.5 collective-permute-start.4
  648.7 160.7 %copy-start.28 = (pred[3]{0:T(512)(128)(4,1)S(1)}, pred[3]{0:T(512)(128)(4,1)}, u32[]{:S(2)}) copy-start(pred[3]{0:T(512)(128)(4,1)} %iota_compare_fusion.3) | copy-start | bytes 13
  808.7 6.6 collective-permute-start.5
  818.0 14.2 %copy-start.26 = (pred[3]{0:T(512)(128)(4,1)S(1)}, pred[3]{0:T(512)(128)(4,1)}, u32[]{:S(2)}) copy-start(pred[3]{0:T(512)(128)(4,1)} %iota_compare_fusion.2) | copy-start | bytes 13
  826.4 5.8 collective-permute-start.6
  890.7 29.5 %collective-permute-start.7 = (f32[3,256,2048]{2,1,0:T(8,128)}, f32[3,256,2048]{2,1,0:T(8,128)}, u32[]{:S(2)}, u32[]{:S(2)}) collective-permute-start(f32[3,256,2048]{2,1,0:T(8,128)} %constant_dynamic-slice_fusion), channel_id=1, source_target_pairs={{0,4},{4,0},{1,5},{5,1},{2,6},{6,2},{3,7},{7,3},{8,12},{12,8},{9,1... | collective-permute-start | bytes 18874376 | tf_op jit(solution)/shard_map/ppermute | solution.py:1360
  909.4 10.8 %copy-start.5 = (f32[3,512,2048]{2,1,0:T(8,128)S(1)}, f32[3,512,2048]{2,1,0:T(8,128)}, u32[]{:S(2)}) copy-start(f32[3,512,2048]{2,1,0:T(8,128)} %get-tuple-element.115) | copy-start | bytes 37748740
  (16 other events, 61.4 us)
Sparse Core Ops, SparseCore 0:
  18.9 73.6 all-reduce.7
Sparse Core Ops, SparseCore 1:
  22.5 122.0 all-gather.3
  244.0 135.2 all-gather.5

commit v4 on v3

--- a/solution.py
+++ b/solution.py
@@ -440,7 +440,7 @@
     def piece(self, n):
         src_ref, dst_ref, send_sem, recv_sem = self.refs
         if self.to_rows:
-            m, h, to_c = n // 4, n // 2 % 2, lax.rem(n + self.c, 2)
+            m, h, to_c = lax.rem(n // 4 + self.z, SLOTS), n // 2 % 2, lax.rem(n + self.c, 2)
             to_z, slot = place_of(m * self.count + 2 * self.c + h)
             own = src_ref.shape[1] // 4
             src = src_ref.at[m, pl.ds(pl.multiple_of((2 * h + to_c) * own, 16), own), :]
@@ -493,7 +493,7 @@
 
     def start_at(self, step, steps):
         for n in range(self.pieces):
-            @pl.when(step == n * steps * 7 // (8 * self.pieces))
+            @pl.when(step == n * steps // (2 * self.pieces))
             def _():
                 self.start(n)
 
@@ -652,6 +652,14 @@
     return v[:half] + v[half:]
 
 
+def twice(v):
+    return jnp.concatenate([v, v], axis=0)
+
+
+def pick_kernel(ids_ref, pack_ref, out_ref):
+    out_ref[0, 0] = pack_ref[0, 0, 0]
+
+
 def merge(ref):
     return ref[...].reshape(ref.shape[0] * ref.shape[1], ref.shape[2])
 
@@ -671,11 +679,11 @@
             tail = mm(low_ref[m], tailw_ref[...])
             bcin_ref[m] = tail[:, : 2 * NS].astype(jnp.bfloat16)
             rate_ref[m] = tail[:, 2 * NS :]
-            lr_ref[m] = twice_split(mm_t(low_ref[m], down_ref[m]))
+            lr_ref[m] = twice_split(mm_t(low_ref[m], twice(down_ref[0, m])))
 
     value = mm(merge(low_ref), w_ref[0])
     for m in range(slots):
-        part = value[m * tokens : (m + 1) * tokens] + mm(lr_ref[m], up_ref[m])
+        part = value[m * tokens : (m + 1) * tokens] + mm(lr_ref[m], twice(up_ref[m, 0]))
 
         @pl.when(step < grid[1] // 2)
         def _():
@@ -804,7 +812,7 @@
     @pl.when(step == 0)
     def _():
         for m in range(slots):
-            rg_ref[m] = twice_split(mm_t(gb_ref[m], up_ref[m]))
+            rg_ref[m] = twice_split(mm_t(gb_ref[m], twice(up_ref[0, m])))
 
     gb = merge(gb_ref)
     width = w_ref.shape[3]
@@ -812,7 +820,7 @@
     for n in range(1, w_ref.shape[0]):
         total = total + mm_t(gb[:, n * width : (n + 1) * width], w_ref[n, 0])
     for m in range(slots):
-        gs = total[m * tokens : (m + 1) * tokens] + mm(rg_ref[m], down_ref[m])
+        gs = total[m * tokens : (m + 1) * tokens] + mm(rg_ref[m], twice(down_ref[m, 0]))
         gs_ref[m] = gs
         z = z_ref[m]
         dots = lane_sum(gs * gain_ref[...] * (mixed_ref[m] * (z * jax.nn.sigmoid(z))))
@@ -830,6 +838,15 @@
 
 def turned(v):
     return v.astype(jnp.float32).T.astype(jnp.bfloat16)
+
+
+def rank_sum(rows_ref, m, factor_ref, first):
+    width = factor_ref.shape[3]
+    total = 0.0
+    for n in range(factor_ref.shape[1]):
+        factor = twice(factor_ref[m, n, first : first + R])
+        total = total + mm_t(rows_ref[m, :, n * width : (n + 1) * width], factor)
+    return total
 
 
 def branch_kernel(
@@ -842,7 +859,7 @@
     @pl.when(step == 0)
     def _():
         for m in range(slots):
-            ro = twice_split(mm_t(scaled_ref[m], down_ref[m]))
+            ro = twice_split(rank_sum(scaled_ref, m, down_ref, 0))
             ro_ref[m] = ro
             rot_ref[m] = turned(ro)
             rgt_ref[m] = turned(rg_ref[m])
@@ -854,7 +871,7 @@
         total = total + mm(scaled[:, n * width : (n + 1) * width], w_ref[0, n])
     cols = g_down_ref.shape[2]
     for m in range(slots):
-        branch_ref[m] = total[m * tokens : (m + 1) * tokens] + mm(ro_ref[m], up_ref[m])
+        branch_ref[m] = total[m * tokens : (m + 1) * tokens] + mm(ro_ref[m], twice(up_ref[0, m]))
         g_up_ref[m] = fold(mm(rot_ref[m], gb_ref[m]))
         g_down_ref[m] = fold(mm(rgt_ref[m], scaled_ref[m, :, pl.ds(pl.multiple_of(step * cols, 128), cols)]))
     end(grid, mover)
@@ -866,12 +883,12 @@
 ):
     step = pl.program_id(1)
     begin(grid, mover)
-    slots, tokens, chan = gz_ref.shape
+    slots, tokens = gz_ref.shape[:2]
 
     @pl.when(step == 0)
     def _():
         for m in range(slots):
-            ri = twice_split(mm_t(gz_ref[m], up_ref[m, :, :chan]) + mm_t(gx_ref[m], up_ref[m, :, chan:]))
+            ri = twice_split(rank_sum(gz_ref, m, up_ref, 0) + rank_sum(gx_ref, m, up_ref, R))
             ri_ref[m] = ri
             rit_ref[m] = turned(ri)
             lrt_ref[m] = turned(lr_ref[m])
@@ -880,7 +897,7 @@
     cols = upz_ref.shape[2]
     at = pl.ds(pl.multiple_of(step * cols, 128), cols)
     for m in range(slots):
-        g_ref[m] = total[m * tokens : (m + 1) * tokens] + mm(ri_ref[m], down_ref[m])
+        g_ref[m] = total[m * tokens : (m + 1) * tokens] + mm(ri_ref[m], twice(down_ref[0, m]))
         upz_ref[m] = fold(mm(lrt_ref[m], gz_ref[m, :, at]))
         upx_ref[m] = fold(mm(lrt_ref[m], gx_ref[m, :, at]))
         g_down_ref[m] = fold(mm(rit_ref[m], low_ref[m]))
@@ -1039,7 +1056,8 @@
 
 
 def finish_kernel(
-    count, near_ref, far_ref, picks_ref, rows_ref, moved_ref, near_out_ref, far_out_ref, near1_ref, far1_ref, near2_ref,
+    count, out_ref, up_z_ref, up_x_ref, up_out_ref, down_ref, mine_ref, picks_ref, rows_ref, moved_ref, near_out_ref, far_out_ref,
+    near_ref, far_ref, near1_ref, far1_ref, near2_ref,
     near2_in_ref, far2_ref, far2_in_ref, n1s, n1r, f1s, f1r, n2s, n2r, f2s, f2r, send_sem, recv_sem
 ):
     d, c, z = lax.axis_index("dp"), lax.axis_index("seq"), lax.axis_index("mp")
@@ -1051,6 +1069,22 @@
     for i, j in others:
         device = (lax.rem(d + i, blocks), lax.rem(c + j, 2), z)
         pl.semaphore_signal(barrier, 1, device_id=device, device_id_type=MESH)
+
+    def by_sequence(ref, m):
+        return sum(mine_ref[m, i] * ref[i] for i in range(SLOTS))
+
+    part, each = near_ref.shape[4], far_ref.shape[5]
+    for m in range(SLOTS):
+        for kind, ref in enumerate((out_ref, up_z_ref, up_x_ref)):
+            total = by_sequence(ref, m).astype(jnp.bfloat16)
+            for n in range(count):
+                near_ref[n, m, kind] = total[:, n * part : (n + 1) * part]
+        for kind, ref in enumerate((up_out_ref, down_ref)):
+            total = by_sequence(ref, m)
+            for b in range(blocks):
+                for n in range(2 * count):
+                    at = (b * 2 * count + n) * each
+                    far_ref[n, m, kind, b] = total[:, at : at + each].astype(jnp.bfloat16)
     pl.semaphore_wait(barrier, waits + len(others))
 
     def remote(src, dst, send, recv, *device):
@@ -1317,25 +1351,29 @@
     return lax.optimization_barrier((value,) + deps)[0]
 
 
-def finish(near, far, picks, rows, moved, count):
-    dma, f32 = pltpu.SemaphoreType.DMA, jnp.float32
+def finish(grads, mine, picks, rows, moved, count, blocks):
+    dma, f32, bf16 = pltpu.SemaphoreType.DMA, jnp.float32, jnp.bfloat16
     anywhere, vmem = pl.BlockSpec(memory_space=pl.ANY), pl.BlockSpec(memory_space=pltpu.VMEM)
-    blocks = far.shape[3]
-    near_shape, far_shape = near.shape[2:], far.shape[2:3] + far.shape[4:]
+    smem = pl.BlockSpec(memory_space=pltpu.SMEM)
+    near_shape = (3, R, grads[0].shape[2] // count)
+    far_shape = (2, R, D // (2 * blocks * count))
+    near_all = (count, SLOTS) + near_shape
+    far_all = (2 * count, SLOTS, 2, blocks) + far_shape[1:]
     return pl.pallas_call(
         functools.partial(finish_kernel, count),
         name="finish",
-        in_specs=[vmem, vmem, pl.BlockSpec(memory_space=pltpu.SMEM), anywhere],
+        in_specs=[vmem] * 5 + [smem, smem, anywhere],
         out_specs=[anywhere, vmem, vmem],
         out_shape=[moved, jax.ShapeDtypeStruct((2,) + near_shape, f32), jax.ShapeDtypeStruct((ADAPT,) + far_shape, f32)],
         scratch_shapes=[
-            pltpu.VMEM(near.shape, near.dtype), pltpu.VMEM(far.shape, far.dtype), pltpu.VMEM((ADAPT,) + near_shape, f32),
-            pltpu.VMEM((2 * blocks,) + near_shape, f32), pltpu.VMEM((blocks, ADAPT) + far_shape, f32),
-            pltpu.VMEM((blocks, ADAPT) + far_shape, f32), dma((count,)), dma((count,)), dma((2 * count,)), dma((2 * count,)),
-            dma((2 * blocks,)), dma((2 * blocks,)), dma((blocks,)), dma((blocks,)), dma((count * SLOTS,)), dma((SLOTS, 4)),
+            pltpu.VMEM(near_all, bf16), pltpu.VMEM(far_all, bf16), pltpu.VMEM(near_all, bf16), pltpu.VMEM(far_all, bf16),
+            pltpu.VMEM((ADAPT,) + near_shape, f32), pltpu.VMEM((2 * blocks,) + near_shape, f32),
+            pltpu.VMEM((blocks, ADAPT) + far_shape, f32), pltpu.VMEM((blocks, ADAPT) + far_shape, f32), dma((count,)), dma((count,)),
+            dma((2 * count,)), dma((2 * count,)), dma((2 * blocks,)), dma((2 * blocks,)), dma((blocks,)), dma((blocks,)),
+            dma((count * SLOTS,)), dma((SLOTS, 4)),
         ],
         compiler_params=pltpu.CompilerParams(vmem_limit_bytes=VMEM_LIMIT, collective_id=5, has_side_effects=True),
-    )(near, far, picks, rows)
+    )(*grads, mine, picks, rows)
 
 
 def fast_body(
@@ -1371,11 +1409,11 @@
             lax.dynamic_index_in_dim(v, 1 - core, axis, False),
         )
 
-    line = 2 * part
+    line = part
     bc_piece = lax.dynamic_slice_in_dim(w_bc, z * (w_bc.shape[0] // nz), w_bc.shape[0] // nz, 0)
     pairs = jnp.stack([jnp.transpose(in_down, (0, 2, 1)), out_up.reshape(ADAPT, R, -1)], 1)
     same = [bc_piece, pairs]
-    sized = [halves(in_up, 2), halves(out_down.T, 1), halves(w_dt.T, 0)]
+    sized = [halves(jnp.transpose(in_up, (1, 0, 2)), 2), halves(out_down.T, 1), halves(w_dt.T, 0)]
     packs = []
     for k in range(2):
         packs.append(jnp.concatenate([v.reshape(-1, line) for v in [s[k] for s in sized] + same], 0))
@@ -1465,20 +1503,25 @@
     mask_own = (own_pos < lengths).astype(f32)[..., None]
     mask = (all_pos < lengths).astype(f32)[..., None]
     picks = (adapter_ids == jnp.arange(ADAPT)).astype(f32)
-    near, wide_rows = [], []
-    for m in range(micros):
-        got = lax.dynamic_index_in_dim(pack, ids[m] // 2, 0, False)[:, :, : bounds[2]]
-        near.append(lax.dynamic_index_in_dim(got, ids[m] % 2, 1, False))
-        wide_rows.append(lax.dynamic_slice_in_dim(pack, bounds[4] + 2 * ids[m], 2, 3))
-    near = jnp.stack(near)
-    u_in = near[:, :, : bounds[1]].reshape(micros, nz, R, 2, part)
-    u_in = jnp.transpose(u_in, (0, 2, 3, 1, 4)).reshape(micros, R, 2 * chan)
-    a_out = near[:, :, bounds[1] :].reshape(micros, nz, R, part)
-    a_out = jnp.transpose(a_out, (0, 2, 1, 3)).reshape(micros, R, chan)
+    tall = bounds[2]
+    factors = pl.pallas_call(
+        pick_kernel,
+        name="pick",
+        grid_spec=pltpu.PrefetchScalarGridSpec(
+            num_scalar_prefetch=1,
+            grid=(micros, nz),
+            in_specs=[block((1, 1, 1, tall, part), lambda m, n, k: (k[m] // 2, n, lax.rem(k[m], 2), 0, 0))],
+            out_specs=block((1, 1, tall, part), lambda m, n, k: (m, n, 0, 0)),
+        ),
+        out_shape=shape((micros, nz, tall, part), bf16),
+    )(ids, pack)
+    per = 2 * R * each // line
+    wide_rows = [lax.dynamic_slice_in_dim(pack, bounds[4] + per * ids[m], per, 3) for m in range(micros)]
     wide_rows = jnp.stack(wide_rows).reshape(micros, nd, nz, 2, 2, R, each)
     wide_rows = jnp.transpose(wide_rows, (4, 0, 5, 1, 3, 2, 6)).reshape(2, micros, R, D)
-    u_in, a_out = [jnp.concatenate([v, v], 1) for v in (u_in, a_out)]
-    a_in, u_out = jnp.concatenate([wide_rows, wide_rows], 2)
+
+    def wide_block(kind, width, index):
+        return block((1, micros, R, width), lambda m, g: (kind, 0, 0, index(g)))
 
     def every(width, index=None):
         if index is None:
@@ -1487,7 +1530,6 @@
 
     by_step = lambda m, g: (0, 0, g)
     rank_b16 = shape((micros, tokens, 2 * R), bf16)
-    all_down = block((micros, 2 * R, D), lambda m, g: (0, 0, 0))
     half_steps = chan // part
     steps = 2 * half_steps
     cot = cotangent[:, 0]
@@ -1497,8 +1539,8 @@
     xin, z_in, bcin, rate_in, lr, low, cot_early = call(
         project_kernel, "project", (1, steps),
         [(low_own, hbm), (zx_weight, block((1, D, part), lambda m, g: (1 - g // half_steps, 0, g % half_steps))),
-         (first_weight, block((D, 2 * NS + 128), z2)), (a_in, all_down),
-         (u_in, block((micros, 2 * R, part), lambda m, g: (0, 0, (g + half_steps) % steps)))],
+         (first_weight, block((D, 2 * NS + 128), z2)), (wide_rows, wide_block(0, D, lambda g: 0)),
+         (factors, block((micros, 1, R, part), lambda m, g: (0, g % half_steps, 1 - g // half_steps, 0)))],
         [(tok_b16, every(part, lambda m, g: (0, 0, jnp.minimum(g, half_steps - 1)))),
          (tok_f32, every(part, lambda m, g: (0, 0, jnp.maximum(g - half_steps, 0)))),
          (shape((micros, tokens, 2 * NS), bf16), every(2 * NS)), (sums_f32, every(128)), (rank_b16, every(2 * R)), (shape((micros, tokens, D), bf16), hbm)],
@@ -1535,8 +1577,8 @@
     part_block = every(part, by_step)
     gs, dots, rg, gb = call(
         gs_kernel, "gs", (1, nz),
-        [(gb_own, hbm), (out_all, block((nd, 1, part, cols), lambda m, g: (0, g, 0, 0))), (u_out, all_down),
-         (a_out, block((micros, 2 * R, part), by_step)), (mixed, part_block), (z_in, part_block),
+        [(gb_own, hbm), (out_all, block((nd, 1, part, cols), lambda m, g: (0, g, 0, 0))), (wide_rows, wide_block(1, D, lambda g: 0)),
+         (factors, block((micros, 1, R, part), lambda m, g: (0, g, 2, 0))), (mixed, part_block), (z_in, part_block),
          (gain, block((1, part), lambda m, g: (0, g)))],
         [(tok_f32, part_block), (sums_f32, every(128)), (rank_b16, every(2 * R)), (shape((micros, tokens, D), bf16), hbm)],
         pair_scratch, 6 * tokens * D * chan, act_bytes * 15, 7,
@@ -1558,7 +1600,7 @@
     partial, g_up_out, g_out = call(
         branch_kernel, "branch", (1, nd),
         [(scaled, every(chan)), (out_all, block((1,) + out_all.shape[1:], lambda m, g: (g, 0, 0, 0))),
-         (a_out, block((micros, 2 * R, chan), lambda m, g: (0, 0, 0))), (u_out, block((micros, 2 * R, cols), by_step)),
+         (factors, block((micros, nz, R, part), lambda m, g: (0, 0, 2, 0))), (wide_rows, wide_block(1, cols, lambda g: g)),
          (rg, every(2 * R)), (gb, step_cols)],
         [(shape((micros, tokens, D), f32), step_cols), (shape((micros, R, D), f32), rank_cols),
          (shape((micros, R, chan), f32), block((micros, R, chan // nd), by_step))],
@@ -1605,7 +1647,7 @@
         unproject_kernel, "unproject", (1, nz),
         [(gz, every(chan)), (gx, every(chan)), (tail, every(NS + 128)),
          (zx_weight, block((2, wide_cols, chan), lambda m, g: (0, g, 0))), (tail_weight, block((wide_cols, NS + 128), lambda m, g: (g, 0))),
-         (u_in, block((micros, 2 * R, 2 * chan), lambda m, g: (0, 0, 0))), (a_in, block((micros, 2 * R, wide_cols), by_step)),
+         (factors, block((micros, nz, 2 * R, part), lambda m, g: (0, 0, 0, 0))), (wide_rows, wide_block(0, wide_cols, lambda g: g)),
          (lr, every(2 * R)), (low, every(wide_cols, by_step))],
         [(shape((micros, tokens, D), f32), every(wide_cols, by_step)), (shape((micros, R, chan), f32), block((micros, R, part), by_step)),
          (shape((micros, R, chan), f32), block((micros, R, part), by_step)),
@@ -1620,14 +1662,9 @@
     out = jnp.where(in_last, out_last, out_first)[:, None]
     mine = (sequence == jnp.arange(micros)[:, None]).astype(f32)
 
-    def by_sequence(v):
-        return jnp.sum(mine.reshape(mine.shape + (1,) * (v.ndim - 1)) * v[None], axis=1)
-
-    near = jnp.stack([by_sequence(g).reshape(micros, R, nz, part) for g in (g_out, g_up_z, g_up_x)])
-    near = jnp.transpose(near, (3, 1, 0, 2, 4)).astype(bf16)
-    far = jnp.stack([by_sequence(g).reshape(micros, R, nd, 2, nz, each) for g in (g_up_out, g_down)])
-    far = jnp.transpose(far, (4, 5, 1, 0, 3, 2, 6)).astype(bf16).reshape(2 * nz, micros, 2, nd, R, each)
-    delta, near, far = finish(near, far, picks, delta.astype(bf16), shape((micros, seg, feats), bf16), nz)
+    delta, near, far = finish(
+        [g_out, g_up_z, g_up_x, g_up_out, g_down], mine, picks, delta.astype(bf16), shape((micros, seg, feats), bf16), nz, nd
+    )
     grad = cotangent.astype(f32) + delta[:, None].astype(f32)
     g_out_down = jnp.transpose(near[:, 0], (0, 2, 1)).reshape(2 * part, R)
     g_in_up = jnp.transpose(near[:, 1:], (2, 1, 0, 3)).reshape(R, 2, 2 * part)

time: 1070 us -> 1040 us (0.972)
  local copies, waits for them, and re-layouts: 123 us -> 85.4 us
  Pallas kernels: 810 us -> 836 us
    pallas_call x9, Pallas kernels: 488 us -> 507 us  [call(): pl.pallas_call(kernel, name=name, grid=grid, in_specs=[s for _, s in ins]...]
    another operation x9 -> x0, local copies, waits for them, and re-layouts: 14.6 us -> none  [the longest x6 10.2 us: fast_body(): jnp.stack([by_sequence(g).reshape(micros, R, nz, part) for g in (g_out, g...]
  transfers between devices with their start and end apart: 11 -> 11, of which waited for: 5 -> 6; matrix products, arithmetic and copies ran while one was open for 12% -> 8% of each run, Pallas kernels for 37% -> 39%
where the time goes in v4:
time: 1040 us; the launch traced here: 1030 us
  Pallas kernels  836 us (80%)
  local copies, waits for them, and re-layouts  85.4 us (8%)
  other arithmetic  58.6 us (6%)
  waiting for transfers between devices  21.3 us (2%)
  between operations  19.2 us (2%)
    pallas_call x9, Pallas kernels, call(): pl.pallas_call(kernel, name=name, grid=grid, in_specs=[s for _, s in ins]...  507 us
    pallas_call x1, Pallas kernels, gather(): pl.pallas_call(functools.partial(gather_kernel, nd, nz), name='gather', o...  217 us
    pallas_call x1, Pallas kernels, finish(): pl.pallas_call(functools.partial(finish_kernel, count), name='finish', in...  105 us
  transfers between devices with their start and end apart: 11, of which 6 were waited for; matrix products, arithmetic and copies ran while one was open for 8% of the time, Pallas kernels for 39%

profile of v4, /device:TPU:9, one launch (start us, length us, event | category | flops | bytes accessed | tf_op | source)
XLA Modules:
  0.0 1030.7 jit_solution(7073091597473652154)
XLA Ops:
  22.3 216.6 %gather.11 = (bf16[2,2048,2048]{2,1,0:T(8,128)(2,1)}, bf16[3,256,2048]{2,1,0:T(8,128)(2,1)}) custom-call(bf16[2,256,1024]{2,1,0:T(8,128)(2,1)} %bitcast.118, bf16[3,1024,512]{2,1,0:T(8,128)(2,1)} %bitcast.119), custom_call_target="tpu_custom_call" | custom-call | tf_op jit(solution)/shard_map/gather/pallas_call | solution.py:1298
  260.7 4.8 copy.112
  265.5 7.4 pick.1.refs_4_.down_ref.refs_5_
  301.5 93.7 %project.1 = (bf16[3,512,2048]{2,1,0:T(8,128)(2,1)}, f32[3,512,2048]{2,1,0:T(8,128)}, bf16[3,512,256]{2,1,0:T(8,128)(2,1)}, f32[3,512,128]{2,1,0:T(8,128)}, bf16...) custom-call(bf16[3,256,2048]{2,1,0:T(8,128)(2,1)} %fusion.2.refs_0_, ...), custom_call_target="tpu_custom_call" | custom-call | flops 8589934592 | bytes 16777216 | tf_op jit(solution)/shard_map/project/pallas_call | solution.py:1333
  403.5 5.7 prep.1
  409.2 80.5 %ssd_forward.1 = (f32[3,512,2048]{2,1,0:T(8,128)}, f32[3,512,128]{2,1,0:T(8,128)}, f32[3,128,2048]{2,1,0:T(8,128)}, f32[3,128,2048]{2,1,0:T(8,128)}, bf16[2,256,2048]{2,1,0:T(8,128)(2,1)}) custom-call(bf16[3,512,2048]{2,1,0:T(8,128)(2,1)} %get-tuple-element.72.refs_0_.refs_1_, bf16[3,16,2048]{2,1,0:T(8,128)(2,1)} %slice.137.refs_1_.refs_2_, ...), custom_call_target="tpu_custom_call" | custom-call | flops 3221225472 | bytes 12582912 | tf_op jit(solution)/shard_map/ssd_forward/pallas_call | solution.py:1333
  491.1 3.9 maximum_multiply_fusion.own_ref
  495.0 32.3 %gs.1 = (f32[3,512,2048]{2,1,0:T(8,128)}, f32[3,512,128]{2,1,0:T(8,128)}, bf16[3,512,32]{2,1,0:T(8,128)(2,1)}, bf16[3,512,2048]{2,1,0:T(8,128)(2,1)}) custom-call(bf16[3,256,2048]{2,1,0:T(8,128)(2,1)} %maximum_multiply_fusion.own_ref, bf16[4,4,512,512]{3,2,1,0:T(8,128)(2,1)} %bitcast.145, bf16[2,3,16,2048]{3,2,1,0:T(8,128)(2,1)} %reshape.539.refs_3_.up_ref.refs_6_, ...), custom_call_target="tpu_custom_call" | custom-call | flops 12884901888 | bytes 62914560 | tf_op jit(solution)/shard_map/gs/pallas_call | solution.py:1333
  536.4 40.8 %gate_back.1 = (f32[3,512,2048]{2,1,0:T(8,128)}, bf16[3,512,2048]{2,1,0:T(8,128)(2,1)}, bf16[3,512,2048]{2,1,0:T(8,128)(2,1)}, f32[3,128,2048]{2,1,0:T(8,128)}, f32[3,512,128]{2,1,0:T(8,128)}) custom-call(f32[3,512,2048]{2,1,0:T(8,128)} %get-tuple-element.83.gs_ref, f32[3,512,2048]{2,1,0:T(8,128)} %get-tuple-element.82.mixed_ref, ...), custom_call_target="tpu_custom_call" | custom-call | flops 805306368 | bytes 20971520 | tf_op jit(solution)/shard_map/gate_back/pallas_call | solution.py:1333
  577.2 24.8 %branch.1 = (f32[3,512,2048]{2,1,0:T(8,128)}, f32[3,16,2048]{2,1,0:T(8,128)}, f32[3,16,2048]{2,1,0:T(8,128)}) custom-call(bf16[3,512,2048]{2,1,0:T(8,128)(2,1)} %get-tuple-element.91.scaled_ref, bf16[4,4,512,512]{3,2,1,0:T(8,128)(2,1)} %bitcast.146, bf16[3,4,48,512]{3,2,1,0:T(8,128)(2,1)} %pick.1.refs_4_.down_ref.refs_5_, ...), custom_call_target="tpu_custom_call" | custom-call | flops 12884901888 | bytes 50331648 | tf_op jit(solution)/shard_map/branch/pallas_call | solution.py:1333
  602.0 6.3 constant_dynamic-slice_fusion.3
  608.6 10.2 collective-permute-done.4
  618.8 8.3 fusion.3.refs_12_
  627.1 173.9 %ssd_back.1 = (bf16[3,512,2048]{2,1,0:T(8,128)(2,1)}, f32[3,8,2048]{2,1,0:T(8,128)}, f32[3,8,2048]{2,1,0:T(8,128)}, f32[3,512,256]{2,1,0:T(8,128)}, f32[3,512,12...) custom-call(f32[3,512,2048]{2,1,0:T(8,128)} %get-tuple-element.87.refs_0_, ...), custom_call_target="tpu_custom_call" | custom-call | flops 6442450944 | bytes 12582912 | tf_op jit(solution)/shard_map/ssd_back/pallas_call | solution.py:1333
  812.0 7.4 bc_back.1
  820.4 3.5 collective-permute-start.6
  831.3 47.9 %unproject.1 = (f32[3,512,2048]{2,1,0:T(8,128)}, f32[3,16,2048]{2,1,0:T(8,128)}, f32[3,16,2048]{2,1,0:T(8,128)}, f32[3,16,2048]{2,1,0:T(8,128)}, bf16[3,1024,512]{2,1,0:T(8,128)(2,1)}) custom-call(bf16[3,512,2048]{2,1,0:T(8,128)(2,1)} %get-tuple-element.86.refs_0_, bf16[3,512,2048]{2,1,0:T(8,128)(2,1)} %slice_dynamic-update-slice_fusion.refs_1_, ...), custom_call_target="tpu_custom_call" | custom-call | flops 25769803776 | bytes 37748736 | tf_op jit(solution)/shard_map/unproject/pallas_call | solution.py:1333
  879.2 6.3 constant_dynamic-slice_fusion
  887.2 4.4 select_bitcast_fusion
  891.6 4.4 collective-permute-done.7
  896.0 5.7 fusion.4
  901.7 5.1 fusion.6.rows_ref
  906.8 104.9 %finish.1 = (bf16[3,1024,512]{2,1,0:T(8,128)(2,1)}, f32[2,3,16,512]{3,2,1,0:T(8,128)}, f32[8,2,16,64]{3,2,1,0:T(8,128)}) custom-call(f32[3,16,2048]{2,1,0:T(8,128)} %get-tuple-element.110.out_ref, f32[3,16,2048]{2,1,0:T(8,128)} %get-tuple-element.111.up_z_ref, f32[3,16,2048]{2,1,0:T(8,128)} %get-tuple-element.112.up_x_ref, ...), custom_call_target="tpu_custom_call" | custom-call | tf_op jit(solution)/shard_map/finish/pallas_call | solution.py:1362
  1017.3 5.5 fusion.7
  (189 shorter events, 107.2 us)
Async XLA Ops:
  8.0 236.5 %copy-start.3 = (s32[3,1]{0,1:T(1,128)S(1)}, s32[3,1]{0,1:T(1,128)}, u32[]{:S(2)}) copy-start(s32[3,1]{0,1:T(1,128)} %param.25) | copy-start | bytes 40
  8.0 247.5 %all-reduce.8.cloned.1.call-start = ((), (), s32[]{:S(2)}) async-start(), calls=%async_computation.2 | async-start | bytes 172032
  11.3 233.8 %copy-start.2 = (s32[3,1]{0,1:T(1,128)S(1)}, s32[3,1]{0,1:T(1,128)}, u32[]{:S(2)}) copy-start(s32[3,1]{0,1:T(1,128)} %param.26) | copy-start | bytes 40
  13.0 5.8 collective-permute-start
  18.3 242.4 %all-gather.4.cloned.1.call-start = ((), (), s32[]{:S(2)}) async-start(), calls=%async_computation | async-start | bytes 4038656 | tf_op jit(solution)/shard_map/all_gather | solution.py:1426
  19.7 475.2 %all-gather.6.cloned.1.call-start = ((), (), s32[]{:S(2)}) async-start(), calls=%async_computation.1 | async-start | bytes 8912896 | tf_op jit(solution)/shard_map/all_gather | solution.py:1430
  22.3 230.9 %copy-start.10 = (f32[2048]{0:T(1024)S(1)}, f32[2048]{0:T(1024)}, u32[]{:S(2)}) copy-start(f32[2048]{0:T(1024)} %param.27) | copy-start | bytes 24580
  238.9 14.2 %copy-start.4 = (bf16[3,256,2048]{2,1,0:T(8,128)(2,1)S(1)}, bf16[3,256,2048]{2,1,0:T(8,128)(2,1)}, u32[]{:S(2)}) copy-start(bf16[3,256,2048]{2,1,0:T(8,128)(2,1)} %get-tuple-element.69) | copy-start | bytes 9437188
  240.1 3.4 collective-permute-start.2
  245.8 19.7 %copy-start.11 = (s32[3]{0:T(128)}, s32[3]{0:T(128)S(1)}, u32[]{:S(2)}) copy-start(s32[3]{0:T(128)S(1)} %get-tuple-element.175.ids_ref) | copy-start | bytes 40
  301.5 95.4 %copy-start.12 = (pred[3]{0:T(512)(128)(4,1)S(1)}, pred[3]{0:T(512)(128)(4,1)}, u32[]{:S(2)}) copy-start(pred[3]{0:T(512)(128)(4,1)} %iota_compare_fusion.2) | copy-start | bytes 13
  301.5 100.6 %copy-start.13 = (pred[3]{0:T(512)(128)(4,1)S(1)}, pred[3]{0:T(512)(128)(4,1)}, u32[]{:S(2)}) copy-start(pred[3]{0:T(512)(128)(4,1)} %iota_compare_fusion.3) | copy-start | bytes 13
  397.0 5.1 collective-permute-start.1
  528.7 1.4 collective-permute-start.3
  608.3 10.5 %collective-permute-start.4 = (f32[3,256,2048]{2,1,0:T(8,128)}, f32[3,256,2048]{2,1,0:T(8,128)}, u32[]{:S(2)}, u32[]{:S(2)}) collective-permute-start(f32[3,256,2048]{2,1,0:T(8,128)} %constant_dynamic-slice_fusion.3), channel_id=1, source_target_pairs={{0,4},{4,0},{1,5},{5,1},{2,6},{6,2},{3,7},{7,3},{8,12},{12,8},{9,1... | collective-permute-start | bytes 18874376 | tf_op jit(solution)/shard_map/ppermute | solution.py:1398
  801.0 8.2 collective-permute-start.5
  801.7 7.6 copy-start.8
  820.4 5.8 collective-permute-start.6
  885.5 10.5 %collective-permute-start.7 = (f32[3,256,2048]{2,1,0:T(8,128)}, f32[3,256,2048]{2,1,0:T(8,128)}, u32[]{:S(2)}, u32[]{:S(2)}) collective-permute-start(f32[3,256,2048]{2,1,0:T(8,128)} %constant_dynamic-slice_fusion), channel_id=1, source_target_pairs={{0,4},{4,0},{1,5},{5,1},{2,6},{6,2},{3,7},{7,3},{8,12},{12,8},{9,1... | collective-permute-start | bytes 18874376 | tf_op jit(solution)/shard_map/ppermute | solution.py:1398
  887.1 14.5 %slice-start = ((s8[12582912]{0:T(1024)(128)(4,1)}), s8[4194304]{0:T(1024)(128)(4,1)S(1)}, s32[]{:S(2)}) async-start(s8[12582912]{0:T(1024)(128)(4,1)} %bitcast.109), calls=%async_computation.3 | async-start | bytes 8388608
  887.2 14.5 %slice-start.1 = ((s8[12582912]{0:T(1024)(128)(4,1)}), s8[4194304]{0:T(1024)(128)(4,1)S(1)}, s32[]{:S(2)}) async-start(s8[12582912]{0:T(1024)(128)(4,1)} %bitcast.109), calls=%async_computation.4 | async-start | bytes 8388608
  891.6 10.1 slice-start.2
  906.8 110.4 %copy-start.5 = (bf16[3,1,1024,512]{3,2,1,0:T(8,128)(2,1)S(1)}, bf16[3,1,1024,512]{3,2,1,0:T(8,128)(2,1)}, u32[]{:S(2)}) copy-start(bf16[3,1,1024,512]{3,2,1,0:T(8,128)(2,1)} %param.24) | copy-start | bytes 9437188
  1017.3 5.5 copy-start.1
  (4 other events, 4.4 us)
Sparse Core Ops, SparseCore 0:
  18.5 74.8 all-reduce.7
Sparse Core Ops, SparseCore 1:
  22.1 122.6 all-gather.3
  244.5 142.5 all-gather.5

commit v5 on v4

--- a/solution.py
+++ b/solution.py
@@ -602,6 +602,46 @@
     def finish(self):
         self.far.wait_send()
         self.keep.wait()
+
+
+class PairSum:
+    def __init__(self, part_ref, sum_ref, send_sem, recv_sem):
+        self.refs = part_ref, sum_ref, send_sem, recv_sem
+        self.d, self.c, self.z = lax.axis_index("dp"), lax.axis_index("seq"), lax.axis_index("mp")
+
+    def greet(self, barrier):
+        pl.semaphore_signal(barrier, 1, device_id=(self.d, 1 - self.c, self.z), device_id_type=MESH)
+        return 1
+
+    def rows(self, c):
+        own = self.refs[1].shape[2]
+        return pl.ds(pl.multiple_of(c * own, 16), own)
+
+    def copy(self, step):
+        part_ref, sum_ref, send_sem, recv_sem = self.refs
+        return pltpu.make_async_remote_copy(
+            src_ref=part_ref.at[lax.rem(step, 2), :, self.rows(1 - self.c), :], dst_ref=sum_ref.at[step],
+            send_sem=send_sem.at[step], recv_sem=recv_sem.at[step], device_id=(self.d, 1 - self.c, self.z), device_id_type=MESH,
+        )
+
+    def free(self, step):
+        @pl.when(step >= 2)
+        def _():
+            self.copy(step - 2).wait_send()
+
+    def send(self, step):
+        self.copy(step).start()
+
+    def take(self, step):
+        part_ref, sum_ref = self.refs[:2]
+        self.copy(step).wait_recv()
+        for m in range(sum_ref.shape[1]):
+            sum_ref[step, m] += part_ref[lax.rem(step, 2), m, self.rows(self.c), :]
+
+    def finish(self):
+        steps = self.refs[1].shape[0]
+        for step in (steps - 2, steps - 1):
+            self.copy(step).wait_send()
 
 
 def carried_by(kernel, count, first, to_rows, n_in, n_out, *refs):
@@ -850,10 +890,12 @@
 
 
 def branch_kernel(
-    grid, scaled_ref, w_ref, down_ref, up_ref, rg_ref, gb_ref, branch_ref, g_up_ref, g_down_ref, ro_ref, rot_ref, rgt_ref, mover=None
+    grid, scaled_ref, w_ref, down_ref, up_ref, rg_ref, gb_ref, x_ref, mask_ref, out_ref, g_up_ref, g_down_ref, ro_ref, rot_ref,
+    rgt_ref, part_ref, sum_ref, send_sem, recv_sem
 ):
     step = pl.program_id(1)
-    begin(grid, mover)
+    pair = PairSum(part_ref, sum_ref, send_sem, recv_sem)
+    begin(grid, pair)
     slots, tokens = scaled_ref.shape[:2]
 
     @pl.when(step == 0)
@@ -870,19 +912,39 @@
     for n in range(1, w_ref.shape[1]):
         total = total + mm(scaled[:, n * width : (n + 1) * width], w_ref[0, n])
     cols = g_down_ref.shape[2]
+    width = up_ref.shape[3]
+    pair.free(step)
     for m in range(slots):
-        branch_ref[m] = total[m * tokens : (m + 1) * tokens] + mm(ro_ref[m], twice(up_ref[0, m]))
+        part_ref[lax.rem(step, 2), m] = total[m * tokens : (m + 1) * tokens] + mm(ro_ref[m], twice(up_ref[0, m]))
+    pair.send(step)
+    for m in range(slots):
         g_up_ref[m] = fold(mm(rot_ref[m], gb_ref[m]))
         g_down_ref[m] = fold(mm(rgt_ref[m], scaled_ref[m, :, pl.ds(pl.multiple_of(step * cols, 128), cols)]))
-    end(grid, mover)
+
+    def put(n):
+        pair.take(n)
+        at = pl.ds(pl.multiple_of(n * width, 128), width)
+        for m in range(slots):
+            out_ref[m, :, at] = (x_ref[m, :, at].astype(jnp.float32) + mask_ref[m] * sum_ref[n, m]).astype(jnp.bfloat16)
+
+    @pl.when(step > 0)
+    def _():
+        put(step - 1)
+
+    @pl.when(step == grid[1] - 1)
+    def _():
+        put(step)
+
+    end(grid, pair)
 
 
 def unproject_kernel(
-    grid, gz_ref, gx_ref, tail_ref, w_ref, tailw_ref, up_ref, down_ref, lr_ref, low_ref, g_ref, upz_ref, upx_ref, g_down_ref,
-    ri_ref, rit_ref, lrt_ref, mover=None
+    grid, gz_ref, gx_ref, tail_ref, w_ref, tailw_ref, up_ref, down_ref, lr_ref, low_ref, x_ref, inv_ref, gain_ref, delta_ref,
+    upz_ref, upx_ref, g_down_ref, ri_ref, rit_ref, lrt_ref, part_ref, sum_ref, send_sem, recv_sem, mover=None
 ):
     step = pl.program_id(1)
-    begin(grid, mover)
+    pair = PairSum(part_ref, sum_ref, send_sem, recv_sem)
+    begin(grid, pair, mover)
     slots, tokens = gz_ref.shape[:2]
 
     @pl.when(step == 0)
@@ -896,12 +958,37 @@
     total = mm_t(merge(gz_ref), w_ref[0]) + mm_t(merge(gx_ref), w_ref[1]) + mm_t(merge(tail_ref), tailw_ref[...])
     cols = upz_ref.shape[2]
     at = pl.ds(pl.multiple_of(step * cols, 128), cols)
+    pair.free(step)
     for m in range(slots):
-        g_ref[m] = total[m * tokens : (m + 1) * tokens] + mm(ri_ref[m], twice(down_ref[0, m]))
+        part_ref[lax.rem(step, 2), m] = total[m * tokens : (m + 1) * tokens] + mm(ri_ref[m], twice(down_ref[0, m]))
+    pair.send(step)
+    for m in range(slots):
         upz_ref[m] = fold(mm(lrt_ref[m], gz_ref[m, :, at]))
         upx_ref[m] = fold(mm(lrt_ref[m], gx_ref[m, :, at]))
         g_down_ref[m] = fold(mm(rit_ref[m], low_ref[m]))
-    end(grid, mover)
+
+    @pl.when(step > 0)
+    def _():
+        pair.take(step - 1)
+
+    @pl.when(step == grid[1] - 1)
+    def _():
+        pair.take(step)
+        width = sum_ref.shape[3]
+        for m in range(slots):
+            spread = 0.0
+            for n in range(sum_ref.shape[0]):
+                at = slice(n * width, (n + 1) * width)
+                gn = sum_ref[n, m] * gain_ref[:, at]
+                sum_ref[n, m] = gn
+                spread = spread + jnp.sum(gn * x_ref[m, :, at].astype(jnp.float32), axis=1, keepdims=True)
+            inv = inv_ref[m]
+            spread = spread * (inv * inv * inv / x_ref.shape[2])
+            for n in range(sum_ref.shape[0]):
+                at = slice(n * width, (n + 1) * width)
+                delta_ref[m, :, at] = (inv * sum_ref[n, m] - x_ref[m, :, at].astype(jnp.float32) * spread).astype(jnp.bfloat16)
+
+    end(grid, pair, mover)
 
 
 def gate_back_kernel(
@@ -1497,6 +1584,7 @@
     line_scratch = [pltpu.VMEM((groups, NS, wide), f32), pltpu.VMEM((2 * groups, NS, wide), f32)] + [dma((groups,))] * 2
     scan_grid = (micros, groups)
 
+    x_low = x_rows
     x_rows = x_rows.astype(f32)
     inv_rms = lax.rsqrt(jnp.mean(x_rows * x_rows, axis=-1, keepdims=True) + eps)
     low_own = (x_rows * inv_rms * norm_gain).astype(bf16)
@@ -1568,10 +1656,6 @@
         6 * tokens * Q * chan * 2, act_bytes * 3, 3, (cot, shape((micros - early, own, D), bf16), tuple(range(early, micros)), True),
     )
 
-    def reduce_rows(v):
-        theirs = lax.dynamic_slice_in_dim(v, (1 - core) * own, own, 1)
-        return lax.dynamic_slice_in_dim(v, core * own, own, 1) + other(theirs)
-
     cols = out_all.shape[3]
     gb_own = jnp.concatenate([cot_early, cot_late], 0) * mask_own.astype(bf16)
     part_block = every(part, by_step)
@@ -1597,16 +1681,22 @@
     step_cols = every(cols, by_step)
     rank_scratch = [pltpu.VMEM((micros, tokens, 2 * R), bf16)] + [pltpu.VMEM((micros, 2 * R, tokens), bf16)] * 2
     rank_cols = block((micros, R, cols), by_step)
-    partial, g_up_out, g_out = call(
+    own_rows = pl.BlockSpec((micros, own, D), lambda m, g: (0, 0, 0), pipeline_mode=pl.Buffered(1))
+    own_col = block((micros, own, 1), lambda m, g: (0, 0, 0))
+
+    def pair_sum(steps):
+        width = D // steps
+        return [pltpu.VMEM((2, micros, tokens, width), f32), pltpu.VMEM((steps, micros, own, width), f32), dma((steps,)), dma((steps,))]
+
+    out_rows, g_up_out, g_out = call(
         branch_kernel, "branch", (1, nd),
         [(scaled, every(chan)), (out_all, block((1,) + out_all.shape[1:], lambda m, g: (g, 0, 0, 0))),
          (factors, block((micros, nz, R, part), lambda m, g: (0, 0, 2, 0))), (wide_rows, wide_block(1, cols, lambda g: g)),
-         (rg, every(2 * R)), (gb, step_cols)],
-        [(shape((micros, tokens, D), f32), step_cols), (shape((micros, R, D), f32), rank_cols),
+         (rg, every(2 * R)), (gb, step_cols), (x_low, own_rows), (mask_own, own_col)],
+        [(shape((micros, own, D), bf16), own_rows), (shape((micros, R, D), f32), rank_cols),
          (shape((micros, R, chan), f32), block((micros, R, chan // nd), by_step))],
-        rank_scratch, 6 * tokens * D * chan, act_bytes * 12,
-    )
-    out_rows = (x_rows + mask_own * reduce_rows(partial)).astype(bf16)
+        rank_scratch + pair_sum(nd), 6 * tokens * D * chan, act_bytes * 12, 8,
+    )
 
     first_slots, last_slots = tuple(range(micros - 1)), (micros - 1,)
 
@@ -1642,20 +1732,20 @@
     gx = lax.dynamic_update_slice_in_dim(gx, tail[..., :chan], tokens - 8, 1)
     gbc = lax.dynamic_update_slice_in_dim(gbc, tail[..., chan:], tokens - 8, 1)
     tail = jnp.concatenate([lax.dynamic_slice_in_dim(gbc, core * NS, NS, 2), g_rate], 2)
-    wide_cols = D // nz
-    g_low, g_up_z, g_up_x, g_down, out_last = call(
-        unproject_kernel, "unproject", (1, nz),
+    back_steps = 2 * nz
+    wide_cols, back_chan = D // back_steps, chan // back_steps
+    delta, g_up_z, g_up_x, g_down, out_last = call(
+        unproject_kernel, "unproject", (1, back_steps),
         [(gz, every(chan)), (gx, every(chan)), (tail, every(NS + 128)),
          (zx_weight, block((2, wide_cols, chan), lambda m, g: (0, g, 0))), (tail_weight, block((wide_cols, NS + 128), lambda m, g: (g, 0))),
          (factors, block((micros, nz, 2 * R, part), lambda m, g: (0, 0, 0, 0))), (wide_rows, wide_block(0, wide_cols, lambda g: g)),
-         (lr, every(2 * R)), (low, every(wide_cols, by_step))],
-        [(shape((micros, tokens, D), f32), every(wide_cols, by_step)), (shape((micros, R, chan), f32), block((micros, R, part), by_step)),
-         (shape((micros, R, chan), f32), block((micros, R, part), by_step)),
+         (lr, every(2 * R)), (low, every(wide_cols, by_step)), (x_low, own_rows), (inv_rms, own_col),
+         (norm_gain[None], block((1, D), z2))],
+        [(shape((micros, own, D), bf16), own_rows), (shape((micros, R, chan), f32), block((micros, R, back_chan), by_step)),
+         (shape((micros, R, chan), f32), block((micros, R, back_chan), by_step)),
          (shape((micros, R, D), f32), block((micros, R, wide_cols), by_step))],
-        rank_scratch, 12 * tokens * D * chan, act_bytes * 9, 6, (out_rows[-1:], shape((micros, seg, feats), bf16), last_slots, False),
-    )
-    gn = reduce_rows(g_low) * norm_gain
-    delta = inv_rms * gn - x_rows * (inv_rms**3 * jnp.mean(gn * x_rows, axis=-1, keepdims=True))
+        rank_scratch + pair_sum(back_steps), 12 * tokens * D * chan, act_bytes * 9, 6, (out_rows[-1:], shape((micros, seg, feats), bf16), last_slots, False),
+    )
     held_runs = jnp.arange(micros)[:, None] * nz + 2 * core + jnp.arange(2)
     in_last = place_of(held_runs)[1] == micros - 1
     in_last = jnp.repeat(in_last, tokens, axis=1)[..., None]
@@ -1663,7 +1753,7 @@
     mine = (sequence == jnp.arange(micros)[:, None]).astype(f32)
 
     delta, near, far = finish(
-        [g_out, g_up_z, g_up_x, g_up_out, g_down], mine, picks, delta.astype(bf16), shape((micros, seg, feats), bf16), nz, nd
+        [g_out, g_up_z, g_up_x, g_up_out, g_down], mine, picks, delta, shape((micros, seg, feats), bf16), nz, nd
     )
     grad = cotangent.astype(f32) + delta[:, None].astype(f32)
     g_out_down = jnp.transpose(near[:, 0], (0, 2, 1)).reshape(2 * part, R)

time: 1040 us -> 981 us (0.943)
  local copies, waits for them, and re-layouts: 85.4 us -> 47.2 us
  other arithmetic: 58.6 us -> 32.4 us
  Pallas kernels: 836 us -> 856 us
  waiting for transfers between devices: 21.3 us -> 6.85 us
    pallas_call x9, Pallas kernels: 507 us -> 528 us  [call(): pl.pallas_call(kernel, name=name, grid=grid, in_specs=[s for _, s in ins]...]
    ppermute x6 -> x4, waiting for transfers between devices: 16.6 us -> 1.17 us  [other(): return lax.ppermute(v, 'seq', [(0, 1), (1, 0)])]
    convert_element_type x2 -> x1, other arithmetic: 13.4 us -> 0.08 us  [fast_body(): gb_own = jnp.concatenate([cot_early, cot_late], 0) * mask_own.astype(bf16)]
    dynamic_slice x2 -> x0, local copies, waits for them, and re-layouts: 12.6 us -> none  [reduce_rows(): theirs = lax.dynamic_slice_in_dim(v, (1 - core) * own, own, 1)]
  transfers between devices with their start and end apart: 11 -> 9, of which waited for: 6 -> 3; matrix products, arithmetic and copies ran while one was open for 8% -> 5% of each run, Pallas kernels for 39% -> 42%
where the time goes in v5:
time: 981 us; the launch traced here: 973 us
  Pallas kernels  856 us (87%)
  local copies, waits for them, and re-layouts  47.2 us (5%)
  other arithmetic  32.4 us (3%)
  between operations  19.1 us (2%)
  starting transfers between devices  11.7 us (1%)
    pallas_call x9, Pallas kernels, call(): pl.pallas_call(kernel, name=name, grid=grid, in_specs=[s for _, s in ins]...  528 us
    pallas_call x1, Pallas kernels, gather(): pl.pallas_call(functools.partial(gather_kernel, nd, nz), name='gather', o...  217 us
    pallas_call x1, Pallas kernels, finish(): pl.pallas_call(functools.partial(finish_kernel, count), name='finish', in...  104 us
  transfers between devices with their start and end apart: 9, of which 3 were waited for; matrix products, arithmetic and copies ran while one was open for 5% of the time, Pallas kernels for 42%

profile of v5, /device:TPU:9, one launch (start us, length us, event | category | flops | bytes accessed | tf_op | source)
XLA Modules:
  0.0 973.0 jit_solution(12811447889889640612)
XLA Ops:
  21.0 216.9 %gather.11 = (bf16[2,2048,2048]{2,1,0:T(8,128)(2,1)}, bf16[3,256,2048]{2,1,0:T(8,128)(2,1)}) custom-call(bf16[2,256,1024]{2,1,0:T(8,128)(2,1)} %bitcast.119, bf16[3,1024,512]{2,1,0:T(8,128)(2,1)} %bitcast.120), custom_call_target="tpu_custom_call" | custom-call | tf_op jit(solution)/shard_map/gather/pallas_call | solution.py:1385
  239.2 2.1 collective-permute-start.2
  250.2 2.5 fusion.2.refs_0_
  257.6 2.9 copy.115
  262.9 7.4 pick.1.refs_4_.down_ref.refs_5_
  277.0 78.9 %project.1 = (bf16[3,512,2048]{2,1,0:T(8,128)(2,1)}, f32[3,512,2048]{2,1,0:T(8,128)}, bf16[3,512,256]{2,1,0:T(8,128)(2,1)}, f32[3,512,128]{2,1,0:T(8,128)}, bf16...) custom-call(bf16[3,256,2048]{2,1,0:T(8,128)(2,1)} %fusion.2.refs_0_, ...), custom_call_target="tpu_custom_call" | custom-call | flops 8589934592 | bytes 16777216 | tf_op jit(solution)/shard_map/project/pallas_call | solution.py:1420
  357.7 1.9 collective-permute-start.1
  359.7 4.8 collective-permute-done.1
  365.8 5.5 prep.1
  371.3 95.2 %ssd_forward.1 = (f32[3,512,2048]{2,1,0:T(8,128)}, f32[3,512,128]{2,1,0:T(8,128)}, f32[3,128,2048]{2,1,0:T(8,128)}, f32[3,128,2048]{2,1,0:T(8,128)}, bf16[2,256,2048]{2,1,0:T(8,128)(2,1)}) custom-call(bf16[3,512,2048]{2,1,0:T(8,128)(2,1)} %get-tuple-element.72.refs_0_.refs_1_, bf16[3,16,2048]{2,1,0:T(8,128)(2,1)} %slice.137.refs_1_.refs_2_, ...), custom_call_target="tpu_custom_call" | custom-call | flops 3221225472 | bytes 12582912 | tf_op jit(solution)/shard_map/ssd_forward/pallas_call | solution.py:1420
  468.0 3.6 maximum_multiply_fusion.own_ref
  471.6 32.2 %gs.1 = (f32[3,512,2048]{2,1,0:T(8,128)}, f32[3,512,128]{2,1,0:T(8,128)}, bf16[3,512,32]{2,1,0:T(8,128)(2,1)}, bf16[3,512,2048]{2,1,0:T(8,128)(2,1)}) custom-call(bf16[3,256,2048]{2,1,0:T(8,128)(2,1)} %maximum_multiply_fusion.own_ref, bf16[4,4,512,512]{3,2,1,0:T(8,128)(2,1)} %bitcast.147, bf16[2,3,16,2048]{3,2,1,0:T(8,128)(2,1)} %reshape.561.refs_3_.up_ref.refs_6_, ...), custom_call_target="tpu_custom_call" | custom-call | flops 12884901888 | bytes 62914560 | tf_op jit(solution)/shard_map/gs/pallas_call | solution.py:1420
  508.8 2.1 multiply_multiply_fusion.coef_ref
  511.0 41.2 %gate_back.1 = (f32[3,512,2048]{2,1,0:T(8,128)}, bf16[3,512,2048]{2,1,0:T(8,128)(2,1)}, bf16[3,512,2048]{2,1,0:T(8,128)(2,1)}, f32[3,128,2048]{2,1,0:T(8,128)}, f32[3,512,128]{2,1,0:T(8,128)}) custom-call(f32[3,512,2048]{2,1,0:T(8,128)} %get-tuple-element.83.gs_ref, f32[3,512,2048]{2,1,0:T(8,128)} %get-tuple-element.82.mixed_ref, ...), custom_call_target="tpu_custom_call" | custom-call | flops 805306368 | bytes 20971520 | tf_op jit(solution)/shard_map/gate_back/pallas_call | solution.py:1420
  552.1 31.3 %branch.1 = (bf16[3,256,2048]{2,1,0:T(8,128)(2,1)}, f32[3,16,2048]{2,1,0:T(8,128)}, f32[3,16,2048]{2,1,0:T(8,128)}) custom-call(bf16[3,512,2048]{2,1,0:T(8,128)(2,1)} %get-tuple-element.91.scaled_ref, bf16[4,4,512,512]{3,2,1,0:T(8,128)(2,1)} %bitcast.148, bf16[3,4,48,512]{3,2,1,0:T(8,128)(2,1)} %pick.1.refs_4_.down_ref.refs_5_, ...), custom_call_target="tpu_custom_call" | custom-call | flops 12884901888 | bytes 50331648 | tf_op jit(solution)/shard_map/branch/pallas_call | solution.py:1420
  583.4 174.4 %ssd_back.1 = (bf16[3,512,2048]{2,1,0:T(8,128)(2,1)}, f32[3,8,2048]{2,1,0:T(8,128)}, f32[3,8,2048]{2,1,0:T(8,128)}, f32[3,512,256]{2,1,0:T(8,128)}, f32[3,512,12...) custom-call(f32[3,512,2048]{2,1,0:T(8,128)} %get-tuple-element.87.refs_0_, ...), custom_call_target="tpu_custom_call" | custom-call | flops 6442450944 | bytes 12582912 | tf_op jit(solution)/shard_map/ssd_back/pallas_call | solution.py:1420
  760.8 2.3 slice.124.refs_12_
  764.6 7.5 bc_back.1
  772.9 5.6 collective-permute-start.5
  783.3 2.0 pad_maximum_fusion.2.refs_2_
  785.2 61.6 %unproject.1 = (bf16[3,256,2048]{2,1,0:T(8,128)(2,1)}, f32[3,16,2048]{2,1,0:T(8,128)}, f32[3,16,2048]{2,1,0:T(8,128)}, f32[3,16,2048]{2,1,0:T(8,128)}, bf16[3,1024,512]{2,1,0:T(8,128)(2,1)}) custom-call(bf16[3,512,2048]{2,1,0:T(8,128)(2,1)} %get-tuple-element.86.refs_0_, bf16[3,512,2048]{2,1,0:T(8,128)(2,1)} %slice_dynamic-update-slice_fusion.refs_1_, ...), custom_call_target="tpu_custom_call" | custom-call | flops 25769803776 | bytes 37748736 | tf_op jit(solution)/shard_map/unproject/pallas_call | solution.py:1420
  846.9 103.7 %finish.1 = (bf16[3,1024,512]{2,1,0:T(8,128)(2,1)}, f32[2,3,16,512]{3,2,1,0:T(8,128)}, f32[8,2,16,64]{3,2,1,0:T(8,128)}) custom-call(f32[3,16,2048]{2,1,0:T(8,128)} %get-tuple-element.110.out_ref, f32[3,16,2048]{2,1,0:T(8,128)} %get-tuple-element.111.up_z_ref, f32[3,16,2048]{2,1,0:T(8,128)} %get-tuple-element.112.up_x_ref, ...), custom_call_target="tpu_custom_call" | custom-call | tf_op jit(solution)/shard_map/finish/pallas_call | solution.py:1449
  952.4 5.7 fusion.3
  961.9 3.4 select_bitcast_fusion
  (180 shorter events, 59.3 us)
Async XLA Ops:
  8.0 2.8 copy-start
  8.0 11.8 %copy-start.10 = (bf16[256,2,1024]{2,1,0:T(2,128)(2,1)S(1)}, bf16[256,2,1024]{2,1,0:T(2,128)(2,1)}, u32[]{:S(2)}) copy-start(bf16[256,2,1024]{2,1,0:T(2,128)(2,1)} %param.28) | copy-start | bytes 3145732
  8.0 244.6 %all-reduce.8.cloned.1.call-start = ((), (), s32[]{:S(2)}) async-start(), calls=%async_computation.2 | async-start | bytes 172032
  13.0 5.8 collective-permute-start
  18.3 239.3 %all-gather.4.cloned.1.call-start = ((), (), s32[]{:S(2)}) async-start(), calls=%async_computation | async-start | bytes 4038656 | tf_op jit(solution)/shard_map/all_gather | solution.py:1513
  19.7 451.9 %all-gather.6.cloned.1.call-start = ((), (), s32[]{:S(2)}) async-start(), calls=%async_computation.1 | async-start | bytes 8912896 | tf_op jit(solution)/shard_map/all_gather | solution.py:1517
  21.0 222.4 %copy-start.2 = (s32[3,1]{0,1:T(1,128)S(1)}, s32[3,1]{0,1:T(1,128)}, u32[]{:S(2)}) copy-start(s32[3,1]{0,1:T(1,128)} %param.26) | copy-start | bytes 40
  21.0 223.1 %copy-start.3 = (s32[3,1]{0,1:T(1,128)S(1)}, s32[3,1]{0,1:T(1,128)}, u32[]{:S(2)}) copy-start(s32[3,1]{0,1:T(1,128)} %param.25) | copy-start | bytes 40
  238.0 9.5 copy-start.5
  239.2 3.3 collective-permute-start.2
  243.4 6.7 copy-start.16
  244.8 7.8 copy-start.15
  357.7 6.7 collective-permute-start.1
  371.3 96.7 %copy-start.11 = (bf16[1,256,2048]{2,1,0:T(8,128)(2,1)S(1)}, bf16[1,256,2048]{2,1,0:T(8,128)(2,1)}, u32[]{:S(2)}) copy-start(bf16[1,256,2048]{2,1,0:T(8,128)(2,1)} %get-tuple-element.71) | copy-start | bytes 3145732
  505.3 1.7 collective-permute-start.3
  507.7 3.3 copy-start.7
  757.8 5.3 copy-start.14
  757.9 5.3 copy-start.13
  757.9 5.3 copy-start.9
  757.9 5.3 collective-permute-start.4
  772.9 7.2 collective-permute-start.5
  846.9 105.5 %copy-start.6 = (bf16[3,1,1024,512]{3,2,1,0:T(8,128)(2,1)S(1)}, bf16[3,1,1024,512]{3,2,1,0:T(8,128)(2,1)}, u32[]{:S(2)}) copy-start(bf16[3,1,1024,512]{3,2,1,0:T(8,128)(2,1)} %param.24) | copy-start | bytes 9437188
  952.4 9.6 copy-start.8
  961.9 3.4 copy-start.1
  (2 other events, 2.6 us)
Sparse Core Ops, SparseCore 0:
  18.4 73.7 all-reduce.7
Sparse Core Ops, SparseCore 1:
  22.1 121.9 all-gather.3
  243.5 140.7 all-gather.5

commit v6 on v5

--- a/solution.py
+++ b/solution.py
@@ -1160,6 +1160,10 @@
     def by_sequence(ref, m):
         return sum(mine_ref[m, i] * ref[i] for i in range(SLOTS))
 
+    pl.semaphore_wait(barrier, waits + len(others))
+    for n in range(mover.pieces // 2):
+        mover.start(n)
+
     part, each = near_ref.shape[4], far_ref.shape[5]
     for m in range(SLOTS):
         for kind, ref in enumerate((out_ref, up_z_ref, up_x_ref)):
@@ -1172,7 +1176,6 @@
                 for n in range(2 * count):
                     at = (b * 2 * count + n) * each
                     far_ref[n, m, kind, b] = total[:, at : at + each].astype(jnp.bfloat16)
-    pl.semaphore_wait(barrier, waits + len(others))
 
     def remote(src, dst, send, recv, *device):
         return pltpu.make_async_remote_copy(
@@ -1193,7 +1196,7 @@
         copies.append(remote(far_ref.at[to_c * count + to], far1_ref.at[me], f1s.at[j * count + i], f1r.at[me], d, to_c, to))
     for copy in copies:
         copy.start()
-    for n in range(mover.pieces):
+    for n in range(mover.pieces // 2, mover.pieces):
         mover.start(n)
 
     near = near_ref[z].astype(jnp.float32)

time: 981 us -> 981 us (level)
  transfers between devices with their start and end apart: 9 -> 9, of which waited for: 3 -> 3; matrix products, arithmetic and copies ran while one was open for 5% -> 5% of each run, Pallas kernels for 42% -> 41%
where the time goes in v6:
time: 981 us; the launch traced here: 973 us
  Pallas kernels  856 us (87%)
  local copies, waits for them, and re-layouts  47.1 us (5%)
  other arithmetic  32.4 us (3%)
  between operations  19.1 us (2%)
  starting transfers between devices  11.7 us (1%)
    pallas_call x9, Pallas kernels, call(): pl.pallas_call(kernel, name=name, grid=grid, in_specs=[s for _, s in ins]...  528 us
    pallas_call x1, Pallas kernels, gather(): pl.pallas_call(functools.partial(gather_kernel, nd, nz), name='gather', o...  217 us
    pallas_call x1, Pallas kernels, finish(): pl.pallas_call(functools.partial(finish_kernel, count), name='finish', in...  104 us
  transfers between devices with their start and end apart: 9, of which 3 were waited for; matrix products, arithmetic and copies ran while one was open for 5% of the time, Pallas kernels for 41%

profile of v6, /device:TPU:9, one launch (start us, length us, event | category | flops | bytes accessed | tf_op | source)
XLA Modules:
  0.0 973.2 jit_solution(4095214093415063050)
XLA Ops:
  21.0 216.9 %gather.11 = (bf16[2,2048,2048]{2,1,0:T(8,128)(2,1)}, bf16[3,256,2048]{2,1,0:T(8,128)(2,1)}) custom-call(bf16[2,256,1024]{2,1,0:T(8,128)(2,1)} %bitcast.119, bf16[3,1024,512]{2,1,0:T(8,128)(2,1)} %bitcast.120), custom_call_target="tpu_custom_call" | custom-call | tf_op jit(solution)/shard_map/gather/pallas_call | solution.py:1388
  239.2 2.1 collective-permute-start.2
  250.2 2.5 fusion.2.refs_0_
  257.6 2.9 copy.115
  262.9 7.4 pick.1.refs_4_.down_ref.refs_5_
  277.0 78.9 %project.1 = (bf16[3,512,2048]{2,1,0:T(8,128)(2,1)}, f32[3,512,2048]{2,1,0:T(8,128)}, bf16[3,512,256]{2,1,0:T(8,128)(2,1)}, f32[3,512,128]{2,1,0:T(8,128)}, bf16...) custom-call(bf16[3,256,2048]{2,1,0:T(8,128)(2,1)} %fusion.2.refs_0_, ...), custom_call_target="tpu_custom_call" | custom-call | flops 8589934592 | bytes 16777216 | tf_op jit(solution)/shard_map/project/pallas_call | solution.py:1423
  357.7 1.9 collective-permute-start.1
  359.7 4.8 collective-permute-done.1
  365.8 5.5 prep.1
  371.3 95.2 %ssd_forward.1 = (f32[3,512,2048]{2,1,0:T(8,128)}, f32[3,512,128]{2,1,0:T(8,128)}, f32[3,128,2048]{2,1,0:T(8,128)}, f32[3,128,2048]{2,1,0:T(8,128)}, bf16[2,256,2048]{2,1,0:T(8,128)(2,1)}) custom-call(bf16[3,512,2048]{2,1,0:T(8,128)(2,1)} %get-tuple-element.72.refs_0_.refs_1_, bf16[3,16,2048]{2,1,0:T(8,128)(2,1)} %slice.137.refs_1_.refs_2_, ...), custom_call_target="tpu_custom_call" | custom-call | flops 3221225472 | bytes 12582912 | tf_op jit(solution)/shard_map/ssd_forward/pallas_call | solution.py:1423
  467.9 3.6 maximum_multiply_fusion.own_ref
  471.5 32.2 %gs.1 = (f32[3,512,2048]{2,1,0:T(8,128)}, f32[3,512,128]{2,1,0:T(8,128)}, bf16[3,512,32]{2,1,0:T(8,128)(2,1)}, bf16[3,512,2048]{2,1,0:T(8,128)(2,1)}) custom-call(bf16[3,256,2048]{2,1,0:T(8,128)(2,1)} %maximum_multiply_fusion.own_ref, bf16[4,4,512,512]{3,2,1,0:T(8,128)(2,1)} %bitcast.147, bf16[2,3,16,2048]{3,2,1,0:T(8,128)(2,1)} %reshape.561.refs_3_.up_ref.refs_6_, ...), custom_call_target="tpu_custom_call" | custom-call | flops 12884901888 | bytes 62914560 | tf_op jit(solution)/shard_map/gs/pallas_call | solution.py:1423
  508.8 2.1 multiply_multiply_fusion.coef_ref
  510.9 41.2 %gate_back.1 = (f32[3,512,2048]{2,1,0:T(8,128)}, bf16[3,512,2048]{2,1,0:T(8,128)(2,1)}, bf16[3,512,2048]{2,1,0:T(8,128)(2,1)}, f32[3,128,2048]{2,1,0:T(8,128)}, f32[3,512,128]{2,1,0:T(8,128)}) custom-call(f32[3,512,2048]{2,1,0:T(8,128)} %get-tuple-element.83.gs_ref, f32[3,512,2048]{2,1,0:T(8,128)} %get-tuple-element.82.mixed_ref, ...), custom_call_target="tpu_custom_call" | custom-call | flops 805306368 | bytes 20971520 | tf_op jit(solution)/shard_map/gate_back/pallas_call | solution.py:1423
  552.1 31.3 %branch.1 = (bf16[3,256,2048]{2,1,0:T(8,128)(2,1)}, f32[3,16,2048]{2,1,0:T(8,128)}, f32[3,16,2048]{2,1,0:T(8,128)}) custom-call(bf16[3,512,2048]{2,1,0:T(8,128)(2,1)} %get-tuple-element.91.scaled_ref, bf16[4,4,512,512]{3,2,1,0:T(8,128)(2,1)} %bitcast.148, bf16[3,4,48,512]{3,2,1,0:T(8,128)(2,1)} %pick.1.refs_4_.down_ref.refs_5_, ...), custom_call_target="tpu_custom_call" | custom-call | flops 12884901888 | bytes 50331648 | tf_op jit(solution)/shard_map/branch/pallas_call | solution.py:1423
  583.4 174.4 %ssd_back.1 = (bf16[3,512,2048]{2,1,0:T(8,128)(2,1)}, f32[3,8,2048]{2,1,0:T(8,128)}, f32[3,8,2048]{2,1,0:T(8,128)}, f32[3,512,256]{2,1,0:T(8,128)}, f32[3,512,12...) custom-call(f32[3,512,2048]{2,1,0:T(8,128)} %get-tuple-element.87.refs_0_, ...), custom_call_target="tpu_custom_call" | custom-call | flops 6442450944 | bytes 12582912 | tf_op jit(solution)/shard_map/ssd_back/pallas_call | solution.py:1423
  760.8 2.3 slice.124.refs_12_
  764.6 7.5 bc_back.1
  772.9 5.6 collective-permute-start.5
  783.2 2.0 pad_maximum_fusion.2.refs_2_
  785.2 61.6 %unproject.1 = (bf16[3,256,2048]{2,1,0:T(8,128)(2,1)}, f32[3,16,2048]{2,1,0:T(8,128)}, f32[3,16,2048]{2,1,0:T(8,128)}, f32[3,16,2048]{2,1,0:T(8,128)}, bf16[3,1024,512]{2,1,0:T(8,128)(2,1)}) custom-call(bf16[3,512,2048]{2,1,0:T(8,128)(2,1)} %get-tuple-element.86.refs_0_, bf16[3,512,2048]{2,1,0:T(8,128)(2,1)} %slice_dynamic-update-slice_fusion.refs_1_, ...), custom_call_target="tpu_custom_call" | custom-call | flops 25769803776 | bytes 37748736 | tf_op jit(solution)/shard_map/unproject/pallas_call | solution.py:1423
  846.9 103.9 %finish.1 = (bf16[3,1024,512]{2,1,0:T(8,128)(2,1)}, f32[2,3,16,512]{3,2,1,0:T(8,128)}, f32[8,2,16,64]{3,2,1,0:T(8,128)}) custom-call(f32[3,16,2048]{2,1,0:T(8,128)} %get-tuple-element.110.out_ref, f32[3,16,2048]{2,1,0:T(8,128)} %get-tuple-element.111.up_z_ref, f32[3,16,2048]{2,1,0:T(8,128)} %get-tuple-element.112.up_x_ref, ...), custom_call_target="tpu_custom_call" | custom-call | tf_op jit(solution)/shard_map/finish/pallas_call | solution.py:1452
  952.5 5.7 fusion.3
  962.1 3.4 select_bitcast_fusion
  (180 shorter events, 59.3 us)
Async XLA Ops:
  8.0 2.8 copy-start
  8.0 11.8 %copy-start.10 = (bf16[256,2,1024]{2,1,0:T(2,128)(2,1)S(1)}, bf16[256,2,1024]{2,1,0:T(2,128)(2,1)}, u32[]{:S(2)}) copy-start(bf16[256,2,1024]{2,1,0:T(2,128)(2,1)} %param.28) | copy-start | bytes 3145732
  8.0 244.6 %all-reduce.8.cloned.1.call-start = ((), (), s32[]{:S(2)}) async-start(), calls=%async_computation.2 | async-start | bytes 172032
  13.0 5.8 collective-permute-start
  18.3 239.3 %all-gather.4.cloned.1.call-start = ((), (), s32[]{:S(2)}) async-start(), calls=%async_computation | async-start | bytes 4038656 | tf_op jit(solution)/shard_map/all_gather | solution.py:1516
  19.7 451.8 %all-gather.6.cloned.1.call-start = ((), (), s32[]{:S(2)}) async-start(), calls=%async_computation.1 | async-start | bytes 8912896 | tf_op jit(solution)/shard_map/all_gather | solution.py:1520
  21.0 222.4 %copy-start.2 = (s32[3,1]{0,1:T(1,128)S(1)}, s32[3,1]{0,1:T(1,128)}, u32[]{:S(2)}) copy-start(s32[3,1]{0,1:T(1,128)} %param.26) | copy-start | bytes 40
  21.0 223.1 %copy-start.3 = (s32[3,1]{0,1:T(1,128)S(1)}, s32[3,1]{0,1:T(1,128)}, u32[]{:S(2)}) copy-start(s32[3,1]{0,1:T(1,128)} %param.25) | copy-start | bytes 40
  238.0 9.5 copy-start.5
  239.2 3.3 collective-permute-start.2
  243.4 6.7 copy-start.16
  244.8 7.8 copy-start.15
  357.7 6.8 collective-permute-start.1
  371.3 96.6 %copy-start.11 = (bf16[1,256,2048]{2,1,0:T(8,128)(2,1)S(1)}, bf16[1,256,2048]{2,1,0:T(8,128)(2,1)}, u32[]{:S(2)}) copy-start(bf16[1,256,2048]{2,1,0:T(8,128)(2,1)} %get-tuple-element.71) | copy-start | bytes 3145732
  505.2 1.7 collective-permute-start.3
  507.6 3.3 copy-start.7
  757.8 5.3 copy-start.14
  757.8 5.3 copy-start.13
  757.9 5.3 copy-start.9
  757.9 5.3 collective-permute-start.4
  772.9 7.2 collective-permute-start.5
  846.9 105.7 %copy-start.6 = (bf16[3,1,1024,512]{3,2,1,0:T(8,128)(2,1)S(1)}, bf16[3,1,1024,512]{3,2,1,0:T(8,128)(2,1)}, u32[]{:S(2)}) copy-start(bf16[3,1,1024,512]{3,2,1,0:T(8,128)(2,1)} %param.24) | copy-start | bytes 9437188
  952.5 9.6 copy-start.8
  962.1 3.4 copy-start.1
  (2 other events, 2.6 us)
Sparse Core Ops, SparseCore 0:
  18.4 73.7 all-reduce.7
Sparse Core Ops, SparseCore 1:
  22.1 121.9 all-gather.3
  243.5 140.7 all-gather.5
